TPU v7x, 32 devices: a whole 2x2x4 slice. The times are simulated.
32 devices in a mesh: dp: 16 (over z, y, x), tensor: 2 (over core).
Axes of the slice: x: 2, y: 2, z: 4, core: 2. Of those that a mesh axis runs over, the one named last changes fastest.
Arguments:
- hidden_in: bfloat16 [32768, 768], P(('dp', 'tensor')), may hold values from -6 to 6
- first_gain: float32 [768], replicated, may hold values from 0.5 to 1.5
- first_shift: float32 [768], replicated, may hold values from -2 to 2
- qkv_weight: bfloat16 [768, 3, 768], P('dp', None, 'tensor'), may hold values from -0.21875 to 0.21875
- qv_bias: float32 [2, 768], P(None, 'tensor'), may hold values from -2 to 2
- out_weight: bfloat16 [768, 768], P('dp', 'tensor'), may hold values from -0.875 to 0.875
- out_bias: float32 [768], replicated, may hold values from -2 to 2
- second_gain: float32 [768], replicated, may hold values from 0.5 to 1.5
- second_shift: float32 [768], replicated, may hold values from -2 to 2
- fc_weight: bfloat16 [768, 3072], P('dp', 'tensor'), may hold values from -0.21875 to 0.21875
- fc_bias: float32 [3072], P('tensor'), may hold values from -2 to 2
- proj_weight: bfloat16 [768, 3072], P('dp', 'tensor'), may hold values from -0.15625 to 0.15625
- proj_bias: float32 [768], replicated, may hold values from -2 to 2
- cotangent: bfloat16 [32768, 768], P(('dp', 'tensor')), may hold values from -6 to 6
Outputs:
- block_out: bfloat16 [32768, 768], P(('dp', 'tensor'))
- grad_hidden: bfloat16 [32768, 768], P(('dp', 'tensor'))
- grad_first_gain: float32 [768], replicated
- grad_first_shift: float32 [768], replicated
- grad_qkv_weight: float32 [768, 3, 768], P('dp', None, 'tensor')
- grad_qv_bias: float32 [2, 768], P(None, 'tensor')
- grad_out_weight: float32 [768, 768], P('dp', 'tensor')
- grad_out_bias: float32 [768], replicated
- grad_second_gain: float32 [768], replicated
- grad_second_shift: float32 [768], replicated
- grad_fc_weight: float32 [768, 3072], P('dp', 'tensor')
- grad_fc_bias: float32 [3072], P('tensor')
- grad_proj_weight: float32 [768, 3072], P('dp', 'tensor')
- grad_proj_bias: float32 [768], replicated
All inputs are finite; a program needn't handle non-finite values.
Results may differ from a plain program's by a relative error of at most 0.017.
Values may be sent and summed in bfloat16 or wider, within the bound.
No kernel may reach another device: no remote copies, remote signals or barrier semaphores. Data moves between devices by JAX's collectives and lax.ppermute only.
A program may use at most 320 MiB of HBM per device.

v0:
```python
import functools
import math

import jax
import jax.numpy as jnp
from jax import lax
from jax.experimental import pallas as pl
from jax.experimental.pallas import tpu as pltpu
from jax.sharding import PartitionSpec as P

HEAD_DIM = 64
SEQ_LEN = 2048
PAIR = 2 * HEAD_DIM
F32 = jnp.float32
BF16 = jnp.bfloat16
VMEM_BYTES = 56 * 1024 * 1024
MASKED = -1e30
SMALL_COST = pl.CostEstimate(flops=1, bytes_accessed=1, transcendentals=0)


def norm_layer(rows_in, gain_vec, shift_vec):
    row_mean = jnp.mean(rows_in, axis=-1, keepdims=True)
    centred = rows_in - row_mean
    variance = jnp.mean(centred * centred, axis=-1, keepdims=True)
    return centred * lax.rsqrt(variance + 1e-05) * gain_vec + shift_vec


def dot(left, right, left_axis=1, right_axis=0):
    return lax.dot_general(
        left, right, (((left_axis,), (right_axis,)), ((), ())), preferred_element_type=F32
    )


def bits_of(count):
    return count.bit_length() - 1


def gather_orders(count):
    even = list(range(bits_of(count)))[::-1]
    odd = even[:-2] + [0, 1]
    if len(even) == 4:
        odd = [2, 3, 0, 1]
    return even, odd


def scatter_orders(count):
    bits = list(range(bits_of(count)))
    return bits, [1, 0] + bits[2:]


def place_info():
    return jnp.stack([lax.axis_index("dp"), lax.axis_index("tensor")]).astype(jnp.int32)


def gathered_owner(info, place, count):
    even, odd = (
        sum(((place >> step) & 1) << bit for step, bit in enumerate(order))
        for order in gather_orders(count)
    )
    return jnp.where(info[1] % 2 == 0, even, odd) ^ info[0]


def scatter_block(info, step, block, sent, count):
    found = []
    for order in scatter_orders(count):
        bit = order[step]
        at = sorted(order[step:]).index(bit)
        own = ((info[0] >> bit) & 1) ^ (1 if sent else 0)
        found.append(((block >> at) << (at + 1)) | (own << at) | (block & ((1 << at) - 1)))
    return jnp.where(info[1] % 2 == 0, found[0], found[1])


def forward_kernel(weight_ref, bias_ref, *refs, rows, halves):
    if halves:
        info_ref, own_ref, other_ref = refs[:3]
        normed_ref, qkv_ref, out_ref, lse_ref, token_ref = refs[-5:]
        half = own_ref.shape[0]
        normed_ref[pl.ds(pl.multiple_of(info_ref[1] * half, half), half), :] = own_ref[...]
        normed_ref[pl.ds(pl.multiple_of((1 - info_ref[1]) * half, half), half), :] = other_ref[...]
    else:
        normed_ref = refs[0]
        qkv_ref, out_ref, lse_ref, token_ref = refs[-4:]
    token_ref[...] = jnp.zeros_like(token_ref)
    qkv_ref[...] = (dot(normed_ref[...], weight_ref[...]) + bias_ref[...]).astype(BF16)
    lane = lax.broadcasted_iota(jnp.int32, (1, PAIR), 1)
    mine = [lane < HEAD_DIM, lane >= HEAD_DIM]
    causal = lax.broadcasted_iota(jnp.int32, (rows, rows), 1) <= lax.broadcasted_iota(
        jnp.int32, (rows, rows), 0
    )
    zero = jnp.zeros((), BF16)
    one = jnp.ones((), BF16)
    scale = jnp.asarray(1.0 / math.sqrt(HEAD_DIM), BF16)
    keys = qkv_ref[:, PAIR : 2 * PAIR]
    values = qkv_ref[:, 2 * PAIR :]
    values_one = [jnp.where(lanes, values, one) for lanes in mine]
    for block in range(SEQ_LEN // rows):
        start = block * rows
        here = pl.ds(start, rows)
        queries = qkv_ref[here, :PAIR] * scale
        halves = []
        for head in range(2):
            query = jnp.where(mine[head], queries, zero)
            near = jnp.where(causal, dot(query, keys[start : start + rows], 1, 1), MASKED)
            top = jnp.max(near, axis=1, keepdims=True)
            if block:
                far = dot(query, keys[:start], 1, 1)
                top = jnp.maximum(top, jnp.max(far, axis=1, keepdims=True))
                far = jnp.exp(far - top).astype(BF16)
            near = jnp.exp(near - top).astype(BF16)
            weighted = dot(near, values_one[head][start : start + rows])
            if block:
                weighted = weighted + dot(far, values_one[head][:start])
            total = pltpu.roll(weighted, HEAD_DIM, 1)
            halves.append(weighted / total)
            lse = top + jnp.log(jnp.where(mine[head], total, weighted))
            lse_ref[head : head + 1, here] = jnp.transpose(lse)[0:1]
        out_ref[here, :] = jnp.where(mine[0], halves[0], halves[1]).astype(BF16)


def to_row(columns):
    folded = sum(columns[:, c : c + 128] for c in range(0, columns.shape[1], 128))
    return jnp.sum(jnp.transpose(folded), axis=0, keepdims=True)


def backward_kernel(
    info_ref,
    qkv_ref,
    heads_ref,
    lse_ref,
    own_ref,
    other_ref,
    normed_ref,
    weight_ref,
    out_weight_ref,
    norm_ref,
    *refs,
    rows,
    ties,
    kind,
):
    before_ref = refs[0]
    result_ref, sums_ref, vector_ref, token_ref = refs[ties : ties + 4]
    grad_ref, dq_ref, product_ref = refs[-3:]
    token_ref[...] = jnp.zeros_like(token_ref)
    tokens = qkv_ref.shape[0]
    part = own_ref.shape[0]
    grad_ref[pl.ds(pl.multiple_of(info_ref[1] * part, part), part), :] = own_ref[...]
    grad_ref[pl.ds(pl.multiple_of((1 - info_ref[1]) * part, part), part), :] = other_ref[...]

    lane = lax.broadcasted_iota(jnp.int32, (1, PAIR), 1)
    mine = [lane < HEAD_DIM, lane >= HEAD_DIM]
    causal = lax.broadcasted_iota(jnp.int32, (rows, rows), 0) <= lax.broadcasted_iota(
        jnp.int32, (rows, rows), 1
    )
    zero = jnp.zeros((), BF16)
    scale = jnp.asarray(1.0 / math.sqrt(HEAD_DIM), BF16)
    grad = dot(grad_ref[...], out_weight_ref[...]).astype(BF16)
    out = heads_ref[...]
    queries = [jnp.where(lanes, qkv_ref[:, :PAIR], zero) * scale for lanes in mine]
    grads = [jnp.where(lanes, grad, zero) for lanes in mine]
    product = jnp.transpose(grad.astype(F32) * out.astype(F32))
    delta = [
        jnp.sum(product[:HEAD_DIM], axis=0, keepdims=True),
        jnp.sum(product[HEAD_DIM:], axis=0, keepdims=True),
    ]
    for block in range(tokens // rows):
        start = block * rows
        here = pl.ds(start, rows)
        keys = qkv_ref[here, PAIR : 2 * PAIR]
        values = qkv_ref[here, 2 * PAIR :]
        keys_turned = jnp.transpose(keys * scale)
        key_grad = jnp.zeros((rows, PAIR), F32)
        value_grad = jnp.zeros((rows, PAIR), F32)
        for head in range(2):
            part = slice(HEAD_DIM * head, HEAD_DIM * (head + 1))
            for low, high in ((start, start + rows), (start + rows, tokens)):
                if low == high:
                    continue
                scores = dot(keys, queries[head][low:high], 1, 1)
                if low == start:
                    scores = jnp.where(causal, scores, MASKED)
                probs = jnp.exp(scores - lse_ref[head : head + 1, low:high])
                grad_probs = dot(values, grads[head][low:high], 1, 1)
                grad_scores = (probs * (grad_probs - delta[head][:, low:high])).astype(BF16)
                value_grad = value_grad + dot(probs.astype(BF16), grads[head][low:high])
                key_grad = key_grad + dot(grad_scores, queries[head][low:high])
                turned = dot(keys_turned[part], grad_scores)
                if block == 0:
                    dq_ref[part, low:high] = turned
                else:
                    dq_ref[part, low:high] += turned
        result_ref[here, PAIR : 2 * PAIR] = key_grad.astype(BF16)
        result_ref[here, 2 * PAIR :] = value_grad.astype(BF16)
    result_ref[:, :PAIR] = jnp.transpose(dq_ref[...]).astype(BF16)

    result = result_ref[...]
    sums = jnp.sum(result.astype(F32), axis=0, keepdims=True)
    sums_ref[...] = sums
    weight_grad = jnp.transpose(dot(result, normed_ref[...], 0, 0))
    out_weight_grad = jnp.transpose(dot(out, grad_ref[...], 0, 0))
    high = sums.astype(BF16)
    low = (sums - high.astype(F32)).astype(BF16)
    weight = weight_ref[...]
    shift = dot(high, weight, 1, 1) + dot(low, weight, 1, 1)
    gain = (to_row(weight.astype(F32) * weight_grad) - norm_ref[1:2, :] * shift) / norm_ref[0:1, :]
    vector_ref[0:1, :] = gain
    vector_ref[1:2, :] = shift
    wide = weight_grad.shape[1]
    if kind == "flat":
        whole_ref = refs[ties + 4]
        whole_ref[:, :wide] = weight_grad
        whole_ref[:, wide:] = out_weight_grad
        return
    target = refs[ties + 4] if kind == "whole" else product_ref
    count, shard = target.shape[:2]
    target[:, :, :wide] = weight_grad.reshape(count, shard, wide)
    target[:, :, wide:] = out_weight_grad.reshape(count, shard, PAIR)
    if kind == "whole":
        return
    kept_ref, away_ref = refs[ties + 4 : ties + 6]
    for block in range(count // 2):
        keep = scatter_block(info_ref, 0, block, False, count)
        send = scatter_block(info_ref, 0, block, True, count)
        start = 0
        if kind == "joined":
            start = before_ref.shape[2]
            kept_ref[block, :, :start] = before_ref[keep]
            away_ref[block, :, :start] = before_ref[send].astype(BF16)
        kept_ref[block, :, start:] = product_ref[keep]
        away_ref[block, :, start:] = product_ref[send].astype(BF16)


def feed_forward_kernel(
    info_ref,
    own_ref,
    other_ref,
    cot_own_ref,
    cot_other_ref,
    bias_ref,
    *refs,
    blocks,
    placed,
):
    weights, refs = refs[: 2 if placed else 4], refs[2 if placed else 4 :]
    terms_own_ref, terms_other_ref, back_own_ref, back_other_ref, sums_ref = refs[:5]
    refs = refs[5:]
    step = pl.program_id(0)
    own = step < blocks
    if placed:
        grad_fc_ref, grad_proj_ref = refs
        fc, proj = (ref[...] for ref in weights)
    else:
        kept_ref, away_ref, fc_ref, proj_ref, grad_fc_ref, grad_proj_ref, away_scratch, sems = refs
        count = fc_ref.shape[0]
        half = count // 2

        @pl.when(step == 0)
        def _():
            copies = []
            for number, target in enumerate((fc_ref, proj_ref)):
                for place in range(count):
                    source = weights[2 * number + place // half].at[place % half]
                    copies.append(
                        pltpu.make_async_copy(
                            source,
                            target.at[gathered_owner(info_ref, place, count)],
                            sems.at[number * count + place],
                        )
                    )
                    copies[-1].start()
            for copy in copies:
                copy.wait()

        fc, proj = (ref[...].reshape(-1, ref.shape[2]) for ref in (fc_ref, proj_ref))

    @pl.when(step == 0)
    def _():
        sums_ref[...] = jnp.zeros_like(sums_ref)
        grad_fc_ref[...] = jnp.zeros_like(grad_fc_ref)
        grad_proj_ref[...] = jnp.zeros_like(grad_proj_ref)

    rows = jnp.where(own, own_ref[...], other_ref[...])
    cot = jnp.where(own, cot_own_ref[...], cot_other_ref[...])
    pre = dot(rows, fc) + bias_ref[...]
    slope = math.sqrt(2.0 / math.pi)
    square = pre * pre
    bent = jnp.tanh(slope * pre * (1.0 + 0.044715 * square))
    upper = 0.5 * (1.0 + bent)
    act = (pre * upper).astype(BF16)
    terms = dot(act, proj, 1, 1)
    grad_proj_ref[...] += dot(cot, act, 0, 0).reshape(grad_proj_ref.shape)
    derivative = upper + 0.5 * pre * (1.0 - bent * bent) * (
        slope * (1.0 + 3.0 * 0.044715 * square)
    )
    grad_pre = (dot(cot, proj) * derivative).astype(BF16)
    back = dot(grad_pre, fc, 1, 1)
    grad_fc_ref[...] += dot(rows, grad_pre, 0, 0).reshape(grad_fc_ref.shape)
    sums_ref[...] += jnp.sum(grad_pre.astype(F32), axis=0, keepdims=True)

    @pl.when(own)
    def _():
        terms_own_ref[...] = terms
        back_own_ref[...] = back

    @pl.when(jnp.logical_not(own))
    def _():
        terms_other_ref[...] = terms.astype(BF16)
        back_other_ref[...] = back.astype(BF16)

    if not placed:
        hidden = fc_ref.shape[2]

        @pl.when(step == 2 * blocks - 1)
        def _():
            copies = []
            for number, grad_ref in enumerate((grad_fc_ref, grad_proj_ref)):
                for block in range(half):
                    copies.append(
                        pltpu.make_async_copy(
                            grad_ref.at[scatter_block(info_ref, 0, block, False, count)],
                            kept_ref.at[block, :, pl.ds(number * hidden, hidden)],
                            sems.at[number * half + block],
                        )
                    )
                    copies[-1].start()
            for number, grad_ref in enumerate((grad_fc_ref, grad_proj_ref)):
                for block in range(half):
                    away_scratch[block, :, number * hidden : (number + 1) * hidden] = grad_ref[
                        scatter_block(info_ref, 0, block, True, count)
                    ].astype(BF16)
            send = pltpu.make_async_copy(away_scratch, away_ref, sems.at[2 * half])
            send.start()
            for copy in copies + [send]:
                copy.wait()


ANY_SPEC = pl.BlockSpec(memory_space=pl.ANY)
TOKEN_SHAPE = jax.ShapeDtypeStruct((1, 1), F32)
TOKEN_SPEC = pl.BlockSpec((1, 1), lambda *_: (0, 0))


def attend_forward(pair, normed, weight, bias, ties):
    halves = isinstance(normed, tuple)
    tokens = 2 * normed[1].shape[0] if halves else normed.shape[0]
    features, columns = weight.shape
    every = pl.BlockSpec((tokens, features), lambda: (0, 0))
    in_specs = [
        pl.BlockSpec((features, columns), lambda: (0, 0)),
        pl.BlockSpec((1, columns), lambda: (0, 0)),
    ]
    out_specs = [
        pl.BlockSpec((tokens, columns), lambda: (0, 0)),
        pl.BlockSpec((tokens, PAIR), lambda: (0, 0)),
        pl.BlockSpec((2, tokens), lambda: (0, 0)),
        pl.BlockSpec((1, 1), lambda: (0, 0)),
    ]
    out_shape = [
        jax.ShapeDtypeStruct((tokens, columns), BF16),
        jax.ShapeDtypeStruct((tokens, PAIR), BF16),
        jax.ShapeDtypeStruct((2, tokens), F32),
        TOKEN_SHAPE,
    ]
    if halves:
        half = pl.BlockSpec((tokens // 2, features), lambda: (0, 0))
        in_specs += [pl.BlockSpec(memory_space=pltpu.SMEM), half, half]
        out_specs = [every] + out_specs
        out_shape = [jax.ShapeDtypeStruct((tokens, features), BF16)] + out_shape
    else:
        in_specs += [every]
    in_specs += [ANY_SPEC] * len(ties)
    out = pl.pallas_call(
        functools.partial(forward_kernel, rows=512, halves=halves),
        in_specs=in_specs,
        out_specs=out_specs,
        out_shape=out_shape,
        compiler_params=pltpu.CompilerParams(vmem_limit_bytes=VMEM_BYTES),
        cost_estimate=SMALL_COST,
        name=f"attend_forward_{pair}",
    )(weight, bias, *(normed if halves else (normed,)), *ties)
    return out[0] if halves else normed, *out[-4:-1], out[-1].reshape(())


def attend_backward(
    pair, kind, projected, heads_flat, lse, info, own, other, normed, weight, out_weight, norm, ties
):
    tokens, columns = projected.shape
    features = normed.shape[1]
    count = lax.axis_size("dp")
    shard = features // count
    fixed = lambda shape: pl.BlockSpec(shape, lambda _: (0,) * len(shape))
    scalars = pl.BlockSpec(memory_space=pltpu.SMEM)
    out_shape = [
        jax.ShapeDtypeStruct((tokens, columns), BF16),
        jax.ShapeDtypeStruct((1, columns), F32),
        jax.ShapeDtypeStruct((2, features), F32),
        TOKEN_SHAPE,
    ]
    wide = 4 * PAIR
    product = pltpu.VMEM((8, 128), F32)
    tie_specs = [ANY_SPEC] * len(ties)
    if shard % 16:
        inner = "flat"
        out_shape += [jax.ShapeDtypeStruct((features, wide), F32)]
    elif kind == "whole":
        inner = kind
        out_shape += [jax.ShapeDtypeStruct((count, shard, wide), F32)]
    else:
        inner = kind
        width = wide
        if kind == "joined":
            width += ties[0].shape[2]
            tie_specs[0] = fixed(ties[0].shape)
        out_shape += [
            jax.ShapeDtypeStruct((count // 2, shard, width), held) for held in (F32, BF16)
        ]
        product = pltpu.VMEM((count, shard, wide), F32)
    out = pl.pallas_call(
        functools.partial(backward_kernel, rows=256, ties=len(ties), kind=inner),
        grid=(1,),
        in_specs=[
            scalars,
            fixed(projected.shape),
            pl.BlockSpec((tokens, PAIR), lambda _: (0, pair)),
            fixed(lse.shape),
            fixed(own.shape),
            fixed(other.shape),
            fixed(normed.shape),
            pl.BlockSpec((features, columns), lambda _: (0, pair)),
            pl.BlockSpec((features, PAIR), lambda _: (0, pair)),
            fixed(norm.shape),
        ]
        + tie_specs,
        out_specs=[fixed(result.shape) for result in out_shape],
        out_shape=out_shape,
        scratch_shapes=[
            pltpu.VMEM((tokens, features), BF16),
            pltpu.VMEM((PAIR, tokens), F32),
            product,
        ],
        compiler_params=pltpu.CompilerParams(vmem_limit_bytes=VMEM_BYTES),
        cost_estimate=SMALL_COST,
        name=f"attend_backward_{pair}",
    )(info, projected, heads_flat, lse, own, other, normed, weight, out_weight, norm, *ties)
    if kind == "whole":
        gradient = out[4]
    elif shard % 16:
        gradient = Scatter(out[4] if kind == "split" else jnp.concatenate([ties[0], out[4]], axis=1))
    else:
        gradient = Scatter(out[4], out[5])
    return out[0], out[1], out[2], out[3], gradient


def feed_forward(info, own, other, cot_own, cot_other, bias, fc, proj):
    tokens, features = own.shape
    hidden = bias.shape[0]
    block = 512
    blocks = tokens // block
    count = lax.axis_size("dp")
    shard = features // count
    placed = shard % 16 != 0
    first = pl.BlockSpec((block, features), lambda i: (jnp.minimum(i, blocks - 1), 0))
    second = pl.BlockSpec((block, features), lambda i: (jnp.maximum(i - blocks, 0), 0))
    out_specs = [first, second, first, second, pl.BlockSpec((1, hidden), lambda i: (0, 0))]
    out_shape = [
        jax.ShapeDtypeStruct((tokens, features), kind) for kind in (F32, BF16, F32, BF16)
    ] + [jax.ShapeDtypeStruct((1, hidden), F32)]
    scratch = []
    weights = [fc.held, fc.got, proj.held, proj.got]
    weight_specs = [ANY_SPEC] * 4
    if placed:
        weights = [fc.result(), proj.result()]
        weight_specs = [pl.BlockSpec((features, hidden), lambda i: (0, 0))] * 2
        out_specs += [pl.BlockSpec((features, hidden), lambda i: (0, 0))] * 2
        out_shape += [jax.ShapeDtypeStruct((features, hidden), F32)] * 2
    else:
        out_specs += [ANY_SPEC] * 2
        out_shape += [
            jax.ShapeDtypeStruct((count // 2, shard, 2 * hidden), kind) for kind in (F32, BF16)
        ]
        scratch = [
            pltpu.VMEM((count, shard, hidden), BF16),
            pltpu.VMEM((count, shard, hidden), BF16),
            pltpu.VMEM((count, shard, hidden), F32),
            pltpu.VMEM((count, shard, hidden), F32),
            pltpu.VMEM((count // 2, shard, 2 * hidden), BF16),
            pltpu.SemaphoreType.DMA((2 * count,)),
        ]
    out = pl.pallas_call(
        functools.partial(feed_forward_kernel, blocks=blocks, placed=placed),
        grid=(2 * blocks,),
        in_specs=[
            pl.BlockSpec(memory_space=pltpu.SMEM),
            first,
            second,
            first,
            second,
            pl.BlockSpec((1, hidden), lambda i: (0, 0)),
        ]
        + weight_specs,
        out_specs=out_specs,
        out_shape=out_shape,
        scratch_shapes=scratch,
        compiler_params=pltpu.CompilerParams(vmem_limit_bytes=VMEM_BYTES),
        cost_estimate=SMALL_COST,
        name="feed_forward",
    )(info, own, other, cot_own, cot_other, bias.reshape(1, hidden), *weights)
    if placed:
        return (*out[:5], Scatter(jnp.concatenate(out[5:], axis=1)))
    return (*out[:5], Scatter(*out[5:]))


def exchange(block, bits):
    count = lax.axis_size("dp")
    width = lax.axis_size("tensor")
    pairs = [
        (i * width + t, (i ^ (1 << bits[t % 2])) * width + t)
        for i in range(count)
        for t in range(width)
    ]
    return lax.ppermute(block, ("dp", "tensor"), pairs)


def swap(block):
    count = lax.axis_size("tensor")
    return lax.ppermute(block, "tensor", [(i, count - 1 - i) for i in range(count)])


class Gather:
    def __init__(self, shard):
        self.orders = list(zip(*gather_orders(lax.axis_size("dp"))))
        self.held = shard[None]
        self.step = 0
        self.got = exchange(self.held, self.orders[0])

    def advance(self, token=None):
        self.step += 1
        if self.step < len(self.orders):
            joined = [self.held, self.got]
            if token is not None:
                joined = [part + token.astype(BF16) for part in joined]
            self.held = jnp.concatenate(joined, axis=0)
            self.got = exchange(self.held, self.orders[self.step])
        return self

    def result(self, token=None):
        while self.step < len(self.orders) - 1:
            self.advance()
        return place_rows(place_info(), self.held, self.got, token)


def place_kernel(info_ref, token_ref, held_ref, got_ref, out_ref, sems):
    half = held_ref.shape[0]
    copies = []
    for place in range(2 * half):
        source = held_ref.at[place] if place < half else got_ref.at[place - half]
        owner = gathered_owner(info_ref, place, 2 * half)
        copies.append(pltpu.make_async_copy(source, out_ref.at[owner], sems.at[place]))
        copies[-1].start()
    for copy in copies:
        copy.wait()


def place_rows(info, held, got, token=None):
    half, rows, columns = held.shape
    count = 2 * half
    if rows % 16:
        owners = gathered_owner(info, jnp.arange(count, dtype=jnp.int32), count)
        placed = jnp.concatenate([held, got], axis=0)[jnp.argsort(owners)]
        return placed.reshape(count * rows, columns)
    placed = pl.pallas_call(
        place_kernel,
        in_specs=[pl.BlockSpec(memory_space=pltpu.SMEM)] * 2 + [ANY_SPEC] * 2,
        out_specs=pl.BlockSpec(memory_space=pltpu.VMEM),
        out_shape=jax.ShapeDtypeStruct((count, rows, columns), BF16),
        scratch_shapes=[pltpu.SemaphoreType.DMA((count,))],
        compiler_params=pltpu.CompilerParams(vmem_limit_bytes=16 * 1024 * 1024),
        cost_estimate=SMALL_COST,
        name="place_rows",
    )(info, jnp.zeros((1, 1), F32) if token is None else token.reshape(1, 1), held, got)
    return placed.reshape(count * rows, columns)


def join_kernel(info_ref, token_ref, keep_ref, send_ref, got_keep_ref, got_send_ref, *refs):
    kept_ref, away_ref = refs[-2:]
    kept_ref[...] = keep_ref[...] + got_keep_ref[...].astype(F32)
    away_ref[...] = (send_ref[...] + got_send_ref[...].astype(F32)).astype(BF16)


def join_halves(info, step, held, got, token, ties):
    count, rows, columns = held.shape
    half = count // 2
    size = lax.axis_size("dp")

    def at(sent):
        return pl.BlockSpec(
            (1, rows, columns), lambda i, info: (scatter_block(info, step, i, sent, size), 0, 0)
        )

    result = pl.BlockSpec((1, rows, columns), lambda i, info: (i, 0, 0))
    return pl.pallas_call(
        join_kernel,
        grid_spec=pltpu.PrefetchScalarGridSpec(
            num_scalar_prefetch=1,
            grid=(half,),
            in_specs=[pl.BlockSpec(memory_space=pltpu.SMEM), at(False), at(True), at(False), at(True)]
            + [ANY_SPEC] * len(ties),
            out_specs=[result, result],
        ),
        out_shape=[jax.ShapeDtypeStruct((half, rows, columns), kind) for kind in (F32, BF16)],
        compiler_params=pltpu.CompilerParams(vmem_limit_bytes=16 * 1024 * 1024),
        cost_estimate=SMALL_COST,
        name="join_halves",
    )(info, jnp.zeros((1, 1), F32) if token is None else token, held, held, got, got, *ties)


class Scatter:
    def __init__(self, whole, away=None):
        self.orders = list(zip(*scatter_orders(lax.axis_size("dp"))))
        self.step = 0
        if away is None:
            count = lax.axis_size("dp")
            self.split(whole.reshape(count, whole.shape[0] // count, whole.shape[1]))
        else:
            self.kept, self.away = whole, away
        self.got = exchange(self.away, self.orders[0])

    def split(self, held):
        count = lax.axis_size("dp")
        blocks = jnp.arange(held.shape[0] // 2, dtype=jnp.int32)
        keep, send = (
            scatter_block(place_info(), self.step, blocks, sent, count) for sent in (False, True)
        )
        self.kept = jnp.take(held, keep, axis=0)
        self.away = jnp.take(held, send, axis=0).astype(BF16)

    def advance(self, token=None, ties=()):
        self.step += 1
        if self.kept.shape[1] % 16:
            self.split(self.kept + self.got.astype(F32))
        else:
            self.kept, self.away = join_halves(
                place_info(), self.step, self.kept, self.got, token, ties
            )
        self.got = exchange(self.away, self.orders[self.step])

    def result(self):
        while self.step < len(self.orders) - 1:
            self.advance()
        return (self.kept + self.got.astype(F32))[0]


def sum_vectors(vector, both):
    for bit in range(bits_of(lax.axis_size("dp"))):
        vector = vector + exchange(vector, (bit, bit))
    return jnp.concatenate([vector[:both] + swap(vector[:both]), vector[both:]])


def per_device(
    hidden_in,
    first_gain,
    first_shift,
    qkv_weight,
    qv_bias,
    out_weight,
    out_bias,
    second_gain,
    second_shift,
    fc_weight,
    fc_bias,
    proj_weight,
    proj_bias,
    cotangent,
):
    tensor_pos = lax.axis_index("tensor")
    half = hidden_in.shape[0]
    width = hidden_in.shape[1]
    shard_rows = qkv_weight.shape[0]
    head_width = qkv_weight.shape[2]
    pairs = head_width // PAIR
    columns = 3 * PAIR

    def split_rows(whole):
        own = lax.dynamic_slice_in_dim(whole, tensor_pos * half, half, 0)
        other = lax.dynamic_slice_in_dim(whole, (1 - tensor_pos) * half, half, 0)
        return own, other

    by_pair = qkv_weight.reshape(shard_rows, 3, pairs, PAIR).swapaxes(1, 2)
    by_pair = by_pair.reshape(shard_rows, pairs * columns)
    first_gather = Gather(by_pair[:, :columns])
    rest_gather = Gather(jnp.concatenate([by_pair[:, columns:], out_weight], axis=1))
    fc_gather = Gather(fc_weight)
    proj_gather = Gather(proj_weight)

    rows_first = hidden_in.astype(F32)
    row_mean = jnp.mean(rows_first, axis=-1, keepdims=True)
    centred = rows_first - row_mean
    first_rsqrt = lax.rsqrt(jnp.mean(centred * centred, axis=-1, keepdims=True) + 1e-05)
    normed_piece = (centred * first_rsqrt * first_gain + first_shift).astype(BF16)
    info = place_info()
    normed_first = (info, normed_piece, swap(normed_piece))
    cot_other = swap(cotangent)

    bias_parts = jnp.stack([qv_bias[0], jnp.zeros_like(qv_bias[0]), qv_bias[1]])
    bias_cols = bias_parts.reshape(3, pairs, PAIR).swapaxes(0, 1).reshape(pairs, 1, columns)
    fc_gather.advance()
    proj_gather.advance()
    full_qkv = [first_gather.result()]
    projected, heads, lses = [], [], []
    for pair in range(pairs):
        weight = full_qkv[pair]
        normed_first, columns_out, heads_out, lse, token = attend_forward(
            pair,
            normed_first,
            weight,
            bias_cols[pair],
            [fc_gather.held, proj_gather.held] if pair else [],
        )
        projected.append(columns_out)
        heads.append(heads_out)
        lses.append(lse)
        if pair == 0:
            rest = rest_gather.result(token)
            full_qkv += [
                rest[:, p * columns : (p + 1) * columns] for p in range(pairs - 1)
            ]
            full_out = rest[:, (pairs - 1) * columns :]
        if pair < pairs - 1:
            fc_gather.advance(token)
            proj_gather.advance(token)
    full_qkv = jnp.concatenate(full_qkv, axis=1)
    heads_flat = jnp.concatenate(heads, axis=1)
    heads_own, heads_other = split_rows(heads_flat)
    attn_other = swap(dot(heads_other, full_out, 1, 1).astype(BF16))
    middle = rows_first + (dot(heads_own, full_out, 1, 1) + attn_other.astype(F32)) + out_bias

    normed_mid, second_back = jax.vjp(norm_layer, middle, second_gain, second_shift)
    normed_own = normed_mid.astype(BF16)
    normed_other = swap(normed_own)

    terms_own, terms_other, back_own, back_other, sum_fc, ff_sum = feed_forward(
        info, normed_own, normed_other, cotangent, cot_other, fc_bias, fc_gather, proj_gather
    )
    back_other = swap(back_other)
    terms_other = swap(terms_other)
    block_out = (middle + (terms_own + terms_other.astype(F32)) + proj_bias).astype(BF16)
    back_second = back_own + back_other.astype(F32)

    grad_top = cotangent.astype(F32)
    mid_part, grad_gain_two, grad_shift_two = second_back(back_second)
    grad_middle = grad_top + mid_part
    grad_attn = grad_middle.astype(BF16)
    grad_attn_other = swap(grad_attn)
    hidden = fc_weight.shape[1]
    early = jnp.concatenate(
        [
            grad_gain_two,
            grad_shift_two,
            jnp.sum(grad_attn.astype(F32), axis=0),
            jnp.sum(grad_top, axis=0),
            sum_fc.reshape(-1),
        ]
    )

    norm_first = jnp.stack([first_gain, first_shift])
    shared = (info, grad_attn, grad_attn_other, normed_first, full_qkv, full_out, norm_first)
    kinds = ["split"] + ["whole"] * (pairs - 2) + ["joined"]
    results, column_sums, vector_parts = [], [], []
    first_sum = rest_sum = whole = None
    for pair in range(pairs):
        ties = [] if whole is None else [whole]
        if pair:
            ties += [ff_sum.away, first_sum.away]
        result, sums, vector, token, gradient = attend_backward(
            pair, kinds[pair], projected[pair], heads_flat, lses[pair], *shared, ties
        )
        results.append(result)
        column_sums.append(sums)
        vector_parts.append(vector)
        ff_sum.advance(token)
        if pair:
            first_sum.advance(token)
        if pair == 0:
            first_sum = gradient
        elif pair == pairs - 1:
            rest_sum = gradient
        else:
            whole = gradient
    grad_projected = jnp.concatenate(results, axis=1)
    grad_own, grad_other = split_rows(grad_projected)
    back_other = dot(grad_other, full_qkv, 1, 1).astype(BF16)
    back_own = dot(grad_own, full_qkv, 1, 1)
    back_first = back_own + swap(back_other).astype(F32)
    rest_sum.advance(ties=(back_other,))
    vector_parts = sum(vector_parts[1:], vector_parts[0])
    column_sums = jnp.concatenate(column_sums, axis=0).reshape(pairs, 3, PAIR)
    vectors = sum_vectors(
        jnp.concatenate(
            [
                vector_parts.reshape(-1),
                early,
                column_sums[:, 0].reshape(-1),
                column_sums[:, 2].reshape(-1),
            ]
        ),
        6 * width,
    )
    scaled = back_first * first_gain
    normalised = centred * first_rsqrt
    grad_hidden = grad_middle + first_rsqrt * (
        scaled
        - jnp.mean(scaled, axis=-1, keepdims=True)
        - normalised * jnp.mean(scaled * normalised, axis=-1, keepdims=True)
    )
    own_heads = jnp.concatenate([first_sum.result(), rest_sum.result()], axis=1).reshape(
        shard_rows, pairs, 4, PAIR
    )
    own_outw = own_heads[:, :, 3].reshape(shard_rows, head_width)
    own_qkv = own_heads[:, :, :3].swapaxes(1, 2).reshape(shard_rows, 3, head_width)
    own_ff = ff_sum.result()
    sums = vectors[: 6 * width].reshape(6, width)
    hidden_sums = vectors[6 * width : 6 * width + hidden]
    return (
        block_out,
        grad_hidden.astype(BF16),
        sums[0],
        sums[1],
        own_qkv,
        vectors[6 * width + hidden :].reshape(2, head_width),
        own_outw,
        sums[4],
        sums[2],
        sums[3],
        own_ff[:, :hidden],
        hidden_sums,
        own_ff[:, hidden:],
        sums[5],
    )


def solution(mesh):
    placed = (
        P(("dp", "tensor"), None),
        P(),
        P(),
        P("dp", None, "tensor"),
        P(None, "tensor"),
        P("dp", "tensor"),
        P(),
        P(),
        P(),
        P("dp", "tensor"),
        P("tensor"),
        P("dp", "tensor"),
        P(),
        P(("dp", "tensor"), None),
    )
    return jax.shard_map(
        per_device,
        mesh=mesh,
        in_specs=placed,
        out_specs=(
            P(("dp", "tensor"), None),
            P(("dp", "tensor"), None),
            P(),
            P(),
            P("dp", None, "tensor"),
            P(None, "tensor"),
            P("dp", "tensor"),
            P(),
            P(),
            P(),
            P("dp", "tensor"),
            P("tensor"),
            P("dp", "tensor"),
            P(),
        ),
        check_vma=False,
    )
```

profile of v0, /device:TPU:0, one launch (start us, length us, event | category | flops | bytes accessed | tf_op | source)
XLA Modules:
  0.0 363.9 jit_solution(4414000674618368482)
XLA Ops:
  2.0 4.1 %collective-permute-start = (bf16[1,48,384]{2,1,0:T(8,128)(2,1)S(1)}, bf16[1,48,384]{2,1,0:T(8,128)(2,1)S(1)}, u32[]{:S(2)}, u32[]{:S(2)}) collective-permute-start(bf16[1,48,384]{2,1,0:T(8,128)(2,1)S(1)} %slice_bitcast_fusion), channel_id=1, source_target_pairs={{0,16},{1,9},{2,18},{3,11},{4,20},{5,13},{6,22},{7,15},{8,24},{9,1... | collective-permute-start | bytes 110600 | tf_op jit(solution)/shard_map/ppermute | solution.py:520
  7.0 1.7 convert_reduce_fusion
  9.3 1.8 fusion.6.refs_1_
  11.1 2.9 collective-permute-start.11
  14.0 1.9 collective-permute-start.6
  16.3 9.4 %collective-permute-done.6 = bf16[2,48,1152]{2,1,0:T(8,128)(2,1)S(1)} collective-permute-done((bf16[2,48,1152]{2,1,0:T(8,128)(2,1)S(1)}, bf16[2,48,1152]{2,1,0:T(8,128)(2,1)S(1)}, u32[]{:S(2)}, u32[]{:S(2)}) %collective-permute-start.6) | collective-permute-done | bytes 221216 | tf_op jit(solution)/shard_map/ppermute | solution.py:520
  25.7 1.6 collective-permute-start.7
  28.2 7.5 %collective-permute-done.2 = bf16[4,48,384]{2,1,0:T(8,128)(2,1)S(1)} collective-permute-done((bf16[4,48,384]{2,1,0:T(8,128)(2,1)S(1)}, bf16[4,48,384]{2,1,0:T(8,128)(2,1)S(1)}, u32[]{:S(2)}, u32[]{:S(2)}) %collective-permute-start.2) | collective-permute-done | bytes 147488 | tf_op jit(solution)/shard_map/ppermute | solution.py:520
  35.7 1.6 collective-permute-start.3
  39.8 2.7 collective-permute-done.3.got_ref
  42.5 1.8 place_rows.2
  45.2 12.5 %attend_forward_0.1 = (bf16[2048,768]{1,0:T(8,128)(2,1)}, bf16[2048,384]{1,0:T(8,128)(2,1)}, bf16[2048,128]{1,0:T(8,128)(2,1)}, f32[2,2048]{1,0:T(2,128)}, f32[1,1]{1,0:T(1,128)}) custom-call(bf16[768,384]{1,0:T(8,128)(2,1)} %bitcast.61, f32[1,384]{1,0:T(1,128)} %bitcast.72, s32[2]{0:T(128)} %copy-done.9, bf16[1024,768]{1,0:T(8,128)(2,1)} %fusion.6.refs_1_, ...), custom_call_target="tpu_custom_call" | custom-call | flops 1 | bytes 1 | tf_op jit(solution)/shard_map/attend_forward_0/pallas_call | solution.py:371
  59.3 2.5 collective-permute-start.12
  62.9 1.9 constant_dynamic-update-slice_fusion.2
  65.4 4.0 %place_rows.3 = bf16[16,48,1152]{2,1,0:T(8,128)(2,1)S(1)} custom-call(s32[2]{0:T(128)S(1)} %copy-done.10, f32[1,1]{1,0:T(1,128)} %get-tuple-element.69.token_ref, bf16[8,48,1152]{2,1,0:T(8,128)(2,1)S(1)} %pad_maximum_fusion.3.held_ref, bf16[8,48,1152]{2,1,0:T(8,128)(2,1)S(1)} %collective-permute-done.8.got_ref), custom_call_target="tpu_custom_call" | custom-call | flops 1 | bytes 1 | tf_op jit(solution)/shard_map/place_rows/pallas_call | solution.py:570
  70.8 1.6 collective-permute-start.14
  72.3 2.2 collective-permute-done.10
  74.7 1.8 collective-permute-start.13
  76.4 12.3 %attend_forward_1.1 = (bf16[2048,384]{1,0:T(8,128)(2,1)}, bf16[2048,128]{1,0:T(8,128)(2,1)}, f32[2,2048]{1,0:T(2,128)}, f32[1,1]{1,0:T(1,128)}) custom-call(bf16[768,384]{1,0:T(8,128)(2,1)} %get-tuple-element.136.weight_ref, f32[1,384]{1,0:T(1,128)} %bitcast.74, bf16[2048,768]{1,0:T(8,128)(2,1)} %get-tuple-element.70.refs_0_.normed_ref, ...), custom_call_target="tpu_custom_call" | custom-call | flops 1 | bytes 1 | tf_op jit(solution)/shard_map/attend_forward_1/pallas_call | solution.py:371
  88.7 1.9 constant_dynamic-update-slice_fusion.1
  93.8 12.7 %attend_forward_2.1 = (bf16[2048,384]{1,0:T(8,128)(2,1)}, bf16[2048,128]{1,0:T(8,128)(2,1)}, f32[2,2048]{1,0:T(2,128)}, f32[1,1]{1,0:T(1,128)}) custom-call(bf16[768,384]{1,0:T(8,128)(2,1)} %get-tuple-element.135.weight_ref, f32[1,384]{1,0:T(1,128)} %bitcast.73, bf16[2048,768]{1,0:T(8,128)(2,1)} %get-tuple-element.70.refs_0_.normed_ref, ...), custom_call_target="tpu_custom_call" | custom-call | flops 1 | bytes 1 | tf_op jit(solution)/shard_map/attend_forward_2/pallas_call | solution.py:371
  106.5 2.0 constant_dynamic-update-slice_fusion.heads_ref
  108.5 3.3 convolution_convert_fusion
  112.3 3.2 collective-permute-done.15
  115.5 2.9 fusion.41
  120.2 1.5 collective-permute-start.19
  122.8 13.6 %collective-permute-done.19.refs_3_ = bf16[8,48,1536]{2,1,0:T(8,128)(2,1)S(1)} collective-permute-done((bf16[8,48,1536]{2,1,0:T(8,128)(2,1)S(1)}, bf16[8,48,1536]{2,1,0:T(8,128)(2,1)S(1)}, u32[]{:S(2)}, u32[]{:S(2)}) %collective-permute-start.19) | collective-permute-done | bytes 1179680 | tf_op jit(solution)/shard_map/ppermute | solution.py:520
  136.4 12.6 %collective-permute-done.18.refs_1_ = bf16[8,48,1536]{2,1,0:T(8,128)(2,1)S(1)} collective-permute-done((bf16[8,48,1536]{2,1,0:T(8,128)(2,1)S(1)}, bf16[8,48,1536]{2,1,0:T(8,128)(2,1)S(1)}, u32[]{:S(2)}, u32[]{:S(2)}) %collective-permute-start.18) | collective-permute-done | bytes 1179680 | tf_op jit(solution)/shard_map/ppermute | solution.py:520
  150.1 42.9 %feed_forward.1 = (f32[1024,768]{1,0:T(8,128)}, bf16[1024,768]{1,0:T(8,128)(2,1)}, f32[1024,768]{1,0:T(8,128)}, bf16[1024,768]{1,0:T(8,128)(2,1)}, f32[1,1536]{1...) custom-call(s32[2]{0:T(128)} %copy-done.9, bf16[1024,768]{1,0:T(8,128)(2,1)} %copy-done.24, ...), custom_call_target="tpu_custom_call" | custom-call | flops 1 | bytes 1 | tf_op jit(solution)/shard_map/feed_forward/pallas_call | solution.py:488
  193.6 1.5 collective-permute-start.23
  195.1 1.6 collective-permute-done.21
  196.7 3.3 multiply_reduce_fusion
  200.5 3.1 fusion.36
  203.7 3.1 convert_reduce_fusion.2
  208.0 1.7 pad_maximum_fusion.weight_ref
  211.4 23.0 %attend_backward_0.1 = (bf16[2048,384]{1,0:T(8,128)(2,1)}, f32[1,384]{1,0:T(1,128)}, f32[2,768]{1,0:T(2,128)}, f32[1,1]{1,0:T(1,128)}, f32[8,48,512]{2,1,0:T(8,128)}, /*index=5*/bf16[8,48,512]{2,1,0:T(8,128)(2,1)}) custom-call(s32[2]{0:T(128)} %copy-done.9, bf16[2048,384]{1,0:T(8,128)(2,1)} %get-tuple-element.78.qkv_ref, ...), custom_call_target="tpu_custom_call" | custom-call | flops 1 | bytes 1 | tf_op jit(solution)/shard_map/attend_backward_0/pallas_call | solution.py:417
  234.5 5.1 %join_halves.9 = (f32[4,48,3072]{2,1,0:T(8,128)S(1)}, bf16[4,48,3072]{2,1,0:T(8,128)(2,1)}) custom-call(s32[2]{0:T(128)S(1)} %copy-done.11, f32[1,1]{1,0:T(1,128)} %get-tuple-element.83.token_ref, f32[8,48,3072]{2,1,0:T(8,128)S(1)} %bitcast.56, f32[8,48,3072]{2,1,0:T(8,128)S(1)} %bitcast.56, ...), custom_call_target="tpu_custom_call" | custom-call | flops 1 | bytes 1 | tf_op jit(solution)/shard_map/join_halves/pallas_call | solution.py:600
  240.3 1.5 collective-permute-start.25
  241.8 1.4 constant_dynamic-update-slice_fusion.5
  243.2 22.8 %attend_backward_1.1 = (bf16[2048,384]{1,0:T(8,128)(2,1)}, f32[1,384]{1,0:T(1,128)}, f32[2,768]{1,0:T(2,128)}, f32[1,1]{1,0:T(1,128)}, f32[16,48,512]{2,1,0:T(8,128)}) custom-call(s32[2]{0:T(128)} %copy-done.9, bf16[2048,384]{1,0:T(8,128)(2,1)} %get-tuple-element.81.qkv_ref, bf16[2048,384]{1,0:T(8,128)(2,1)} %constant_dynamic-update-slice_fusion.heads_ref, ...), custom_call_target="tpu_custom_call" | custom-call | flops 1 | bytes 1 | tf_op jit(solution)/shard_map/attend_backward_1/pallas_call | solution.py:417
  266.1 2.9 constant_dynamic-update-slice_fusion.4
  268.9 2.5 join_halves.11
  271.5 1.5 join_halves.10
  274.8 24.0 %attend_backward_2.1 = (bf16[2048,384]{1,0:T(8,128)(2,1)}, f32[1,384]{1,0:T(1,128)}, f32[2,768]{1,0:T(2,128)}, f32[1,1]{1,0:T(1,128)}, f32[8,48,1024]{2,1,0:T(8,128)}, /*index=5*/bf16[8,48,1024]{2,1,0:T(8,128)(2,1)}) custom-call(s32[2]{0:T(128)} %copy-done.9, bf16[2048,384]{1,0:T(8,128)(2,1)} %get-tuple-element.89.qkv_ref, ...), custom_call_target="tpu_custom_call" | custom-call | flops 1 | bytes 1 | tf_op jit(solution)/shard_map/attend_backward_2/pallas_call | solution.py:417
  298.8 1.8 constant_dynamic-update-slice_fusion.3
  300.7 3.4 fusion.21.refs_0_
  306.1 6.0 %collective-permute-done.32.got_keep_ref.got_send_ref = bf16[4,48,512]{2,1,0:T(8,128)(2,1)S(1)} collective-permute-done((bf16[4,48,512]{2,1,0:T(8,128)(2,1)}, bf16[4,48,512]{2,1,0:T(8,128)(2,1)S(1)}, u32[]{:S(2)}, u32[]{:S(2)}) %collective-permute-start.32) | collective-permute-done | bytes 196640 | tf_op jit(solution)/shard_map/ppermute | solution.py:520
  313.7 1.9 join_halves.12
  316.5 1.6 collective-permute-done.35.got_keep_ref.got_send_ref
  318.1 3.0 join_halves.14
  321.1 1.4 collective-permute-start.36
  324.2 2.3 collective-permute-start.34
  326.5 3.2 collective-permute-done.34
  331.1 1.8 collective-permute-start.40
  333.6 2.0 collective-permute-start.37
  335.7 4.1 %fusion.34 = (f32[1024]{0:T(1024)S(1)}, f32[1024]{0:T(1024)S(1)}, f32[1024,768]{1,0:T(8,128)S(1)}) fusion(f32[1024]{0:T(1024)S(1)} %add_rsqrt_fusion, f32[1024]{0:T(1024)S(1)} %broadcast_multiply_fusion.3, bf16[1024,768]{1,0:T(8,128)(2,1)S(1)} %copy-done.16, f32[768]{0:T(1024)S(1)} %copy-done.40, bf16[1024,768]{1,0:T(8,128)(2,1)} %collective-permute-done.26, ...), kind=kOutput, calls=%fused_computation.111 | convolution fusion | flops 1822554112 | bytes 10440708 | tf_op jit(solution)/shard_map/dot_general | solution.py:29
  339.8 3.7 %convert_reduce_fusion.1 = (f32[768]{0:T(1024)S(1)}, bf16[1024,768]{1,0:T(8,128)(2,1)}) fusion(bf16[1024,768]{1,0:T(8,128)(2,1)} %cot_own_ref.1, f32[1024]{0:T(1024)S(1)} %get-tuple-element.159, f32[1024]{0:T(1024)S(1)} %broadcast_multiply_fusion.3, bf16[1024,768]{1,0:T(8,128)(2,1)S(1)} %copy-done.16, f32[1024,768]{1,0:T(8,128)S(1)} %get-tuple-element.158, ...), kind=kLoop, calls=%fused_computation.4 | loop fusion | flops 10222848 | bytes 11033600 | tf_op jit(solution)/shard_map/reduce_sum | solution.py:759
  343.5 1.5 collective-permute-start.27
  345.9 1.6 collective-permute-done.27
  349.1 2.2 collective-permute-done.28
  351.4 1.8 collective-permute-start.29
  353.2 2.0 collective-permute-done.29
  355.2 1.3 collective-permute-start.30
  356.7 3.3 collective-permute-done.30
  (250 shorter events, 39.3 us)
Async XLA Ops:
  0.7 8.6 %copy-start.39 = (f32[768]{0:T(1024)S(1)}, f32[768]{0:T(1024)}, u32[]{:S(2)}) copy-start(f32[768]{0:T(1024)} %param.15) | copy-start | bytes 9220
  0.7 8.6 %copy-start.38 = (f32[768]{0:T(1024)S(1)}, f32[768]{0:T(1024)}, u32[]{:S(2)}) copy-start(f32[768]{0:T(1024)} %param.16) | copy-start | bytes 9220
  2.0 14.1 %collective-permute-start = (bf16[1,48,384]{2,1,0:T(8,128)(2,1)S(1)}, bf16[1,48,384]{2,1,0:T(8,128)(2,1)S(1)}, u32[]{:S(2)}, u32[]{:S(2)}) collective-permute-start(bf16[1,48,384]{2,1,0:T(8,128)(2,1)S(1)} %slice_bitcast_fusion), channel_id=1, source_target_pairs={{0,16},{1,9},{2,18},{3,11},{4,20},{5,13},{6,22},{7,15},{8,24},{9,1... | collective-permute-start | bytes 110600 | tf_op jit(solution)/shard_map/ppermute | solution.py:520
  6.9 9.1 %copy-start.48 = (f32[2,384]{1,0:T(2,128)S(1)}, f32[2,384]{1,0:T(2,128)}, u32[]{:S(2)}) copy-start(f32[2,384]{1,0:T(2,128)} %param.18) | copy-start | bytes 9220
  6.9 7.2 %collective-permute-start.5 = (bf16[1,48,1152]{2,1,0:T(8,128)(2,1)S(1)}, bf16[1,48,1152]{2,1,0:T(8,128)(2,1)S(1)}, u32[]{:S(2)}, u32[]{:S(2)}) collective-permute-start(bf16[1,48,1152]{2,1,0:T(8,128)(2,1)S(1)} %maximum_bitcast_fusion), channel_id=1, source_target_pairs={{0,16},{1,9},{2,18},{3,11},{4,20},{5,13},{6,22},{7,15},{8,24},{9,1... | collective-permute-start | bytes 331784 | tf_op jit(solution)/shard_map/ppermute | solution.py:520
  11.1 34.1 %collective-permute-start.4 = (bf16[1024,768]{1,0:T(8,128)(2,1)}, bf16[1024,768]{1,0:T(8,128)(2,1)}, u32[]{:S(2)}, u32[]{:S(2)}) collective-permute-start(bf16[1024,768]{1,0:T(8,128)(2,1)} %fusion.6.refs_1_), channel_id=1, source_target_pairs={{0,1},{1,0},{2,3},{3,2},{4,5},{5,4},{6,7},{7,6},{8,9},{9,8},{10,11... | collective-permute-start | bytes 4718600 | tf_op jit(solution)/shard_map/ppermute | solution.py:525
  11.1 47.2 %collective-permute-start.11 = (bf16[1,48,1536]{2,1,0:T(8,128)(2,1)}, bf16[1,48,1536]{2,1,0:T(8,128)(2,1)S(1)}, u32[]{:S(2)}, u32[]{:S(2)}) collective-permute-start(bf16[1,48,1536]{2,1,0:T(8,128)(2,1)} %bitcast.12), channel_id=1, source_target_pairs={{0,16},{1,9},{2,18},{3,11},{4,20},{5,13},{6,22},{7,15},{8,24},{9,1... | collective-permute-start | bytes 442376 | tf_op jit(solution)/shard_map/ppermute | solution.py:520
  14.0 47.9 %collective-permute-start.9 = (bf16[1,48,1536]{2,1,0:T(8,128)(2,1)}, bf16[1,48,1536]{2,1,0:T(8,128)(2,1)S(1)}, u32[]{:S(2)}, u32[]{:S(2)}) collective-permute-start(bf16[1,48,1536]{2,1,0:T(8,128)(2,1)} %bitcast.10), channel_id=1, source_target_pairs={{0,16},{1,9},{2,18},{3,11},{4,20},{5,13},{6,22},{7,15},{8,24},{9,1... | collective-permute-start | bytes 442376 | tf_op jit(solution)/shard_map/ppermute | solution.py:520
  14.0 11.6 %collective-permute-start.6 = (bf16[2,48,1152]{2,1,0:T(8,128)(2,1)S(1)}, bf16[2,48,1152]{2,1,0:T(8,128)(2,1)S(1)}, u32[]{:S(2)}, u32[]{:S(2)}) collective-permute-start(bf16[2,48,1152]{2,1,0:T(8,128)(2,1)S(1)} %pad_maximum_fusion.11), channel_id=1, source_target_pairs={{0,8},{1,17},{2,10},{3,19},{4,12},{5,21},{6,14},{7,23},{8,0},{9,25... | collective-permute-start | bytes 663560 | tf_op jit(solution)/shard_map/ppermute | solution.py:520
  16.1 11.2 %collective-permute-start.1 = (bf16[2,48,384]{2,1,0:T(8,128)(2,1)S(1)}, bf16[2,48,384]{2,1,0:T(8,128)(2,1)S(1)}, u32[]{:S(2)}, u32[]{:S(2)}) collective-permute-start(bf16[2,48,384]{2,1,0:T(8,128)(2,1)S(1)} %pad_maximum_fusion.13), channel_id=1, source_target_pairs={{0,8},{1,17},{2,10},{3,19},{4,12},{5,21},{6,14},{7,23},{8,0},{9,25... | collective-permute-start | bytes 221192 | tf_op jit(solution)/shard_map/ppermute | solution.py:520
  25.7 11.6 %collective-permute-start.7 = (bf16[4,48,1152]{2,1,0:T(8,128)(2,1)S(1)}, bf16[4,48,1152]{2,1,0:T(8,128)(2,1)S(1)}, u32[]{:S(2)}, u32[]{:S(2)}) collective-permute-start(bf16[4,48,1152]{2,1,0:T(8,128)(2,1)S(1)} %pad_maximum_fusion.6), channel_id=1, source_target_pairs={{0,4},{1,3},{2,6},{3,1},{4,0},{5,7},{6,2},{7,5},{8,12},{9,11},{10,... | collective-permute-start | bytes 1327112 | tf_op jit(solution)/shard_map/ppermute | solution.py:520
  27.4 8.3 %collective-permute-start.2 = (bf16[4,48,384]{2,1,0:T(8,128)(2,1)S(1)}, bf16[4,48,384]{2,1,0:T(8,128)(2,1)S(1)}, u32[]{:S(2)}, u32[]{:S(2)}) collective-permute-start(bf16[4,48,384]{2,1,0:T(8,128)(2,1)S(1)} %pad_maximum_fusion.12), channel_id=1, source_target_pairs={{0,4},{1,3},{2,6},{3,1},{4,0},{5,7},{6,2},{7,5},{8,12},{9,11},{10,... | collective-permute-start | bytes 442376 | tf_op jit(solution)/shard_map/ppermute | solution.py:520
  35.7 6.8 %collective-permute-start.3 = (bf16[8,48,384]{2,1,0:T(8,128)(2,1)S(1)}, bf16[8,48,384]{2,1,0:T(8,128)(2,1)S(1)}, u32[]{:S(2)}, u32[]{:S(2)}) collective-permute-start(bf16[8,48,384]{2,1,0:T(8,128)(2,1)S(1)} %pad_maximum_fusion.7.held_ref), channel_id=1, source_target_pairs={{0,2},{1,5},{2,0},{3,7},{4,6},{5,1},{6,4},{7,3},{8,10},{9,13},{10,... | collective-permute-start | bytes 884744 | tf_op jit(solution)/shard_map/ppermute | solution.py:520
  37.4 27.3 %collective-permute-start.8 = (bf16[8,48,1152]{2,1,0:T(8,128)(2,1)S(1)}, bf16[8,48,1152]{2,1,0:T(8,128)(2,1)S(1)}, u32[]{:S(2)}, u32[]{:S(2)}) collective-permute-start(bf16[8,48,1152]{2,1,0:T(8,128)(2,1)S(1)} %pad_maximum_fusion.3.held_ref), channel_id=1, source_target_pairs={{0,2},{1,5},{2,0},{3,7},{4,6},{5,1},{6,4},{7,3},{8,10},{9,13},{10,... | collective-permute-start | bytes 2654216 | tf_op jit(solution)/shard_map/ppermute | solution.py:520
  59.3 11.4 %collective-permute-start.12 = (bf16[2,48,1536]{2,1,0:T(8,128)(2,1)S(1)}, bf16[2,48,1536]{2,1,0:T(8,128)(2,1)S(1)}, u32[]{:S(2)}, u32[]{:S(2)}) collective-permute-start(bf16[2,48,1536]{2,1,0:T(8,128)(2,1)S(1)} %get-tuple-element.142), channel_id=1, source_target_pairs={{0,8},{1,17},{2,10},{3,19},{4,12},{5,21},{6,14},{7,23},{8,0},{9,25... | collective-permute-start | bytes 884744 | tf_op jit(solution)/shard_map/ppermute | solution.py:520
  62.8 11.8 %collective-permute-start.10 = (bf16[2,48,1536]{2,1,0:T(8,128)(2,1)S(1)}, bf16[2,48,1536]{2,1,0:T(8,128)(2,1)S(1)}, u32[]{:S(2)}, u32[]{:S(2)}) collective-permute-start(bf16[2,48,1536]{2,1,0:T(8,128)(2,1)S(1)} %get-tuple-element.144), channel_id=1, source_target_pairs={{0,8},{1,17},{2,10},{3,19},{4,12},{5,21},{6,14},{7,23},{8,0},{9,25... | collective-permute-start | bytes 884744 | tf_op jit(solution)/shard_map/ppermute | solution.py:520
  70.8 20.6 %collective-permute-start.14 = (bf16[4,48,1536]{2,1,0:T(8,128)(2,1)S(1)}, bf16[4,48,1536]{2,1,0:T(8,128)(2,1)S(1)}, u32[]{:S(2)}, u32[]{:S(2)}) collective-permute-start(bf16[4,48,1536]{2,1,0:T(8,128)(2,1)S(1)} %pad_maximum_fusion.5.refs_2_), channel_id=1, source_target_pairs={{0,4},{1,3},{2,6},{3,1},{4,0},{5,7},{6,2},{7,5},{8,12},{9,11},{10,... | collective-permute-start | bytes 1769480 | tf_op jit(solution)/shard_map/ppermute | solution.py:520
  74.7 17.9 %collective-permute-start.13 = (bf16[4,48,1536]{2,1,0:T(8,128)(2,1)S(1)}, bf16[4,48,1536]{2,1,0:T(8,128)(2,1)S(1)}, u32[]{:S(2)}, u32[]{:S(2)}) collective-permute-start(bf16[4,48,1536]{2,1,0:T(8,128)(2,1)S(1)} %pad_maximum_fusion.4.refs_1_), channel_id=1, source_target_pairs={{0,4},{1,3},{2,6},{3,1},{4,0},{5,7},{6,2},{7,5},{8,12},{9,11},{10,... | collective-permute-start | bytes 1769480 | tf_op jit(solution)/shard_map/ppermute | solution.py:520
  106.5 9.0 %copy-start.15 = (bf16[1024,768]{1,0:T(8,128)(2,1)S(1)}, bf16[1024,768]{1,0:T(8,128)(2,1)}, u32[]{:S(2)}) copy-start(bf16[1024,768]{1,0:T(8,128)(2,1)} %param.14) | copy-start | bytes 4718596
  106.5 9.0 %copy-start.45 = (f32[768]{0:T(1024)S(1)}, f32[768]{0:T(1024)}, u32[]{:S(2)}) copy-start(f32[768]{0:T(1024)} %param.20) | copy-start | bytes 9220
  111.8 3.8 %collective-permute-start.15 = (bf16[1024,768]{1,0:T(8,128)(2,1)}, bf16[1024,768]{1,0:T(8,128)(2,1)}, u32[]{:S(2)}, u32[]{:S(2)}) collective-permute-start(bf16[1024,768]{1,0:T(8,128)(2,1)} %convolution_convert_fusion), channel_id=1, source_target_pairs={{0,1},{1,0},{2,3},{3,2},{4,5},{5,4},{6,7},{7,6},{8,9},{9,8},{10,11... | collective-permute-start | bytes 4718600 | tf_op jit(solution)/shard_map/ppermute | solution.py:525
  111.8 11.1 %collective-permute-start.17 = (bf16[1024,768]{1,0:T(8,128)(2,1)}, bf16[1024,768]{1,0:T(8,128)(2,1)}, u32[]{:S(2)}, u32[]{:S(2)}) collective-permute-start(bf16[1024,768]{1,0:T(8,128)(2,1)} %cot_own_ref.1), channel_id=1, source_target_pairs={{0,1},{1,0},{2,3},{3,2},{4,5},{5,4},{6,7},{7,6},{8,9},{9,8},{10,11... | collective-permute-start | bytes 4718600 | tf_op jit(solution)/shard_map/ppermute | solution.py:525
  119.7 29.4 %copy-start.24 = (bf16[1024,768]{1,0:T(8,128)(2,1)}, bf16[1024,768]{1,0:T(8,128)(2,1)S(1)}, u32[]{:S(2)}) copy-start(bf16[1024,768]{1,0:T(8,128)(2,1)S(1)} %add_convert_fusion.1.own_ref) | copy-start | bytes 4718596
  119.7 30.4 %collective-permute-start.16 = (bf16[1024,768]{1,0:T(8,128)(2,1)S(1)}, bf16[1024,768]{1,0:T(8,128)(2,1)}, u32[]{:S(2)}, u32[]{:S(2)}) collective-permute-start(bf16[1024,768]{1,0:T(8,128)(2,1)S(1)} %add_convert_fusion.1.own_ref), channel_id=1, source_target_pairs={{0,1},{1,0},{2,3},{3,2},{4,5},{5,4},{6,7},{7,6},{8,9},{9,8},{10,11... | collective-permute-start | bytes 4718600 | tf_op jit(solution)/shard_map/ppermute | solution.py:525
  120.2 16.2 %collective-permute-start.19 = (bf16[8,48,1536]{2,1,0:T(8,128)(2,1)S(1)}, bf16[8,48,1536]{2,1,0:T(8,128)(2,1)S(1)}, u32[]{:S(2)}, u32[]{:S(2)}) collective-permute-start(bf16[8,48,1536]{2,1,0:T(8,128)(2,1)S(1)} %copy-done.22), channel_id=1, source_target_pairs={{0,2},{1,5},{2,0},{3,7},{4,6},{5,1},{6,4},{7,3},{8,10},{9,13},{10,... | collective-permute-start | bytes 3538952 | tf_op jit(solution)/shard_map/ppermute | solution.py:520
  121.7 27.4 %collective-permute-start.18 = (bf16[8,48,1536]{2,1,0:T(8,128)(2,1)S(1)}, bf16[8,48,1536]{2,1,0:T(8,128)(2,1)S(1)}, u32[]{:S(2)}, u32[]{:S(2)}) collective-permute-start(bf16[8,48,1536]{2,1,0:T(8,128)(2,1)S(1)} %copy-done.23), channel_id=1, source_target_pairs={{0,2},{1,5},{2,0},{3,7},{4,6},{5,1},{6,4},{7,3},{8,10},{9,13},{10,... | collective-permute-start | bytes 3538952 | tf_op jit(solution)/shard_map/ppermute | solution.py:520
  136.4 12.6 %copy-start.32 = (bf16[8,48,1536]{2,1,0:T(8,128)(2,1)}, bf16[8,48,1536]{2,1,0:T(8,128)(2,1)S(1)}, u32[]{:S(2)}) copy-start(bf16[8,48,1536]{2,1,0:T(8,128)(2,1)S(1)} %collective-permute-done.19.refs_3_) | copy-start | bytes 3538948
  193.0 3.7 %collective-permute-start.21 = (bf16[1024,768]{1,0:T(8,128)(2,1)}, bf16[1024,768]{1,0:T(8,128)(2,1)S(1)}, u32[]{:S(2)}, u32[]{:S(2)}) collective-permute-start(bf16[1024,768]{1,0:T(8,128)(2,1)} %get-tuple-element.77), channel_id=1, source_target_pairs={{0,1},{1,0},{2,3},{3,2},{4,5},{5,4},{6,7},{7,6},{8,9},{9,8},{10,11... | collective-permute-start | bytes 4718600 | tf_op jit(solution)/shard_map/ppermute | solution.py:525
  193.1 6.9 %collective-permute-start.20 = (bf16[1024,768]{1,0:T(8,128)(2,1)}, bf16[1024,768]{1,0:T(8,128)(2,1)S(1)}, u32[]{:S(2)}, u32[]{:S(2)}) collective-permute-start(bf16[1024,768]{1,0:T(8,128)(2,1)} %get-tuple-element.75), channel_id=1, source_target_pairs={{0,1},{1,0},{2,3},{3,2},{4,5},{5,4},{6,7},{7,6},{8,9},{9,8},{10,11... | collective-permute-start | bytes 4718600 | tf_op jit(solution)/shard_map/ppermute | solution.py:525
  193.6 40.8 %collective-permute-start.23 = (bf16[8,48,3072]{2,1,0:T(8,128)(2,1)}, bf16[8,48,3072]{2,1,0:T(8,128)(2,1)}, u32[]{:S(2)}, u32[]{:S(2)}) collective-permute-start(bf16[8,48,3072]{2,1,0:T(8,128)(2,1)} %get-tuple-element.85), channel_id=1, source_target_pairs={{0,2},{1,5},{2,0},{3,7},{4,6},{5,1},{6,4},{7,3},{8,10},{9,13},{10,... | collective-permute-start | bytes 7077896 | tf_op jit(solution)/shard_map/ppermute | solution.py:520
  206.8 3.5 collective-permute-start.22
  211.4 23.0 %slice-start = ((s8[4718592]{0:T(1024)(128)(4,1)}), s8[4194304]{0:T(1024)(128)(4,1)S(1)}, s32[]{:S(2)}) async-start(s8[4718592]{0:T(1024)(128)(4,1)} %bitcast.55), calls=%async_computation | async-start | bytes 8388608
  211.4 23.0 %slice-start.1 = ((s8[4718592]{0:T(1024)(128)(4,1)}), s8[524288]{0:T(1024)(128)(4,1)S(1)}, s32[]{:S(2)}) async-start(s8[4718592]{0:T(1024)(128)(4,1)} %bitcast.55), calls=%async_computation.1 | async-start | bytes 1048576
  211.4 23.0 %copy-start.11 = (s32[2]{0:T(128)S(1)}, s32[2]{0:T(128)}, u32[]{:S(2)}) copy-start(s32[2]{0:T(128)} %copy-done.9) | copy-start | bytes 28
  239.6 31.9 %collective-permute-start.24 = (bf16[4,48,3072]{2,1,0:T(8,128)(2,1)}, bf16[4,48,3072]{2,1,0:T(8,128)(2,1)S(1)}, u32[]{:S(2)}, u32[]{:S(2)}) collective-permute-start(bf16[4,48,3072]{2,1,0:T(8,128)(2,1)} %get-tuple-element.86.refs_0_), channel_id=1, source_target_pairs={{0,4},{1,3},{2,6},{3,1},{4,0},{5,7},{6,2},{7,5},{8,12},{9,11},{10,... | collective-permute-start | bytes 3538952 | tf_op jit(solution)/shard_map/ppermute | solution.py:520
  240.3 28.6 %collective-permute-start.25 = (bf16[8,48,512]{2,1,0:T(8,128)(2,1)S(1)}, bf16[8,48,512]{2,1,0:T(8,128)(2,1)S(1)}, u32[]{:S(2)}, u32[]{:S(2)}) collective-permute-start(bf16[8,48,512]{2,1,0:T(8,128)(2,1)S(1)} %copy-done.36), channel_id=1, source_target_pairs={{0,2},{1,5},{2,0},{3,7},{4,6},{5,1},{6,4},{7,3},{8,10},{9,13},{10,... | collective-permute-start | bytes 1179656 | tf_op jit(solution)/shard_map/ppermute | solution.py:520
  271.5 27.3 %slice-start.2 = ((s8[4718592]{0:T(1024)(128)(4,1)}), s8[524288]{0:T(1024)(128)(4,1)S(1)}, s32[]{:S(2)}) async-start(s8[4718592]{0:T(1024)(128)(4,1)} %bitcast.68), calls=%async_computation.2 | async-start | bytes 1048576
  274.8 24.0 %slice-start.3 = ((s8[4718592]{0:T(1024)(128)(4,1)}), s8[4194304]{0:T(1024)(128)(4,1)S(1)}, s32[]{:S(2)}) async-start(s8[4718592]{0:T(1024)(128)(4,1)} %bitcast.68), calls=%async_computation.3 | async-start | bytes 8388608
  300.7 12.1 %copy-start.13 = (s32[2]{0:T(128)S(1)}, s32[2]{0:T(128)}, u32[]{:S(2)}) copy-start(s32[2]{0:T(128)} %copy-done.9) | copy-start | bytes 28
  300.7 15.0 %copy-start.43 = (f32[2,768]{1,0:T(2,128)S(1)}, f32[2,768]{1,0:T(2,128)}, u32[]{:S(2)}) copy-start(f32[2,768]{1,0:T(2,128)} %get-tuple-element.98) | copy-start | bytes 18436
  300.7 15.0 %copy-start.44 = (f32[2,768]{1,0:T(2,128)S(1)}, f32[2,768]{1,0:T(2,128)}, u32[]{:S(2)}) copy-start(f32[2,768]{1,0:T(2,128)} %get-tuple-element.99) | copy-start | bytes 18436
  300.7 15.7 %copy-start.49 = (f32[1,384]{1,0:T(1,128)S(1)}, f32[1,384]{1,0:T(1,128)}, u32[]{:S(2)}) copy-start(f32[1,384]{1,0:T(1,128)} %get-tuple-element.102) | copy-start | bytes 4612
  300.7 15.7 %copy-start.50 = (f32[1,384]{1,0:T(1,128)S(1)}, f32[1,384]{1,0:T(1,128)}, u32[]{:S(2)}) copy-start(f32[1,384]{1,0:T(1,128)} %get-tuple-element.103) | copy-start | bytes 4612
  300.7 15.7 %copy-start.51 = (f32[1,384]{1,0:T(1,128)S(1)}, f32[1,384]{1,0:T(1,128)}, u32[]{:S(2)}) copy-start(f32[1,384]{1,0:T(1,128)} %get-tuple-element.104) | copy-start | bytes 4612
  300.7 17.4 %copy-start = (f32[8,48,1024]{2,1,0:T(8,128)S(1)}, f32[8,48,1024]{2,1,0:T(8,128)}, u32[]{:S(2)}) copy-start(f32[8,48,1024]{2,1,0:T(8,128)} %get-tuple-element.111.keep_ref.send_ref) | copy-start | bytes 4718596
  304.1 31.5 %collective-permute-start.26 = (bf16[1024,768]{1,0:T(8,128)(2,1)}, bf16[1024,768]{1,0:T(8,128)(2,1)}, u32[]{:S(2)}, u32[]{:S(2)}) collective-permute-start(bf16[1024,768]{1,0:T(8,128)(2,1)} %fusion.21.refs_0_), channel_id=1, source_target_pairs={{0,1},{1,0},{2,3},{3,2},{4,5},{5,4},{6,7},{7,6},{8,9},{9,8},{10,11... | collective-permute-start | bytes 4718600 | tf_op jit(solution)/shard_map/ppermute | solution.py:525
  304.1 8.0 %collective-permute-start.32 = (bf16[4,48,512]{2,1,0:T(8,128)(2,1)}, bf16[4,48,512]{2,1,0:T(8,128)(2,1)S(1)}, u32[]{:S(2)}, u32[]{:S(2)}) collective-permute-start(bf16[4,48,512]{2,1,0:T(8,128)(2,1)} %get-tuple-element.96.refs_2_), channel_id=1, source_target_pairs={{0,4},{1,3},{2,6},{3,1},{4,0},{5,7},{6,2},{7,5},{8,12},{9,11},{10,... | collective-permute-start | bytes 589832 | tf_op jit(solution)/shard_map/ppermute | solution.py:520
  305.4 12.6 %collective-permute-start.35 = (bf16[8,48,1024]{2,1,0:T(8,128)(2,1)}, bf16[8,48,1024]{2,1,0:T(8,128)(2,1)}, u32[]{:S(2)}, u32[]{:S(2)}) collective-permute-start(bf16[8,48,1024]{2,1,0:T(8,128)(2,1)} %get-tuple-element.112), channel_id=1, source_target_pairs={{0,2},{1,5},{2,0},{3,7},{4,6},{5,1},{6,4},{7,3},{8,10},{9,13},{10,... | collective-permute-start | bytes 2359304 | tf_op jit(solution)/shard_map/ppermute | solution.py:520
  306.0 23.8 %collective-permute-start.39 = (bf16[2,48,3072]{2,1,0:T(8,128)(2,1)}, bf16[2,48,3072]{2,1,0:T(8,128)(2,1)S(1)}, u32[]{:S(2)}, u32[]{:S(2)}) collective-permute-start(bf16[2,48,3072]{2,1,0:T(8,128)(2,1)} %copy-done.8), channel_id=1, source_target_pairs={{0,8},{1,9},{2,10},{3,11},{4,12},{5,13},{6,14},{7,15},{8,0},{9,1},... | collective-permute-start | bytes 1769480 | tf_op jit(solution)/shard_map/ppermute | solution.py:520
  315.6 7.9 %collective-permute-start.33 = (bf16[2,48,512]{2,1,0:T(8,128)(2,1)}, bf16[2,48,512]{2,1,0:T(8,128)(2,1)S(1)}, u32[]{:S(2)}, u32[]{:S(2)}) collective-permute-start(bf16[2,48,512]{2,1,0:T(8,128)(2,1)} %get-tuple-element.108), channel_id=1, source_target_pairs={{0,8},{1,9},{2,10},{3,11},{4,12},{5,13},{6,14},{7,15},{8,0},{9,1},... | collective-permute-start | bytes 294920 | tf_op jit(solution)/shard_map/ppermute | solution.py:520
  318.1 11.7 %copy-start.4 = (f32[2,48,3072]{2,1,0:T(8,128)S(1)}, f32[2,48,3072]{2,1,0:T(8,128)}, u32[]{:S(2)}) copy-start(f32[2,48,3072]{2,1,0:T(8,128)} %copy-done.3) | copy-start | bytes 3538948
  318.1 17.6 %copy-start.35 = (bf16[2048,1152]{1,0:T(8,128)(2,1)S(1)}, bf16[2048,1152]{1,0:T(8,128)(2,1)}, u32[]{:S(2)}) copy-start(bf16[2048,1152]{1,0:T(8,128)(2,1)} %copy-done.34) | copy-start | bytes 14155780
  321.1 11.8 %collective-permute-start.36 = (bf16[4,48,1024]{2,1,0:T(8,128)(2,1)S(1)}, bf16[4,48,1024]{2,1,0:T(8,128)(2,1)S(1)}, u32[]{:S(2)}, u32[]{:S(2)}) collective-permute-start(bf16[4,48,1024]{2,1,0:T(8,128)(2,1)S(1)} %get-tuple-element.114), channel_id=1, source_target_pairs={{0,4},{1,3},{2,6},{3,1},{4,0},{5,7},{6,2},{7,5},{8,12},{9,11},{10,... | collective-permute-start | bytes 1179656 | tf_op jit(solution)/shard_map/ppermute | solution.py:520
  324.1 11.5 %copy-start.16 = (bf16[1024,768]{1,0:T(8,128)(2,1)S(1)}, bf16[1024,768]{1,0:T(8,128)(2,1)}, u32[]{:S(2)}) copy-start(bf16[1024,768]{1,0:T(8,128)(2,1)} %param.14) | copy-start | bytes 4718596
  324.2 11.5 %copy-start.27 = (bf16[768,768]{1,0:T(8,128)(2,1)S(1)}, bf16[768,768]{1,0:T(8,128)(2,1)}, u32[]{:S(2)}) copy-start(bf16[768,768]{1,0:T(8,128)(2,1)} %copy-done.25) | copy-start | bytes 3538948
  324.2 5.6 %collective-permute-start.34 = (bf16[1,48,512]{2,1,0:T(8,128)(2,1)S(1)}, bf16[1,48,512]{2,1,0:T(8,128)(2,1)S(1)}, u32[]{:S(2)}, u32[]{:S(2)}) collective-permute-start(bf16[1,48,512]{2,1,0:T(8,128)(2,1)S(1)} %get-tuple-element.110), channel_id=1, source_target_pairs={{0,16},{1,17},{2,18},{3,19},{4,20},{5,21},{6,22},{7,23},{8,24},{9,... | collective-permute-start | bytes 147464 | tf_op jit(solution)/shard_map/ppermute | solution.py:520
  331.1 14.0 %collective-permute-start.40 = (bf16[1,48,3072]{2,1,0:T(8,128)(2,1)S(1)}, bf16[1,48,3072]{2,1,0:T(8,128)(2,1)S(1)}, u32[]{:S(2)}, u32[]{:S(2)}) collective-permute-start(bf16[1,48,3072]{2,1,0:T(8,128)(2,1)S(1)} %get-tuple-element.121), channel_id=1, source_target_pairs={{0,16},{1,17},{2,18},{3,19},{4,20},{5,21},{6,22},{7,23},{8,24},{9,... | collective-permute-start | bytes 884744 | tf_op jit(solution)/shard_map/ppermute | solution.py:520
  333.6 11.5 %collective-permute-start.37 = (bf16[2,48,1024]{2,1,0:T(8,128)(2,1)S(1)}, bf16[2,48,1024]{2,1,0:T(8,128)(2,1)S(1)}, u32[]{:S(2)}, u32[]{:S(2)}) collective-permute-start(bf16[2,48,1024]{2,1,0:T(8,128)(2,1)S(1)} %get-tuple-element.116), channel_id=1, source_target_pairs={{0,8},{1,9},{2,10},{3,11},{4,12},{5,13},{6,14},{7,15},{8,0},{9,1},... | collective-permute-start | bytes 589832 | tf_op jit(solution)/shard_map/ppermute | solution.py:520
  343.5 3.9 %collective-permute-start.27 = (f32[6912]{0:T(1024)S(1)}, f32[6912]{0:T(1024)S(1)}, u32[]{:S(2)}, u32[]{:S(2)}) collective-permute-start(f32[6912]{0:T(1024)S(1)} %constant_dynamic-update-slice_fusion.7), channel_id=1, source_target_pairs={{0,2},{1,3},{2,0},{3,1},{4,6},{5,7},{6,4},{7,5},{8,10},{9,11},{10,... | collective-permute-start | bytes 82952 | tf_op jit(solution)/shard_map/ppermute | solution.py:520
  345.8 7.4 %collective-permute-start.38 = (bf16[1,48,1024]{2,1,0:T(8,128)(2,1)S(1)}, bf16[1,48,1024]{2,1,0:T(8,128)(2,1)S(1)}, u32[]{:S(2)}, u32[]{:S(2)}) collective-permute-start(bf16[1,48,1024]{2,1,0:T(8,128)(2,1)S(1)} %get-tuple-element.118), channel_id=1, source_target_pairs={{0,16},{1,17},{2,18},{3,19},{4,20},{5,21},{6,22},{7,23},{8,24},{9,... | collective-permute-start | bytes 294920 | tf_op jit(solution)/shard_map/ppermute | solution.py:520
  347.5 3.9 %collective-permute-start.28 = (f32[6912]{0:T(1024)S(1)}, f32[6912]{0:T(1024)S(1)}, u32[]{:S(2)}, u32[]{:S(2)}) collective-permute-start(f32[6912]{0:T(1024)S(1)} %add.180), channel_id=1, source_target_pairs={{0,4},{1,5},{2,6},{3,7},{4,0},{5,1},{6,2},{7,3},{8,12},{9,13},{10,... | collective-permute-start | bytes 82952 | tf_op jit(solution)/shard_map/ppermute | solution.py:520
  351.4 3.9 %collective-permute-start.29 = (f32[6912]{0:T(1024)S(1)}, f32[6912]{0:T(1024)S(1)}, u32[]{:S(2)}, u32[]{:S(2)}) collective-permute-start(f32[6912]{0:T(1024)S(1)} %add.181), channel_id=1, source_target_pairs={{0,8},{1,9},{2,10},{3,11},{4,12},{5,13},{6,14},{7,15},{8,0},{9,1},... | collective-permute-start | bytes 82952 | tf_op jit(solution)/shard_map/ppermute | solution.py:520
  355.2 4.8 %collective-permute-start.30 = (f32[6912]{0:T(1024)S(1)}, f32[6912]{0:T(1024)S(1)}, u32[]{:S(2)}, u32[]{:S(2)}) collective-permute-start(f32[6912]{0:T(1024)S(1)} %add.182), channel_id=1, source_target_pairs={{0,16},{1,17},{2,18},{3,19},{4,20},{5,21},{6,22},{7,23},{8,24},{9,... | collective-permute-start | bytes 82952 | tf_op jit(solution)/shard_map/ppermute | solution.py:520
  360.0 3.0 collective-permute-start.31
  (33 other events, 100.0 us)
where the time goes:
time: 368 us; the launch traced here: 364 us
  Pallas kernels  173 us (47%)
  waiting for transfers between devices  74.8 us (20%)
  starting transfers between devices  42.1 us (11%)
  local copies, waits for them, and re-layouts  29.7 us (8%)
  other arithmetic  27.5 us (7%)
  matrix products  13.7 us (4%)
    pallas_call x3, Pallas kernels, attend_backward(): pl.pallas_call(functools.partial(backward_kernel, rows=256, ties=len(ties...  69.8 us
    ppermute x32, waiting for transfers between devices, exchange(): return lax.ppermute(block, ('dp', 'tensor'), pairs)  69.3 us
    pallas_call x1, Pallas kernels, feed_forward(): pl.pallas_call(functools.partial(feed_forward_kernel, blocks=blocks, plac...  42.9 us
    ppermute x32, starting transfers between devices, exchange(): return lax.ppermute(block, ('dp', 'tensor'), pairs)  40.5 us
    pallas_call x3, Pallas kernels, attend_forward(): pl.pallas_call(functools.partial(forward_kernel, rows=512, halves=halves)...  37.5 us
    unnamed x129, local copies, waits for them, and re-layouts  18.7 us
    pallas_call x9, Pallas kernels, join_halves(): pl.pallas_call(join_kernel, grid_spec=pltpu.PrefetchScalarGridSpec(num_sc...  17.2 us
    dot_general x4, matrix products, dot(): lax.dot_general(left, right, (((left_axis,), (right_axis,)), ((), ())), p...  13.7 us
  transfers between devices with their start and end apart: 41, of which 17 were waited for; matrix products, arithmetic and copies ran while one was open for 13% of the time, Pallas kernels for 24%

commit v1 on v0

--- a/solution.py
+++ b/solution.py
@@ -140,12 +140,20 @@
 ):
     before_ref = refs[0]
     result_ref, sums_ref, vector_ref, token_ref = refs[ties : ties + 4]
-    grad_ref, dq_ref, product_ref = refs[-3:]
+    grad_ref, dq_ref, product_ref, rows_ref, sems = refs[-5:]
     token_ref[...] = jnp.zeros_like(token_ref)
     tokens = qkv_ref.shape[0]
     part = own_ref.shape[0]
-    grad_ref[pl.ds(pl.multiple_of(info_ref[1] * part, part), part), :] = own_ref[...]
-    grad_ref[pl.ds(pl.multiple_of((1 - info_ref[1]) * part, part), part), :] = other_ref[...]
+    own_rows = pl.ds(pl.multiple_of(info_ref[1] * part, part), part)
+    other_rows = pl.ds(pl.multiple_of((1 - info_ref[1]) * part, part), part)
+    own_copy = pltpu.make_async_copy(own_ref, grad_ref.at[own_rows, :], sems.at[0])
+    other_copy = pltpu.make_async_copy(other_ref, grad_ref.at[other_rows, :], sems.at[1])
+    rows_copy = pltpu.make_async_copy(normed_ref, rows_ref, sems.at[2])
+    own_copy.start()
+    other_copy.start()
+    rows_copy.start()
+    own_copy.wait()
+    other_copy.wait()
 
     lane = lax.broadcasted_iota(jnp.int32, (1, PAIR), 1)
     mine = [lane < HEAD_DIM, lane >= HEAD_DIM]
@@ -196,7 +204,8 @@
     result = result_ref[...]
     sums = jnp.sum(result.astype(F32), axis=0, keepdims=True)
     sums_ref[...] = sums
-    weight_grad = jnp.transpose(dot(result, normed_ref[...], 0, 0))
+    rows_copy.wait()
+    weight_grad = jnp.transpose(dot(result, rows_ref[...], 0, 0))
     out_weight_grad = jnp.transpose(dot(out, grad_ref[...], 0, 0))
     high = sums.astype(BF16)
     low = (sums - high.astype(F32)).astype(BF16)
@@ -241,7 +250,7 @@
     blocks,
     placed,
 ):
-    weights, refs = refs[: 2 if placed else 4], refs[2 if placed else 4 :]
+    weights, refs = refs[:2], refs[2:]
     terms_own_ref, terms_other_ref, back_own_ref, back_other_ref, sums_ref = refs[:5]
     refs = refs[5:]
     step = pl.program_id(0)
@@ -259,7 +268,9 @@
             copies = []
             for number, target in enumerate((fc_ref, proj_ref)):
                 for place in range(count):
-                    source = weights[2 * number + place // half].at[place % half]
+                    source = weights[place // half].at[
+                        place % half, :, pl.ds(number * target.shape[2], target.shape[2])
+                    ]
                     copies.append(
                         pltpu.make_async_copy(
                             source,
@@ -381,7 +392,7 @@
 
 
 def attend_backward(
-    pair, kind, projected, heads_flat, lse, info, own, other, normed, weight, out_weight, norm, ties
+    pair, kind, projected, heads, lse, weight, info, own, other, normed, out_weight, norm, ties
 ):
     tokens, columns = projected.shape
     features = normed.shape[1]
@@ -420,12 +431,12 @@
         in_specs=[
             scalars,
             fixed(projected.shape),
-            pl.BlockSpec((tokens, PAIR), lambda _: (0, pair)),
+            fixed(heads.shape),
             fixed(lse.shape),
-            fixed(own.shape),
-            fixed(other.shape),
-            fixed(normed.shape),
-            pl.BlockSpec((features, columns), lambda _: (0, pair)),
+            ANY_SPEC,
+            ANY_SPEC,
+            ANY_SPEC,
+            fixed(weight.shape),
             pl.BlockSpec((features, PAIR), lambda _: (0, pair)),
             fixed(norm.shape),
         ]
@@ -436,11 +447,13 @@
             pltpu.VMEM((tokens, features), BF16),
             pltpu.VMEM((PAIR, tokens), F32),
             product,
+            pltpu.VMEM((tokens, features), BF16),
+            pltpu.SemaphoreType.DMA((3,)),
         ],
         compiler_params=pltpu.CompilerParams(vmem_limit_bytes=VMEM_BYTES),
         cost_estimate=SMALL_COST,
         name=f"attend_backward_{pair}",
-    )(info, projected, heads_flat, lse, own, other, normed, weight, out_weight, norm, *ties)
+    )(info, projected, heads, lse, own, other, normed, weight, out_weight, norm, *ties)
     if kind == "whole":
         gradient = out[4]
     elif shard % 16:
@@ -450,7 +463,7 @@
     return out[0], out[1], out[2], out[3], gradient
 
 
-def feed_forward(info, own, other, cot_own, cot_other, bias, fc, proj):
+def feed_forward(info, own, other, cot_own, cot_other, bias, gather):
     tokens, features = own.shape
     hidden = bias.shape[0]
     block = 512
@@ -465,10 +478,11 @@
         jax.ShapeDtypeStruct((tokens, features), kind) for kind in (F32, BF16, F32, BF16)
     ] + [jax.ShapeDtypeStruct((1, hidden), F32)]
     scratch = []
-    weights = [fc.held, fc.got, proj.held, proj.got]
-    weight_specs = [ANY_SPEC] * 4
+    weights = [gather.held, gather.got]
+    weight_specs = [ANY_SPEC] * 2
     if placed:
-        weights = [fc.result(), proj.result()]
+        both = gather.result()
+        weights = [both[:, :hidden], both[:, hidden:]]
         weight_specs = [pl.BlockSpec((features, hidden), lambda i: (0, 0))] * 2
         out_specs += [pl.BlockSpec((features, hidden), lambda i: (0, 0))] * 2
         out_shape += [jax.ShapeDtypeStruct((features, hidden), F32)] * 2
@@ -509,6 +523,215 @@
     return (*out[:5], Scatter(*out[5:]))
 
 
+def block_call(kernel, grid, in_specs, operands, out, scratch=(), name=None, ties=()):
+    return pl.pallas_call(
+        kernel,
+        grid=grid,
+        in_specs=list(in_specs) + [ANY_SPEC] * len(ties),
+        out_specs=[pl.BlockSpec(block, index) for _, _, block, index in out],
+        out_shape=[jax.ShapeDtypeStruct(shape, kind) for shape, kind, _, _ in out],
+        scratch_shapes=list(scratch),
+        compiler_params=pltpu.CompilerParams(vmem_limit_bytes=VMEM_BYTES),
+        cost_estimate=SMALL_COST,
+        name=name,
+    )(*operands, *ties)
+
+
+def whole_spec(array):
+    return pl.BlockSpec(array.shape, lambda *_: (0,) * array.ndim)
+
+
+def out_product_kernel(info_ref, weight_ref, *refs):
+    heads_refs, (own_ref, other_ref) = refs[:-2], refs[-2:]
+    half = own_ref.shape[0]
+    for target, at in ((other_ref, 1 - info_ref[1]), (own_ref, info_ref[1])):
+        here = pl.ds(pl.multiple_of(at * half, half), half)
+        heads = jnp.concatenate([ref[here, :] for ref in heads_refs], axis=1)
+        target[...] = dot(heads, weight_ref[...], 1, 1).astype(target.dtype)
+
+
+def out_product(info, weight, heads):
+    half = heads[0].shape[0] // 2
+    width = weight.shape[0]
+    return block_call(
+        out_product_kernel,
+        (1,),
+        [pl.BlockSpec(memory_space=pltpu.SMEM), whole_spec(weight)] + [whole_spec(h) for h in heads],
+        [info, weight, *heads],
+        [((half, width), kind, (half, width), lambda _: (0, 0)) for kind in (F32, BF16)],
+        name="out_product",
+    )
+
+
+def back_product_kernel(info_ref, *refs, pairs):
+    own_ref, other_ref = refs[-2:]
+    half = own_ref.shape[0]
+    for target, at in ((other_ref, 1 - info_ref[1]), (own_ref, info_ref[1])):
+        here = pl.ds(pl.multiple_of(at * half, half), half)
+        total = 0.0
+        for result, weight in zip(refs[:pairs], refs[pairs : 2 * pairs]):
+            total = total + dot(result[here, :], weight[...], 1, 1)
+        target[...] = total.astype(target.dtype)
+
+
+def back_product(info, results, weights, ties):
+    half = results[0].shape[0] // 2
+    width = weights[0].shape[0]
+    return block_call(
+        functools.partial(back_product_kernel, pairs=len(results)),
+        (1,),
+        [pl.BlockSpec(memory_space=pltpu.SMEM)] + [whole_spec(a) for a in (*results, *weights)],
+        [info, *results, *weights],
+        [((half, width), kind, (half, width), lambda _: (0, 0)) for kind in (F32, BF16)],
+        name="back_product",
+        ties=ties,
+    )
+
+
+def middle_kernel(hidden_ref, own_ref, other_ref, bias_ref, norm_ref, *refs):
+    middle_ref, normed_ref = refs[-2:]
+    middle = (
+        hidden_ref[...].astype(F32) + (own_ref[...] + other_ref[...].astype(F32)) + bias_ref[...]
+    )
+    middle_ref[...] = middle
+    normed_ref[...] = norm_layer(middle, norm_ref[0:1, :], norm_ref[1:2, :]).astype(BF16)
+
+
+def middle_norm(hidden, own, other, bias, norm, ties):
+    rows, width = hidden.shape
+    tile = pl.BlockSpec((256, width), lambda i: (i, 0))
+    return block_call(
+        middle_kernel,
+        (rows // 256,),
+        [tile, tile, tile, whole_spec(bias), whole_spec(norm)],
+        [hidden, own, other, bias, norm],
+        [(hidden.shape, kind, (256, width), lambda i: (i, 0)) for kind in (F32, BF16)],
+        name="middle_norm",
+        ties=ties,
+    )
+
+
+def norm_slope(rows, grad, gain):
+    centred = rows - jnp.mean(rows, axis=-1, keepdims=True)
+    scale = lax.rsqrt(jnp.mean(centred * centred, axis=-1, keepdims=True) + 1e-05)
+    normalised = centred * scale
+    scaled = grad * gain
+    back = scale * (
+        scaled
+        - jnp.mean(scaled, axis=-1, keepdims=True)
+        - normalised * jnp.mean(scaled * normalised, axis=-1, keepdims=True)
+    )
+    return normalised, back
+
+
+def middle_back_kernel(
+    middle_ref, own_ref, other_ref, cot_ref, norm_ref, grad_ref, attn_ref, sums_ref
+):
+    @pl.when(pl.program_id(0) == 0)
+    def _():
+        sums_ref[...] = jnp.zeros_like(sums_ref)
+
+    back = own_ref[...] + other_ref[...].astype(F32)
+    cot = cot_ref[...].astype(F32)
+    normalised, through = norm_slope(middle_ref[...], back, norm_ref[0:1, :])
+    grad = cot + through
+    attn = grad.astype(BF16)
+    grad_ref[...] = grad
+    attn_ref[...] = attn
+    for row, values in enumerate((back * normalised, back, attn.astype(F32), cot)):
+        sums_ref[row : row + 1, :] += jnp.sum(values, axis=0, keepdims=True)
+
+
+def middle_back(middle, own, other, cot, norm):
+    rows, width = middle.shape
+    tile = pl.BlockSpec((256, width), lambda i: (i, 0))
+    return block_call(
+        middle_back_kernel,
+        (rows // 256,),
+        [tile, tile, tile, tile, whole_spec(norm)],
+        [middle, own, other, cot, norm],
+        [(middle.shape, kind, (256, width), lambda i: (i, 0)) for kind in (F32, BF16)]
+        + [((8, width), F32, (8, width), lambda i: (0, 0))],
+        name="middle_back",
+    )
+
+
+def first_back_kernel(hidden_ref, own_ref, other_ref, grad_ref, norm_ref, *refs):
+    result_ref = refs[-1]
+    back = own_ref[...] + other_ref[...].astype(F32)
+    _, through = norm_slope(hidden_ref[...].astype(F32), back, norm_ref[0:1, :])
+    result_ref[...] = (grad_ref[...] + through).astype(BF16)
+
+
+def first_back(hidden, own, other, grad, norm, ties):
+    rows, width = hidden.shape
+    tile = pl.BlockSpec((256, width), lambda i: (i, 0))
+    return block_call(
+        first_back_kernel,
+        (rows // 256,),
+        [tile, tile, tile, tile, whole_spec(norm)],
+        [hidden, own, other, grad, norm],
+        [(hidden.shape, BF16, (256, width), lambda i: (i, 0))],
+        name="first_back",
+        ties=ties,
+    )[0]
+
+
+def vectors_kernel(early_ref, hidden_ref, *refs, pairs):
+    out_ref = refs[-1]
+    width = out_ref.shape[1]
+    out_ref[...] = jnp.zeros_like(out_ref)
+    out_ref[0:2, :] = sum(ref[...] for ref in refs[:pairs])
+    out_ref[2:6, :] = early_ref[0:4, :]
+    wide = hidden_ref.shape[1] // width
+    for row in range(wide):
+        out_ref[6 + row : 7 + row, :] = hidden_ref[:, row * width : (row + 1) * width]
+    for pair, ref in enumerate(refs[pairs : 2 * pairs]):
+        start = pair * PAIR
+        out_ref[6 + wide : 7 + wide, start : start + PAIR] = ref[:, :PAIR]
+        start += pairs * PAIR
+        out_ref[6 + wide : 7 + wide, start : start + PAIR] = ref[:, 2 * PAIR :]
+
+
+def vectors_of(early, hidden, parts, sums, ties):
+    operands = [early, hidden, *parts, *sums]
+    return block_call(
+        functools.partial(vectors_kernel, pairs=len(parts)),
+        (1,),
+        [whole_spec(a) for a in operands],
+        operands,
+        [((16, early.shape[1]), F32, (16, early.shape[1]), lambda _: (0, 0))],
+        name="vectors",
+        ties=ties,
+    )[0]
+
+
+def join_gathered_kernel(token_ref, held_ref, got_ref, *refs):
+    @pl.when(pl.program_id(0) == 0)
+    def _():
+        refs[-1][...] = held_ref[...]
+
+    @pl.when(pl.program_id(0) == 1)
+    def _():
+        refs[-1][...] = got_ref[...]
+
+
+def join_gathered(held, got, token, ties):
+    if held.shape[1] % 16 or token is None:
+        return jnp.concatenate([held, got], axis=0)
+    count, rows, columns = held.shape
+    token = token.reshape(1, 1)
+    return block_call(
+        join_gathered_kernel,
+        (2,),
+        [pl.BlockSpec(memory_space=pltpu.SMEM), whole_spec(held), whole_spec(got)],
+        [token, held, got],
+        [((2 * count, rows, columns), held.dtype, held.shape, lambda i: (i, 0, 0))],
+        name="join_gathered",
+        ties=ties,
+    )[0]
+
+
 def exchange(block, bits):
     count = lax.axis_size("dp")
     width = lax.axis_size("tensor")
@@ -532,13 +755,10 @@
         self.step = 0
         self.got = exchange(self.held, self.orders[0])
 
-    def advance(self, token=None):
+    def advance(self, token=None, ties=()):
         self.step += 1
         if self.step < len(self.orders):
-            joined = [self.held, self.got]
-            if token is not None:
-                joined = [part + token.astype(BF16) for part in joined]
-            self.held = jnp.concatenate(joined, axis=0)
+            self.held = join_gathered(self.held, self.got, token, ties)
             self.got = exchange(self.held, self.orders[self.step])
         return self
 
@@ -649,10 +869,20 @@
         return (self.kept + self.got.astype(F32))[0]
 
 
-def sum_vectors(vector, both):
-    for bit in range(bits_of(lax.axis_size("dp"))):
-        vector = vector + exchange(vector, (bit, bit))
-    return jnp.concatenate([vector[:both] + swap(vector[:both]), vector[both:]])
+class VectorSum:
+    def __init__(self, rows, both):
+        self.rows, self.both, self.bit = rows, both, 0
+
+    def advance(self, steps=1):
+        for _ in range(steps):
+            if self.bit < bits_of(lax.axis_size("dp")):
+                self.rows = self.rows + exchange(self.rows, (self.bit, self.bit))
+                self.bit += 1
+        return self.rows
+
+    def result(self):
+        self.advance(bits_of(lax.axis_size("dp")))
+        return self.rows[: self.both] + swap(self.rows[: self.both]), self.rows[self.both :]
 
 
 def per_device(
@@ -671,25 +901,18 @@
     proj_bias,
     cotangent,
 ):
-    tensor_pos = lax.axis_index("tensor")
-    half = hidden_in.shape[0]
     width = hidden_in.shape[1]
     shard_rows = qkv_weight.shape[0]
     head_width = qkv_weight.shape[2]
     pairs = head_width // PAIR
     columns = 3 * PAIR
 
-    def split_rows(whole):
-        own = lax.dynamic_slice_in_dim(whole, tensor_pos * half, half, 0)
-        other = lax.dynamic_slice_in_dim(whole, (1 - tensor_pos) * half, half, 0)
-        return own, other
-
     by_pair = qkv_weight.reshape(shard_rows, 3, pairs, PAIR).swapaxes(1, 2)
     by_pair = by_pair.reshape(shard_rows, pairs * columns)
-    first_gather = Gather(by_pair[:, :columns])
-    rest_gather = Gather(jnp.concatenate([by_pair[:, columns:], out_weight], axis=1))
-    fc_gather = Gather(fc_weight)
-    proj_gather = Gather(proj_weight)
+    early = pairs - 1
+    first_gather = Gather(by_pair[:, : early * columns])
+    rest_gather = Gather(jnp.concatenate([by_pair[:, early * columns :], out_weight], axis=1))
+    ff_gather = Gather(jnp.concatenate([fc_weight, proj_weight], axis=1))
 
     rows_first = hidden_in.astype(F32)
     row_mean = jnp.mean(rows_first, axis=-1, keepdims=True)
@@ -702,67 +925,52 @@
 
     bias_parts = jnp.stack([qv_bias[0], jnp.zeros_like(qv_bias[0]), qv_bias[1]])
     bias_cols = bias_parts.reshape(3, pairs, PAIR).swapaxes(0, 1).reshape(pairs, 1, columns)
-    fc_gather.advance()
-    proj_gather.advance()
-    full_qkv = [first_gather.result()]
+    ff_gather.advance()
+    weights = first_gather.result()
+    qkv_weights = [weights[:, p * columns : (p + 1) * columns] for p in range(early)]
     projected, heads, lses = [], [], []
     for pair in range(pairs):
-        weight = full_qkv[pair]
         normed_first, columns_out, heads_out, lse, token = attend_forward(
             pair,
             normed_first,
-            weight,
+            qkv_weights[pair],
             bias_cols[pair],
-            [fc_gather.held, proj_gather.held] if pair else [],
+            [ff_gather.held] if pair else [],
         )
         projected.append(columns_out)
         heads.append(heads_out)
         lses.append(lse)
-        if pair == 0:
+        if pair == early - 1:
             rest = rest_gather.result(token)
-            full_qkv += [
-                rest[:, p * columns : (p + 1) * columns] for p in range(pairs - 1)
-            ]
-            full_out = rest[:, (pairs - 1) * columns :]
+            qkv_weights.append(rest[:, :columns])
+            full_out = rest[:, columns:]
         if pair < pairs - 1:
-            fc_gather.advance(token)
-            proj_gather.advance(token)
-    full_qkv = jnp.concatenate(full_qkv, axis=1)
-    heads_flat = jnp.concatenate(heads, axis=1)
-    heads_own, heads_other = split_rows(heads_flat)
-    attn_other = swap(dot(heads_other, full_out, 1, 1).astype(BF16))
-    middle = rows_first + (dot(heads_own, full_out, 1, 1) + attn_other.astype(F32)) + out_bias
-
-    normed_mid, second_back = jax.vjp(norm_layer, middle, second_gain, second_shift)
-    normed_own = normed_mid.astype(BF16)
+            ff_gather.advance(token)
+
+    attn_own, attn_other = out_product(info, full_out, heads)
+    norm_second = jnp.stack([second_gain, second_shift])
+    middle, normed_own = middle_norm(
+        hidden_in,
+        attn_own,
+        swap(attn_other),
+        out_bias[None],
+        norm_second,
+        [],
+    )
     normed_other = swap(normed_own)
-
     terms_own, terms_other, back_own, back_other, sum_fc, ff_sum = feed_forward(
-        info, normed_own, normed_other, cotangent, cot_other, fc_bias, fc_gather, proj_gather
+        info, normed_own, normed_other, cotangent, cot_other, fc_bias, ff_gather
     )
     back_other = swap(back_other)
     terms_other = swap(terms_other)
     block_out = (middle + (terms_own + terms_other.astype(F32)) + proj_bias).astype(BF16)
-    back_second = back_own + back_other.astype(F32)
-
-    grad_top = cotangent.astype(F32)
-    mid_part, grad_gain_two, grad_shift_two = second_back(back_second)
-    grad_middle = grad_top + mid_part
-    grad_attn = grad_middle.astype(BF16)
+    grad_middle, grad_attn, sums_second = middle_back(
+        middle, back_own, back_other, cotangent, norm_second
+    )
     grad_attn_other = swap(grad_attn)
     hidden = fc_weight.shape[1]
-    early = jnp.concatenate(
-        [
-            grad_gain_two,
-            grad_shift_two,
-            jnp.sum(grad_attn.astype(F32), axis=0),
-            jnp.sum(grad_top, axis=0),
-            sum_fc.reshape(-1),
-        ]
-    )
-
     norm_first = jnp.stack([first_gain, first_shift])
-    shared = (info, grad_attn, grad_attn_other, normed_first, full_qkv, full_out, norm_first)
+    shared = (info, grad_attn, grad_attn_other, normed_first, full_out, norm_first)
     kinds = ["split"] + ["whole"] * (pairs - 2) + ["joined"]
     results, column_sums, vector_parts = [], [], []
     first_sum = rest_sum = whole = None
@@ -771,67 +979,62 @@
         if pair:
             ties += [ff_sum.away, first_sum.away]
         result, sums, vector, token, gradient = attend_backward(
-            pair, kinds[pair], projected[pair], heads_flat, lses[pair], *shared, ties
+            pair,
+            kinds[pair],
+            projected[pair],
+            heads[pair],
+            lses[pair],
+            qkv_weights[pair],
+            *shared,
+            ties,
         )
         results.append(result)
         column_sums.append(sums)
         vector_parts.append(vector)
-        ff_sum.advance(token)
-        if pair:
-            first_sum.advance(token)
+        if pair < pairs - 1:
+            ff_sum.advance(token)
+            if pair:
+                first_sum.advance(token)
         if pair == 0:
             first_sum = gradient
         elif pair == pairs - 1:
             rest_sum = gradient
         else:
             whole = gradient
-    grad_projected = jnp.concatenate(results, axis=1)
-    grad_own, grad_other = split_rows(grad_projected)
-    back_other = dot(grad_other, full_qkv, 1, 1).astype(BF16)
-    back_own = dot(grad_own, full_qkv, 1, 1)
-    back_first = back_own + swap(back_other).astype(F32)
-    rest_sum.advance(ties=(back_other,))
-    vector_parts = sum(vector_parts[1:], vector_parts[0])
-    column_sums = jnp.concatenate(column_sums, axis=0).reshape(pairs, 3, PAIR)
-    vectors = sum_vectors(
-        jnp.concatenate(
-            [
-                vector_parts.reshape(-1),
-                early,
-                column_sums[:, 0].reshape(-1),
-                column_sums[:, 2].reshape(-1),
-            ]
-        ),
-        6 * width,
-    )
-    scaled = back_first * first_gain
-    normalised = centred * first_rsqrt
-    grad_hidden = grad_middle + first_rsqrt * (
-        scaled
-        - jnp.mean(scaled, axis=-1, keepdims=True)
-        - normalised * jnp.mean(scaled * normalised, axis=-1, keepdims=True)
-    )
+    back_own, back_other = back_product(info, results, qkv_weights, [])
+    ff_sum.advance(ties=(back_other,))
+    first_sum.advance(ties=(back_other,))
+    rest_sum.advance(ties=(ff_sum.away, first_sum.away))
+    grad_hidden = first_back(
+        hidden_in, back_own, swap(back_other), grad_middle, norm_first, [rest_sum.away]
+    )
+    vector_sum = VectorSum(
+        vectors_of(sums_second, sum_fc, vector_parts, column_sums, [rest_sum.away]), 6
+    )
+    first_sum.advance(ties=(rest_sum.away,))
+    rest_sum.advance(ties=(first_sum.away, vector_sum.advance()))
+    rest_sum.advance(ties=(vector_sum.advance(2), grad_hidden))
     own_heads = jnp.concatenate([first_sum.result(), rest_sum.result()], axis=1).reshape(
         shard_rows, pairs, 4, PAIR
     )
     own_outw = own_heads[:, :, 3].reshape(shard_rows, head_width)
     own_qkv = own_heads[:, :, :3].swapaxes(1, 2).reshape(shard_rows, 3, head_width)
     own_ff = ff_sum.result()
-    sums = vectors[: 6 * width].reshape(6, width)
-    hidden_sums = vectors[6 * width : 6 * width + hidden]
+    sums, own_sums = vector_sum.result()
+    hidden_rows = hidden // width
     return (
         block_out,
-        grad_hidden.astype(BF16),
+        grad_hidden,
         sums[0],
         sums[1],
         own_qkv,
-        vectors[6 * width + hidden :].reshape(2, head_width),
+        own_sums[hidden_rows].reshape(2, head_width),
         own_outw,
         sums[4],
         sums[2],
         sums[3],
         own_ff[:, :hidden],
-        hidden_sums,
+        own_sums[:hidden_rows].reshape(hidden),
         own_ff[:, hidden:],
         sums[5],
     )

time: 368 us -> 356 us (0.967)
  Pallas kernels: 173 us -> 208 us
  waiting for transfers between devices: 74.8 us -> 57.7 us
  other arithmetic: 27.5 us -> 13.3 us
  matrix products: 13.7 us -> 0 us
    pallas_call x0 -> x8, Pallas kernels: none -> 43.7 us  [block_call(): pl.pallas_call(kernel, grid=grid, in_specs=list(in_specs) + [ANY_SPEC] *...]
    ppermute x32 -> x28, waiting for transfers between devices: 69.3 us -> 52.5 us  [exchange(): return lax.ppermute(block, ('dp', 'tensor'), pairs)]
    dot_general x4 -> x0, matrix products: 13.7 us -> none  [dot(): lax.dot_general(left, right, (((left_axis,), (right_axis,)), ((), ())), p...]
    reduce_sum x5 -> x0, other arithmetic: 13.6 us -> none  [the longest x1 3.66 us: per_device(): jnp.sum(grad_top, axis=0)]
    pallas_call x9, Pallas kernels: 17.2 us -> 8.54 us  [join_halves(): pl.pallas_call(join_kernel, grid_spec=pltpu.PrefetchScalarGridSpec(num_sc...]
    convert_element_type x1, other arithmetic: 0.55 us -> 4.99 us  [per_device(): (middle + (terms_own + terms_other.astype(F32)) + proj_bias).astype(BF16)]
    concatenate x3 -> x0, local copies, waits for them, and re-layouts: 3.81 us -> none  [the longest x1 1.99 us: per_device(): heads_flat = jnp.concatenate(heads, axis=1)]
    ppermute x32 -> x28, starting transfers between devices: 40.5 us -> 43.5 us  [exchange(): return lax.ppermute(block, ('dp', 'tensor'), pairs)]
  transfers between devices with their start and end apart: 41 -> 37, of which waited for: 17 -> 15; matrix products, arithmetic and copies ran while one was open for 13% -> 6% of each run, Pallas kernels for 24% -> 40%
where the time goes in v1:
time: 356 us; the launch traced here: 352 us
  Pallas kernels  208 us (58%)
  waiting for transfers between devices  57.7 us (16%)
  starting transfers between devices  44.7 us (13%)
  local copies, waits for them, and re-layouts  26.5 us (7%)
  other arithmetic  13.3 us (4%)
    pallas_call x3, Pallas kernels, attend_backward(): pl.pallas_call(functools.partial(backward_kernel, rows=256, ties=len(ties...  70.2 us
    ppermute x28, waiting for transfers between devices, exchange(): return lax.ppermute(block, ('dp', 'tensor'), pairs)  52.5 us
    pallas_call x8, Pallas kernels, block_call(): pl.pallas_call(kernel, grid=grid, in_specs=list(in_specs) + [ANY_SPEC] *...  43.7 us
    ppermute x28, starting transfers between devices, exchange(): return lax.ppermute(block, ('dp', 'tensor'), pairs)  43.5 us
    pallas_call x1, Pallas kernels, feed_forward(): pl.pallas_call(functools.partial(feed_forward_kernel, blocks=blocks, plac...  43.1 us
    pallas_call x3, Pallas kernels, attend_forward(): pl.pallas_call(functools.partial(forward_kernel, rows=512, halves=halves)...  37.2 us
    unnamed x96, local copies, waits for them, and re-layouts  17.8 us
    pallas_call x9, Pallas kernels, join_halves(): pl.pallas_call(join_kernel, grid_spec=pltpu.PrefetchScalarGridSpec(num_sc...  8.54 us
  transfers between devices with their start and end apart: 37, of which 15 were waited for; matrix products, arithmetic and copies ran while one was open for 6% of the time, Pallas kernels for 40%

profile of v1, /device:TPU:0, one launch (start us, length us, event | category | flops | bytes accessed | tf_op | source)
XLA Modules:
  0.0 352.1 jit_solution(3423020255247767996)
XLA Ops:
  2.0 4.1 %collective-permute-start = (bf16[1,48,768]{2,1,0:T(8,128)(2,1)S(1)}, bf16[1,48,768]{2,1,0:T(8,128)(2,1)S(1)}, u32[]{:S(2)}, u32[]{:S(2)}) collective-permute-start(bf16[1,48,768]{2,1,0:T(8,128)(2,1)S(1)} %slice_bitcast_fusion), channel_id=1, source_target_pairs={{0,16},{1,9},{2,18},{3,11},{4,20},{5,13},{6,22},{7,15},{8,24},{9,1... | collective-permute-start | bytes 221192 | tf_op jit(solution)/shard_map/ppermute | solution.py:743
  6.1 1.7 convert_reduce_fusion
  8.5 1.8 fusion.5.refs_1_
  10.3 1.2 collective-permute-start.5
  11.5 1.9 collective-permute-start.7
  13.5 1.6 collective-permute-start.1
  15.1 8.5 %collective-permute-done.1 = bf16[2,48,768]{2,1,0:T(8,128)(2,1)S(1)} collective-permute-done((bf16[2,48,768]{2,1,0:T(8,128)(2,1)S(1)}, bf16[2,48,768]{2,1,0:T(8,128)(2,1)S(1)}, u32[]{:S(2)}, u32[]{:S(2)}) %collective-permute-start.1) | collective-permute-done | bytes 147488 | tf_op jit(solution)/shard_map/ppermute | solution.py:743
  23.6 1.6 collective-permute-start.2
  26.6 1.9 collective-permute-start.8
  28.4 2.0 collective-permute-done.2
  30.5 1.6 collective-permute-start.3
  32.1 4.1 %collective-permute-start.6 = (bf16[2,48,3072]{2,1,0:T(8,128)(2,1)S(1)}, bf16[2,48,3072]{2,1,0:T(8,128)(2,1)}, u32[]{:S(2)}, u32[]{:S(2)}) collective-permute-start(bf16[2,48,3072]{2,1,0:T(8,128)(2,1)S(1)} %pad_maximum_fusion.1.held_ref), channel_id=1, source_target_pairs={{0,8},{1,17},{2,10},{3,19},{4,12},{5,21},{6,14},{7,23},{8,0},{9,25... | collective-permute-start | bytes 1769480 | tf_op jit(solution)/shard_map/ppermute | solution.py:743
  37.8 1.6 collective-permute-start.9
  39.4 3.5 collective-permute-done.3.got_ref
  42.9 2.7 place_rows.2
  47.9 12.5 %attend_forward_0.1 = (bf16[2048,768]{1,0:T(8,128)(2,1)}, bf16[2048,384]{1,0:T(8,128)(2,1)}, bf16[2048,128]{1,0:T(8,128)(2,1)}, f32[2,2048]{1,0:T(2,128)}, f32[1,1]{1,0:T(1,128)}) custom-call(bf16[768,384]{1,0:T(8,128)(2,1)} %get-tuple-element.146.weight_ref.refs_3_, f32[1,384]{1,0:T(1,128)} %bitcast.58, s32[2]{0:T(128)} %copy-done.15, ...), custom_call_target="tpu_custom_call" | custom-call | flops 1 | bytes 1 | tf_op jit(solution)/shard_map/attend_forward_0/pallas_call | solution.py:382
  60.3 3.5 join_gathered.2.refs_1_.held_ref
  64.9 1.6 collective-permute-start.10
  67.5 12.3 %attend_forward_1.1 = (bf16[2048,384]{1,0:T(8,128)(2,1)}, bf16[2048,128]{1,0:T(8,128)(2,1)}, f32[2,2048]{1,0:T(2,128)}, f32[1,1]{1,0:T(1,128)}) custom-call(bf16[768,384]{1,0:T(8,128)(2,1)} %get-tuple-element.147.weight_ref.refs_4_, f32[1,384]{1,0:T(1,128)} %bitcast.60, bf16[2048,768]{1,0:T(8,128)(2,1)} %get-tuple-element.76.refs_0_.normed_ref, ...), custom_call_target="tpu_custom_call" | custom-call | flops 1 | bytes 1 | tf_op jit(solution)/shard_map/attend_forward_1/pallas_call | solution.py:382
  79.8 1.4 collective-permute-done.10.got_ref
  81.2 3.0 place_rows.3
  84.2 1.2 fusion.6
  86.5 3.9 %join_gathered.3.refs_1_.refs_0_ = bf16[8,48,3072]{2,1,0:T(8,128)(2,1)} custom-call(f32[1,1]{1,0:T(1,128)} %get-tuple-element.78.token_ref, bf16[4,48,3072]{2,1,0:T(8,128)(2,1)} %join_gathered.2.refs_1_.held_ref, bf16[4,48,3072]{2,1,0:T(8,128)(2,1)} %copy-done.30), custom_call_target="tpu_custom_call" | custom-call | flops 1 | bytes 1 | tf_op jit(solution)/shard_map/join_gathered/pallas_call | solution.py:527
  90.4 12.4 %attend_forward_2.1 = (bf16[2048,384]{1,0:T(8,128)(2,1)}, bf16[2048,128]{1,0:T(8,128)(2,1)}, f32[2,2048]{1,0:T(2,128)}, f32[1,1]{1,0:T(1,128)}) custom-call(bf16[768,384]{1,0:T(8,128)(2,1)} %get-tuple-element.144.weight_ref.refs_5_, f32[1,384]{1,0:T(1,128)} %bitcast.59, bf16[2048,768]{1,0:T(8,128)(2,1)} %get-tuple-element.76.refs_0_.normed_ref, ...), custom_call_target="tpu_custom_call" | custom-call | flops 1 | bytes 1 | tf_op jit(solution)/shard_map/attend_forward_2/pallas_call | solution.py:382
  102.9 5.1 %out_product.1 = (f32[1024,768]{1,0:T(8,128)}, bf16[1024,768]{1,0:T(8,128)(2,1)}) custom-call(s32[2]{0:T(128)} %copy-done.15, bf16[768,384]{1,0:T(8,128)(2,1)} %get-tuple-element.145.weight_ref.out_weight_ref, bf16[2048,128]{1,0:T(8,128)(2,1)} %get-tuple-element.79.refs_0_.heads_ref, bf16[2048,128]{1,0:T(8,128)(2,1)} %get-tuple-element.80.refs_1_.heads_ref, ...), custom_call_target="tpu_custom_call" | custom-call | flops 1 | bytes 1 | tf_op jit(solution)/shard_map/out_product/pallas_call | solution.py:527
  108.0 1.6 collective-permute-start.15
  111.6 1.2 copy-done.28
  112.8 5.6 %middle_norm.1 = (f32[1024,768]{1,0:T(8,128)}, bf16[1024,768]{1,0:T(8,128)(2,1)}) custom-call(bf16[1024,768]{1,0:T(8,128)(2,1)} %hidden_ref.3, f32[1024,768]{1,0:T(8,128)} %get-tuple-element.82.own_ref, bf16[1024,768]{1,0:T(8,128)(2,1)} %copy-done.28, f32[1,768]{1,0:T(1,128)} %broadcast_in_dim.24.bias_ref, f32[2,768]{1,0:T(2,128)} %pad_maximum_fusion.8.norm_ref), custom_call_target="tpu_custom_call" | custom-call | flops 1 | bytes 1 | tf_op jit(solution)/shard_map/middle_norm/pallas_call | solution.py:527
  119.1 17.8 %collective-permute-done.15.refs_1_ = bf16[8,48,3072]{2,1,0:T(8,128)(2,1)S(1)} collective-permute-done((bf16[8,48,3072]{2,1,0:T(8,128)(2,1)S(1)}, bf16[8,48,3072]{2,1,0:T(8,128)(2,1)S(1)}, u32[]{:S(2)}, u32[]{:S(2)}) %collective-permute-start.15) | collective-permute-done | bytes 2359328 | tf_op jit(solution)/shard_map/ppermute | solution.py:743
  136.9 1.5 copy-done.25
  138.4 1.2 copy-done.29
  139.6 43.1 %feed_forward.1 = (f32[1024,768]{1,0:T(8,128)}, bf16[1024,768]{1,0:T(8,128)(2,1)}, f32[1024,768]{1,0:T(8,128)}, bf16[1024,768]{1,0:T(8,128)(2,1)}, f32[1,1536]{1...) custom-call(s32[2]{0:T(128)} %copy-done.15, bf16[1024,768]{1,0:T(8,128)(2,1)} %get-tuple-element.85.own_ref, ...), custom_call_target="tpu_custom_call" | custom-call | flops 1 | bytes 1 | tf_op jit(solution)/shard_map/feed_forward/pallas_call | solution.py:502
  182.7 1.6 collective-permute-start.19
  184.3 2.1 collective-permute-done.17.other_ref
  186.3 1.2 copy-done.26
  187.5 8.0 %middle_back.1 = (f32[1024,768]{1,0:T(8,128)}, bf16[1024,768]{1,0:T(8,128)(2,1)}, f32[8,768]{1,0:T(8,128)}) custom-call(f32[1024,768]{1,0:T(8,128)} %get-tuple-element.84.middle_ref, f32[1024,768]{1,0:T(8,128)} %get-tuple-element.90.own_ref, bf16[1024,768]{1,0:T(8,128)(2,1)} %copy-done.26, bf16[1024,768]{1,0:T(8,128)(2,1)} %cot_ref.1, ...), custom_call_target="tpu_custom_call" | custom-call | flops 1 | bytes 1 | tf_op jit(solution)/shard_map/middle_back/pallas_call | solution.py:527
  196.4 2.9 collective-permute-done.18.other_ref
  199.2 1.2 copy-done.22
  200.4 23.4 %attend_backward_0.1 = (bf16[2048,384]{1,0:T(8,128)(2,1)}, f32[1,384]{1,0:T(1,128)}, f32[2,768]{1,0:T(2,128)}, f32[1,1]{1,0:T(1,128)}, f32[8,48,512]{2,1,0:T(8,128)}, /*index=5*/bf16[8,48,512]{2,1,0:T(8,128)(2,1)}) custom-call(s32[2]{0:T(128)} %copy-done.15, bf16[2048,384]{1,0:T(8,128)(2,1)} %get-tuple-element.88.qkv_ref, ...), custom_call_target="tpu_custom_call" | custom-call | flops 1 | bytes 1 | tf_op jit(solution)/shard_map/attend_backward_0/pallas_call | solution.py:428
  223.9 1.7 join_halves.9
  225.6 1.4 copy-done
  227.0 2.0 collective-permute-start.20
  229.0 1.5 collective-permute-start.21
  230.5 22.8 %attend_backward_1.1 = (bf16[2048,384]{1,0:T(8,128)(2,1)}, f32[1,384]{1,0:T(1,128)}, f32[2,768]{1,0:T(2,128)}, f32[1,1]{1,0:T(1,128)}, f32[16,48,512]{2,1,0:T(8,128)}) custom-call(s32[2]{0:T(128)} %copy-done.15, bf16[2048,384]{1,0:T(8,128)(2,1)} %get-tuple-element.94.qkv_ref, bf16[2048,128]{1,0:T(8,128)(2,1)} %get-tuple-element.80.refs_1_.heads_ref, ...), custom_call_target="tpu_custom_call" | custom-call | flops 1 | bytes 1 | tf_op jit(solution)/shard_map/attend_backward_1/pallas_call | solution.py:428
  253.4 1.5 join_halves.11
  255.1 1.5 join_halves.10
  257.4 23.9 %attend_backward_2.1 = (bf16[2048,384]{1,0:T(8,128)(2,1)}, f32[1,384]{1,0:T(1,128)}, f32[2,768]{1,0:T(2,128)}, f32[1,1]{1,0:T(1,128)}, f32[8,48,1024]{2,1,0:T(8,128)}, /*index=5*/bf16[8,48,1024]{2,1,0:T(8,128)(2,1)}) custom-call(s32[2]{0:T(128)} %copy-done.15, bf16[2048,384]{1,0:T(8,128)(2,1)} %get-tuple-element.102.qkv_ref, ...), custom_call_target="tpu_custom_call" | custom-call | flops 1 | bytes 1 | tf_op jit(solution)/shard_map/attend_backward_2/pallas_call | solution.py:428
  281.9 1.2 collective-permute-start.24
  283.8 9.8 %back_product.1 = (f32[1024,768]{1,0:T(8,128)}, bf16[1024,768]{1,0:T(8,128)(2,1)}) custom-call(s32[2]{0:T(128)} %copy-done.15, bf16[2048,384]{1,0:T(8,128)(2,1)} %get-tuple-element.93.refs_0_, bf16[2048,384]{1,0:T(8,128)(2,1)} %get-tuple-element.101.refs_1_, bf16[2048,384]{1,0:T(8,128)(2,1)} %get-tuple-element.110.refs_2_, ...), custom_call_target="tpu_custom_call" | custom-call | flops 1 | bytes 1 | tf_op jit(solution)/shard_map/back_product/pallas_call | solution.py:527
  293.6 1.4 copy-done.2
  295.7 1.6 collective-permute-start.31
  297.9 2.8 collective-permute-start.36
  302.3 1.4 vectors.1
  303.7 1.2 collective-permute-start.26
  307.3 5.0 %add_convert_fusion = bf16[1024,768]{1,0:T(8,128)(2,1)} fusion(f32[1024,768]{1,0:T(8,128)} %get-tuple-element.84.middle_ref, f32[1024,768]{1,0:T(8,128)} %get-tuple-element.86, bf16[1024,768]{1,0:T(8,128)(2,1)} %collective-permute-done.16, f32[768]{0:T(1024)S(1)} %copy-done.38), kind=kLoop, calls=%fused_computation.8 | loop fusion | flops 3932160 | bytes 9440256 | tf_op jit(solution)/shard_map/convert_element_type | solution.py:966
  312.3 1.6 collective-permute-start.33
  315.5 5.6 %collective-permute-done.27 = f32[16,768]{1,0:T(8,128)S(1)} collective-permute-done((f32[16,768]{1,0:T(8,128)S(1)}, f32[16,768]{1,0:T(8,128)S(1)}, u32[]{:S(2)}, u32[]{:S(2)}) %collective-permute-start.27) | collective-permute-done | bytes 49184 | tf_op jit(solution)/shard_map/ppermute | solution.py:743
  321.9 3.6 %collective-permute-done.28 = f32[16,768]{1,0:T(8,128)S(1)} collective-permute-done((f32[16,768]{1,0:T(8,128)S(1)}, f32[16,768]{1,0:T(8,128)S(1)}, u32[]{:S(2)}, u32[]{:S(2)}) %collective-permute-start.28) | collective-permute-done | bytes 49184 | tf_op jit(solution)/shard_map/ppermute | solution.py:743
  325.5 2.1 collective-permute-start.29
  328.4 2.6 collective-permute-done.29
  333.6 6.3 %first_back.1.refs_1_ = bf16[1024,768]{1,0:T(8,128)(2,1)} custom-call(bf16[1024,768]{1,0:T(8,128)(2,1)} %hidden_ref.3, f32[1024,768]{1,0:T(8,128)} %get-tuple-element.111.own_ref, bf16[1024,768]{1,0:T(8,128)(2,1)} %collective-permute-done.22.other_ref, f32[1024,768]{1,0:T(8,128)} %get-tuple-element.113.grad_ref, f32[2,768]{1,0:T(2,128)} %pad_maximum_fusion.9.norm_ref, ...), custom_call_target="tpu_custom_call" | custom-call | flops 1 | bytes 1 | tf_op jit(solution)/shard_map/first_back/pallas_call | solution.py:527
  340.4 1.4 copy-done.5
  342.4 1.6 collective-permute-start.35
  344.6 5.3 %collective-permute-done.35 = bf16[1,48,1024]{2,1,0:T(8,128)(2,1)S(1)} collective-permute-done((bf16[1,48,1024]{2,1,0:T(8,128)(2,1)S(1)}, bf16[1,48,1024]{2,1,0:T(8,128)(2,1)S(1)}, u32[]{:S(2)}, u32[]{:S(2)}) %collective-permute-start.35) | collective-permute-done | bytes 98336 | tf_op jit(solution)/shard_map/ppermute | solution.py:743
  (186 shorter events, 31.1 us)
Async XLA Ops:
  0.6 7.1 %copy-start.20 = (bf16[1024,768]{1,0:T(8,128)(2,1)S(1)}, bf16[1024,768]{1,0:T(8,128)(2,1)}, u32[]{:S(2)}) copy-start(bf16[1024,768]{1,0:T(8,128)(2,1)} %hidden_ref.3) | copy-start | bytes 4718596
  1.9 6.4 %copy-start.35 = (f32[768]{0:T(1024)S(1)}, f32[768]{0:T(1024)}, u32[]{:S(2)}) copy-start(f32[768]{0:T(1024)} %param.16) | copy-start | bytes 9220
  2.0 6.4 %copy-start.36 = (f32[768]{0:T(1024)S(1)}, f32[768]{0:T(1024)}, u32[]{:S(2)}) copy-start(f32[768]{0:T(1024)} %param.15) | copy-start | bytes 9220
  2.0 11.5 %collective-permute-start = (bf16[1,48,768]{2,1,0:T(8,128)(2,1)S(1)}, bf16[1,48,768]{2,1,0:T(8,128)(2,1)S(1)}, u32[]{:S(2)}, u32[]{:S(2)}) collective-permute-start(bf16[1,48,768]{2,1,0:T(8,128)(2,1)S(1)} %slice_bitcast_fusion), channel_id=1, source_target_pairs={{0,16},{1,9},{2,18},{3,11},{4,20},{5,13},{6,22},{7,15},{8,24},{9,1... | collective-permute-start | bytes 221192 | tf_op jit(solution)/shard_map/ppermute | solution.py:743
  8.4 3.0 copy-start.34
  8.4 6.7 %copy-start.42 = (f32[2,384]{1,0:T(2,128)S(1)}, f32[2,384]{1,0:T(2,128)}, u32[]{:S(2)}) copy-start(f32[2,384]{1,0:T(2,128)} %param.18) | copy-start | bytes 9220
  10.2 36.5 %collective-permute-start.4 = (bf16[1024,768]{1,0:T(8,128)(2,1)}, bf16[1024,768]{1,0:T(8,128)(2,1)S(1)}, u32[]{:S(2)}, u32[]{:S(2)}) collective-permute-start(bf16[1024,768]{1,0:T(8,128)(2,1)} %fusion.5.refs_1_), channel_id=1, source_target_pairs={{0,1},{1,0},{2,3},{3,2},{4,5},{5,4},{6,7},{7,6},{8,9},{9,8},{10,11... | collective-permute-start | bytes 4718600 | tf_op jit(solution)/shard_map/ppermute | solution.py:748
  10.3 21.8 %collective-permute-start.5 = (bf16[1,48,3072]{2,1,0:T(8,128)(2,1)S(1)}, bf16[1,48,3072]{2,1,0:T(8,128)(2,1)S(1)}, u32[]{:S(2)}, u32[]{:S(2)}) collective-permute-start(bf16[1,48,3072]{2,1,0:T(8,128)(2,1)S(1)} %maximum_bitcast_fusion), channel_id=1, source_target_pairs={{0,16},{1,9},{2,18},{3,11},{4,20},{5,13},{6,22},{7,15},{8,24},{9,1... | collective-permute-start | bytes 884744 | tf_op jit(solution)/shard_map/ppermute | solution.py:743
  11.5 14.4 %collective-permute-start.7 = (bf16[1,48,768]{2,1,0:T(8,128)(2,1)S(1)}, bf16[1,48,768]{2,1,0:T(8,128)(2,1)S(1)}, u32[]{:S(2)}, u32[]{:S(2)}) collective-permute-start(bf16[1,48,768]{2,1,0:T(8,128)(2,1)S(1)} %maximum_bitcast_fusion.1), channel_id=1, source_target_pairs={{0,16},{1,9},{2,18},{3,11},{4,20},{5,13},{6,22},{7,15},{8,24},{9,1... | collective-permute-start | bytes 221192 | tf_op jit(solution)/shard_map/ppermute | solution.py:743
  13.5 10.2 %collective-permute-start.1 = (bf16[2,48,768]{2,1,0:T(8,128)(2,1)S(1)}, bf16[2,48,768]{2,1,0:T(8,128)(2,1)S(1)}, u32[]{:S(2)}, u32[]{:S(2)}) collective-permute-start(bf16[2,48,768]{2,1,0:T(8,128)(2,1)S(1)} %pad_maximum_fusion.6), channel_id=1, source_target_pairs={{0,8},{1,17},{2,10},{3,19},{4,12},{5,21},{6,14},{7,23},{8,0},{9,25... | collective-permute-start | bytes 442376 | tf_op jit(solution)/shard_map/ppermute | solution.py:743
  23.6 6.8 %collective-permute-start.2 = (bf16[4,48,768]{2,1,0:T(8,128)(2,1)S(1)}, bf16[4,48,768]{2,1,0:T(8,128)(2,1)S(1)}, u32[]{:S(2)}, u32[]{:S(2)}) collective-permute-start(bf16[4,48,768]{2,1,0:T(8,128)(2,1)S(1)} %pad_maximum_fusion.3), channel_id=1, source_target_pairs={{0,4},{1,3},{2,6},{3,1},{4,0},{5,7},{6,2},{7,5},{8,12},{9,11},{10,... | collective-permute-start | bytes 884744 | tf_op jit(solution)/shard_map/ppermute | solution.py:743
  26.6 10.2 %collective-permute-start.8 = (bf16[2,48,768]{2,1,0:T(8,128)(2,1)}, bf16[2,48,768]{2,1,0:T(8,128)(2,1)}, u32[]{:S(2)}, u32[]{:S(2)}) collective-permute-start(bf16[2,48,768]{2,1,0:T(8,128)(2,1)} %pad_maximum_fusion.7), channel_id=1, source_target_pairs={{0,8},{1,17},{2,10},{3,19},{4,12},{5,21},{6,14},{7,23},{8,0},{9,25... | collective-permute-start | bytes 442376 | tf_op jit(solution)/shard_map/ppermute | solution.py:743
  30.5 12.4 %collective-permute-start.3 = (bf16[8,48,768]{2,1,0:T(8,128)(2,1)S(1)}, bf16[8,48,768]{2,1,0:T(8,128)(2,1)S(1)}, u32[]{:S(2)}, u32[]{:S(2)}) collective-permute-start(bf16[8,48,768]{2,1,0:T(8,128)(2,1)S(1)} %pad_maximum_fusion.held_ref), channel_id=1, source_target_pairs={{0,2},{1,5},{2,0},{3,7},{4,6},{5,1},{6,4},{7,3},{8,10},{9,13},{10,... | collective-permute-start | bytes 1769480 | tf_op jit(solution)/shard_map/ppermute | solution.py:743
  32.1 14.6 %copy-start.24 = (bf16[2,48,3072]{2,1,0:T(8,128)(2,1)}, bf16[2,48,3072]{2,1,0:T(8,128)(2,1)S(1)}, u32[]{:S(2)}) copy-start(bf16[2,48,3072]{2,1,0:T(8,128)(2,1)S(1)} %pad_maximum_fusion.1.held_ref) | copy-start | bytes 1769476
  32.1 28.2 %collective-permute-start.6 = (bf16[2,48,3072]{2,1,0:T(8,128)(2,1)S(1)}, bf16[2,48,3072]{2,1,0:T(8,128)(2,1)}, u32[]{:S(2)}, u32[]{:S(2)}) collective-permute-start(bf16[2,48,3072]{2,1,0:T(8,128)(2,1)S(1)} %pad_maximum_fusion.1.held_ref), channel_id=1, source_target_pairs={{0,8},{1,17},{2,10},{3,19},{4,12},{5,21},{6,14},{7,23},{8,0},{9,25... | collective-permute-start | bytes 1769480 | tf_op jit(solution)/shard_map/ppermute | solution.py:743
  36.8 9.9 %copy-start.15 = (s32[2]{0:T(128)}, s32[2]{0:T(128)S(1)}, u32[]{:S(2)}) copy-start(s32[2]{0:T(128)S(1)} %pad_add_fusion.info_ref.refs_0_) | copy-start | bytes 28
  37.8 26.1 %collective-permute-start.9 = (bf16[4,48,768]{2,1,0:T(8,128)(2,1)S(1)}, bf16[4,48,768]{2,1,0:T(8,128)(2,1)S(1)}, u32[]{:S(2)}, u32[]{:S(2)}) collective-permute-start(bf16[4,48,768]{2,1,0:T(8,128)(2,1)S(1)} %pad_maximum_fusion.4), channel_id=1, source_target_pairs={{0,4},{1,3},{2,6},{3,1},{4,0},{5,7},{6,2},{7,5},{8,12},{9,11},{10,... | collective-permute-start | bytes 884744 | tf_op jit(solution)/shard_map/ppermute | solution.py:743
  63.8 21.6 %collective-permute-start.11 = (bf16[4,48,3072]{2,1,0:T(8,128)(2,1)}, bf16[4,48,3072]{2,1,0:T(8,128)(2,1)S(1)}, u32[]{:S(2)}, u32[]{:S(2)}) collective-permute-start(bf16[4,48,3072]{2,1,0:T(8,128)(2,1)} %join_gathered.2.refs_1_.held_ref), channel_id=1, source_target_pairs={{0,4},{1,3},{2,6},{3,1},{4,0},{5,7},{6,2},{7,5},{8,12},{9,11},{10,... | collective-permute-start | bytes 3538952 | tf_op jit(solution)/shard_map/ppermute | solution.py:743
  64.9 16.3 %collective-permute-start.10 = (bf16[8,48,768]{2,1,0:T(8,128)(2,1)S(1)}, bf16[8,48,768]{2,1,0:T(8,128)(2,1)S(1)}, u32[]{:S(2)}, u32[]{:S(2)}) collective-permute-start(bf16[8,48,768]{2,1,0:T(8,128)(2,1)S(1)} %pad_maximum_fusion.2.held_ref), channel_id=1, source_target_pairs={{0,2},{1,5},{2,0},{3,7},{4,6},{5,1},{6,4},{7,3},{8,10},{9,13},{10,... | collective-permute-start | bytes 1769480 | tf_op jit(solution)/shard_map/ppermute | solution.py:743
  67.5 13.6 %copy-start.16 = (s32[2]{0:T(128)S(1)}, s32[2]{0:T(128)}, u32[]{:S(2)}) copy-start(s32[2]{0:T(128)} %copy-done.15) | copy-start | bytes 28
  90.4 17.6 %copy-start.21 = (bf16[8,48,3072]{2,1,0:T(8,128)(2,1)S(1)}, bf16[8,48,3072]{2,1,0:T(8,128)(2,1)}, u32[]{:S(2)}) copy-start(bf16[8,48,3072]{2,1,0:T(8,128)(2,1)} %join_gathered.3.refs_1_.refs_0_) | copy-start | bytes 7077892
  102.8 6.7 %copy-start.23 = (bf16[1024,768]{1,0:T(8,128)(2,1)S(1)}, bf16[1024,768]{1,0:T(8,128)(2,1)}, u32[]{:S(2)}) copy-start(bf16[1024,768]{1,0:T(8,128)(2,1)} %cot_ref.1) | copy-start | bytes 4718596
  102.8 7.4 %copy-start.39 = (f32[768]{0:T(1024)S(1)}, f32[768]{0:T(1024)}, u32[]{:S(2)}) copy-start(f32[768]{0:T(1024)} %param.20) | copy-start | bytes 9220
  102.8 8.0 %copy-start.40 = (f32[768]{0:T(1024)S(1)}, f32[768]{0:T(1024)}, u32[]{:S(2)}) copy-start(f32[768]{0:T(1024)} %param.22) | copy-start | bytes 9220
  102.9 8.0 %copy-start.41 = (f32[768]{0:T(1024)S(1)}, f32[768]{0:T(1024)}, u32[]{:S(2)}) copy-start(f32[768]{0:T(1024)} %param.21) | copy-start | bytes 9220
  108.0 3.6 %collective-permute-start.12 = (bf16[1024,768]{1,0:T(8,128)(2,1)}, bf16[1024,768]{1,0:T(8,128)(2,1)S(1)}, u32[]{:S(2)}, u32[]{:S(2)}) collective-permute-start(bf16[1024,768]{1,0:T(8,128)(2,1)} %get-tuple-element.83), channel_id=1, source_target_pairs={{0,1},{1,0},{2,3},{3,2},{4,5},{5,4},{6,7},{7,6},{8,9},{9,8},{10,11... | collective-permute-start | bytes 4718600 | tf_op jit(solution)/shard_map/ppermute | solution.py:748
  108.0 28.9 %collective-permute-start.15 = (bf16[8,48,3072]{2,1,0:T(8,128)(2,1)S(1)}, bf16[8,48,3072]{2,1,0:T(8,128)(2,1)S(1)}, u32[]{:S(2)}, u32[]{:S(2)}) collective-permute-start(bf16[8,48,3072]{2,1,0:T(8,128)(2,1)S(1)} %copy-done.21), channel_id=1, source_target_pairs={{0,2},{1,5},{2,0},{3,7},{4,6},{5,1},{6,4},{7,3},{8,10},{9,13},{10,... | collective-permute-start | bytes 7077896 | tf_op jit(solution)/shard_map/ppermute | solution.py:743
  109.6 9.6 %collective-permute-start.14 = (bf16[1024,768]{1,0:T(8,128)(2,1)S(1)}, bf16[1024,768]{1,0:T(8,128)(2,1)}, u32[]{:S(2)}, u32[]{:S(2)}) collective-permute-start(bf16[1024,768]{1,0:T(8,128)(2,1)S(1)} %copy-done.23), channel_id=1, source_target_pairs={{0,1},{1,0},{2,3},{3,2},{4,5},{5,4},{6,7},{7,6},{8,9},{9,8},{10,11... | collective-permute-start | bytes 4718600 | tf_op jit(solution)/shard_map/ppermute | solution.py:748
  112.8 5.7 %copy-start.37 = (f32[1536]{0:T(1024)S(1)}, f32[1536]{0:T(1024)}, u32[]{:S(2)}) copy-start(f32[1536]{0:T(1024)} %param.24) | copy-start | bytes 18436
  118.4 18.5 %collective-permute-start.13 = (bf16[1024,768]{1,0:T(8,128)(2,1)}, bf16[1024,768]{1,0:T(8,128)(2,1)S(1)}, u32[]{:S(2)}, u32[]{:S(2)}) collective-permute-start(bf16[1024,768]{1,0:T(8,128)(2,1)} %get-tuple-element.85.own_ref), channel_id=1, source_target_pairs={{0,1},{1,0},{2,3},{3,2},{4,5},{5,4},{6,7},{7,6},{8,9},{9,8},{10,11... | collective-permute-start | bytes 4718600 | tf_op jit(solution)/shard_map/ppermute | solution.py:748
  182.6 3.7 %collective-permute-start.17 = (bf16[1024,768]{1,0:T(8,128)(2,1)}, bf16[1024,768]{1,0:T(8,128)(2,1)S(1)}, u32[]{:S(2)}, u32[]{:S(2)}) collective-permute-start(bf16[1024,768]{1,0:T(8,128)(2,1)} %get-tuple-element.91), channel_id=1, source_target_pairs={{0,1},{1,0},{2,3},{3,2},{4,5},{5,4},{6,7},{7,6},{8,9},{9,8},{10,11... | collective-permute-start | bytes 4718600 | tf_op jit(solution)/shard_map/ppermute | solution.py:748
  182.7 41.2 %collective-permute-start.19 = (bf16[8,48,3072]{2,1,0:T(8,128)(2,1)}, bf16[8,48,3072]{2,1,0:T(8,128)(2,1)S(1)}, u32[]{:S(2)}, u32[]{:S(2)}) collective-permute-start(bf16[8,48,3072]{2,1,0:T(8,128)(2,1)} %get-tuple-element.98), channel_id=1, source_target_pairs={{0,2},{1,5},{2,0},{3,7},{4,6},{5,1},{6,4},{7,3},{8,10},{9,13},{10,... | collective-permute-start | bytes 7077896 | tf_op jit(solution)/shard_map/ppermute | solution.py:743
  195.6 3.7 %collective-permute-start.18 = (bf16[1024,768]{1,0:T(8,128)(2,1)}, bf16[1024,768]{1,0:T(8,128)(2,1)S(1)}, u32[]{:S(2)}, u32[]{:S(2)}) collective-permute-start(bf16[1024,768]{1,0:T(8,128)(2,1)} %get-tuple-element.92.own_ref), channel_id=1, source_target_pairs={{0,1},{1,0},{2,3},{3,2},{4,5},{5,4},{6,7},{7,6},{8,9},{9,8},{10,11... | collective-permute-start | bytes 4718600 | tf_op jit(solution)/shard_map/ppermute | solution.py:748
  200.4 23.5 %slice-start = ((s8[4718592]{0:T(1024)(128)(4,1)}), s8[4194304]{0:T(1024)(128)(4,1)S(1)}, s32[]{:S(2)}) async-start(s8[4718592]{0:T(1024)(128)(4,1)} %bitcast.49), calls=%async_computation | async-start | bytes 8388608
  200.4 23.5 %slice-start.1 = ((s8[4718592]{0:T(1024)(128)(4,1)}), s8[524288]{0:T(1024)(128)(4,1)S(1)}, s32[]{:S(2)}) async-start(s8[4718592]{0:T(1024)(128)(4,1)} %bitcast.49), calls=%async_computation.1 | async-start | bytes 1048576
  200.4 23.5 %copy-start.17 = (s32[2]{0:T(128)S(1)}, s32[2]{0:T(128)}, u32[]{:S(2)}) copy-start(s32[2]{0:T(128)} %copy-done.15) | copy-start | bytes 28
  227.0 3.5 %copy-start.10 = (bf16[4,48,3072]{2,1,0:T(8,128)(2,1)}, bf16[4,48,3072]{2,1,0:T(8,128)(2,1)S(1)}, u32[]{:S(2)}) copy-start(bf16[4,48,3072]{2,1,0:T(8,128)(2,1)S(1)} %get-tuple-element.99.refs_0_) | copy-start | bytes 3538948
  227.0 28.0 %collective-permute-start.20 = (bf16[4,48,3072]{2,1,0:T(8,128)(2,1)S(1)}, bf16[4,48,3072]{2,1,0:T(8,128)(2,1)S(1)}, u32[]{:S(2)}, u32[]{:S(2)}) collective-permute-start(bf16[4,48,3072]{2,1,0:T(8,128)(2,1)S(1)} %get-tuple-element.99.refs_0_), channel_id=1, source_target_pairs={{0,4},{1,3},{2,6},{3,1},{4,0},{5,7},{6,2},{7,5},{8,12},{9,11},{10,... | collective-permute-start | bytes 3538952 | tf_op jit(solution)/shard_map/ppermute | solution.py:743
  229.0 78.3 %collective-permute-start.16 = (bf16[1024,768]{1,0:T(8,128)(2,1)}, bf16[1024,768]{1,0:T(8,128)(2,1)}, u32[]{:S(2)}, u32[]{:S(2)}) collective-permute-start(bf16[1024,768]{1,0:T(8,128)(2,1)} %get-tuple-element.87), channel_id=1, source_target_pairs={{0,1},{1,0},{2,3},{3,2},{4,5},{5,4},{6,7},{7,6},{8,9},{9,8},{10,11... | collective-permute-start | bytes 4718600 | tf_op jit(solution)/shard_map/ppermute | solution.py:748
  229.0 24.4 %collective-permute-start.21 = (bf16[8,48,512]{2,1,0:T(8,128)(2,1)}, bf16[8,48,512]{2,1,0:T(8,128)(2,1)S(1)}, u32[]{:S(2)}, u32[]{:S(2)}) collective-permute-start(bf16[8,48,512]{2,1,0:T(8,128)(2,1)} %get-tuple-element.100.refs_1_), channel_id=1, source_target_pairs={{0,2},{1,5},{2,0},{3,7},{4,6},{5,1},{6,4},{7,3},{8,10},{9,13},{10,... | collective-permute-start | bytes 1179656 | tf_op jit(solution)/shard_map/ppermute | solution.py:743
  230.5 22.9 %copy-start.9 = (f32[8,48,512]{2,1,0:T(8,128)S(1)}, f32[8,48,512]{2,1,0:T(8,128)}, u32[]{:S(2)}) copy-start(f32[8,48,512]{2,1,0:T(8,128)} %get-tuple-element.108.keep_ref.send_ref) | copy-start | bytes 2359300
  230.5 22.9 %copy-start.18 = (s32[2]{0:T(128)S(1)}, s32[2]{0:T(128)}, u32[]{:S(2)}) copy-start(s32[2]{0:T(128)} %copy-done.15) | copy-start | bytes 28
  257.4 24.5 %copy-start.12 = (bf16[2,48,3072]{2,1,0:T(8,128)(2,1)S(1)}, bf16[2,48,3072]{2,1,0:T(8,128)(2,1)}, u32[]{:S(2)}) copy-start(bf16[2,48,3072]{2,1,0:T(8,128)(2,1)} %copy-done.11) | copy-start | bytes 1769476
  257.4 25.7 %copy-start.14 = (bf16[4,48,512]{2,1,0:T(8,128)(2,1)S(1)}, bf16[4,48,512]{2,1,0:T(8,128)(2,1)}, u32[]{:S(2)}) copy-start(bf16[4,48,512]{2,1,0:T(8,128)(2,1)} %copy-done.13) | copy-start | bytes 589828
  281.3 19.4 %collective-permute-start.23 = (bf16[8,48,1024]{2,1,0:T(8,128)(2,1)}, bf16[8,48,1024]{2,1,0:T(8,128)(2,1)S(1)}, u32[]{:S(2)}, u32[]{:S(2)}) collective-permute-start(bf16[8,48,1024]{2,1,0:T(8,128)(2,1)} %get-tuple-element.115), channel_id=1, source_target_pairs={{0,2},{1,5},{2,0},{3,7},{4,6},{5,1},{6,4},{7,3},{8,10},{9,13},{10,... | collective-permute-start | bytes 2359304 | tf_op jit(solution)/shard_map/ppermute | solution.py:743
  281.9 15.3 %collective-permute-start.24 = (bf16[2,48,3072]{2,1,0:T(8,128)(2,1)S(1)}, bf16[2,48,3072]{2,1,0:T(8,128)(2,1)S(1)}, u32[]{:S(2)}, u32[]{:S(2)}) collective-permute-start(bf16[2,48,3072]{2,1,0:T(8,128)(2,1)S(1)} %copy-done.12), channel_id=1, source_target_pairs={{0,8},{1,9},{2,10},{3,11},{4,12},{5,13},{6,14},{7,15},{8,0},{9,1},... | collective-permute-start | bytes 1769480 | tf_op jit(solution)/shard_map/ppermute | solution.py:743
  283.1 10.5 %collective-permute-start.25 = (bf16[4,48,512]{2,1,0:T(8,128)(2,1)S(1)}, bf16[4,48,512]{2,1,0:T(8,128)(2,1)S(1)}, u32[]{:S(2)}, u32[]{:S(2)}) collective-permute-start(bf16[4,48,512]{2,1,0:T(8,128)(2,1)S(1)} %copy-done.14), channel_id=1, source_target_pairs={{0,4},{1,3},{2,6},{3,1},{4,0},{5,7},{6,2},{7,5},{8,12},{9,11},{10,... | collective-permute-start | bytes 589832 | tf_op jit(solution)/shard_map/ppermute | solution.py:743
  283.8 9.8 %copy-start.19 = (s32[2]{0:T(128)S(1)}, s32[2]{0:T(128)}, u32[]{:S(2)}) copy-start(s32[2]{0:T(128)} %copy-done.15) | copy-start | bytes 28
  295.7 9.3 %collective-permute-start.31 = (bf16[2,48,512]{2,1,0:T(8,128)(2,1)S(1)}, bf16[2,48,512]{2,1,0:T(8,128)(2,1)S(1)}, u32[]{:S(2)}, u32[]{:S(2)}) collective-permute-start(bf16[2,48,512]{2,1,0:T(8,128)(2,1)S(1)} %get-tuple-element.119.refs_1_), channel_id=1, source_target_pairs={{0,8},{1,9},{2,10},{3,11},{4,12},{5,13},{6,14},{7,15},{8,0},{9,1},... | collective-permute-start | bytes 294920 | tf_op jit(solution)/shard_map/ppermute | solution.py:743
  297.2 3.5 copy-start.4
  297.9 23.9 %collective-permute-start.36 = (bf16[1,48,3072]{2,1,0:T(8,128)(2,1)S(1)}, bf16[1,48,3072]{2,1,0:T(8,128)(2,1)S(1)}, u32[]{:S(2)}, u32[]{:S(2)}) collective-permute-start(bf16[1,48,3072]{2,1,0:T(8,128)(2,1)S(1)} %get-tuple-element.117.refs_0_), channel_id=1, source_target_pairs={{0,16},{1,17},{2,18},{3,19},{4,20},{5,21},{6,22},{7,23},{8,24},{9,... | collective-permute-start | bytes 884744 | tf_op jit(solution)/shard_map/ppermute | solution.py:743
  300.7 6.5 %copy-start.38 = (f32[768]{0:T(1024)S(1)}, f32[768]{0:T(1024)}, u32[]{:S(2)}) copy-start(f32[768]{0:T(1024)} %param.26) | copy-start | bytes 9220
  303.7 10.2 %collective-permute-start.26 = (f32[16,768]{1,0:T(8,128)}, f32[16,768]{1,0:T(8,128)S(1)}, u32[]{:S(2)}, u32[]{:S(2)}) collective-permute-start(f32[16,768]{1,0:T(8,128)} %vectors.1), channel_id=1, source_target_pairs={{0,2},{1,3},{2,0},{3,1},{4,6},{5,7},{6,4},{7,5},{8,10},{9,11},{10,... | collective-permute-start | bytes 147464 | tf_op jit(solution)/shard_map/ppermute | solution.py:743
  306.5 9.0 %collective-permute-start.32 = (bf16[1,48,512]{2,1,0:T(8,128)(2,1)S(1)}, bf16[1,48,512]{2,1,0:T(8,128)(2,1)S(1)}, u32[]{:S(2)}, u32[]{:S(2)}) collective-permute-start(bf16[1,48,512]{2,1,0:T(8,128)(2,1)S(1)} %get-tuple-element.131.refs_0_), channel_id=1, source_target_pairs={{0,16},{1,17},{2,18},{3,19},{4,20},{5,21},{6,22},{7,23},{8,24},{9,... | collective-permute-start | bytes 147464 | tf_op jit(solution)/shard_map/ppermute | solution.py:743
  307.3 5.0 %copy-start.8 = (bf16[4,48,1024]{2,1,0:T(8,128)(2,1)S(1)}, bf16[4,48,1024]{2,1,0:T(8,128)(2,1)}, u32[]{:S(2)}) copy-start(bf16[4,48,1024]{2,1,0:T(8,128)(2,1)} %copy-done.6) | copy-start | bytes 1179652
  307.3 6.7 %copy-start.31 = (f32[16,768]{1,0:T(8,128)S(1)}, f32[16,768]{1,0:T(8,128)}, u32[]{:S(2)}) copy-start(f32[16,768]{1,0:T(8,128)} %vectors.1) | copy-start | bytes 147460
  312.3 21.4 %collective-permute-start.22 = (bf16[1024,768]{1,0:T(8,128)(2,1)S(1)}, bf16[1024,768]{1,0:T(8,128)(2,1)}, u32[]{:S(2)}, u32[]{:S(2)}) collective-permute-start(bf16[1024,768]{1,0:T(8,128)(2,1)S(1)} %copy-done.3), channel_id=1, source_target_pairs={{0,1},{1,0},{2,3},{3,2},{4,5},{5,4},{6,7},{7,6},{8,9},{9,8},{10,11... | collective-permute-start | bytes 4718600 | tf_op jit(solution)/shard_map/ppermute | solution.py:748
  312.3 20.1 %collective-permute-start.33 = (bf16[4,48,1024]{2,1,0:T(8,128)(2,1)S(1)}, bf16[4,48,1024]{2,1,0:T(8,128)(2,1)S(1)}, u32[]{:S(2)}, u32[]{:S(2)}) collective-permute-start(bf16[4,48,1024]{2,1,0:T(8,128)(2,1)S(1)} %copy-done.8), channel_id=1, source_target_pairs={{0,4},{1,3},{2,6},{3,1},{4,0},{5,7},{6,2},{7,5},{8,12},{9,11},{10,... | collective-permute-start | bytes 1179656 | tf_op jit(solution)/shard_map/ppermute | solution.py:743
  313.9 7.2 %collective-permute-start.27 = (f32[16,768]{1,0:T(8,128)S(1)}, f32[16,768]{1,0:T(8,128)S(1)}, u32[]{:S(2)}, u32[]{:S(2)}) collective-permute-start(f32[16,768]{1,0:T(8,128)S(1)} %add.65.refs_1_), channel_id=1, source_target_pairs={{0,4},{1,5},{2,6},{3,7},{4,0},{5,1},{6,2},{7,3},{8,12},{9,13},{10,... | collective-permute-start | bytes 147464 | tf_op jit(solution)/shard_map/ppermute | solution.py:743
  321.1 4.4 %collective-permute-start.28 = (f32[16,768]{1,0:T(8,128)S(1)}, f32[16,768]{1,0:T(8,128)S(1)}, u32[]{:S(2)}, u32[]{:S(2)}) collective-permute-start(f32[16,768]{1,0:T(8,128)S(1)} %add.66), channel_id=1, source_target_pairs={{0,8},{1,9},{2,10},{3,11},{4,12},{5,13},{6,14},{7,15},{8,0},{9,1},... | collective-permute-start | bytes 147464 | tf_op jit(solution)/shard_map/ppermute | solution.py:743
  325.5 5.6 %collective-permute-start.29 = (f32[16,768]{1,0:T(8,128)S(1)}, f32[16,768]{1,0:T(8,128)S(1)}, u32[]{:S(2)}, u32[]{:S(2)}) collective-permute-start(f32[16,768]{1,0:T(8,128)S(1)} %add.67.refs_0_), channel_id=1, source_target_pairs={{0,16},{1,17},{2,18},{3,19},{4,20},{5,21},{6,22},{7,23},{8,24},{9,... | collective-permute-start | bytes 147464 | tf_op jit(solution)/shard_map/ppermute | solution.py:743
  331.1 2.5 collective-permute-start.30
  333.1 7.4 %collective-permute-start.34 = (bf16[2,48,1024]{2,1,0:T(8,128)(2,1)S(1)}, bf16[2,48,1024]{2,1,0:T(8,128)(2,1)S(1)}, u32[]{:S(2)}, u32[]{:S(2)}) collective-permute-start(bf16[2,48,1024]{2,1,0:T(8,128)(2,1)S(1)} %get-tuple-element.134), channel_id=1, source_target_pairs={{0,8},{1,9},{2,10},{3,11},{4,12},{5,13},{6,14},{7,15},{8,0},{9,1},... | collective-permute-start | bytes 589832 | tf_op jit(solution)/shard_map/ppermute | solution.py:743
  342.4 7.5 %collective-permute-start.35 = (bf16[1,48,1024]{2,1,0:T(8,128)(2,1)S(1)}, bf16[1,48,1024]{2,1,0:T(8,128)(2,1)S(1)}, u32[]{:S(2)}, u32[]{:S(2)}) collective-permute-start(bf16[1,48,1024]{2,1,0:T(8,128)(2,1)S(1)} %get-tuple-element.136), channel_id=1, source_target_pairs={{0,16},{1,17},{2,18},{3,19},{4,20},{5,21},{6,22},{7,23},{8,24},{9,... | collective-permute-start | bytes 294920 | tf_op jit(solution)/shard_map/ppermute | solution.py:743
  (18 other events, 24.4 us)

commit v2 on v1

--- a/solution.py
+++ b/solution.py
@@ -926,6 +926,8 @@
     bias_parts = jnp.stack([qv_bias[0], jnp.zeros_like(qv_bias[0]), qv_bias[1]])
     bias_cols = bias_parts.reshape(3, pairs, PAIR).swapaxes(0, 1).reshape(pairs, 1, columns)
     ff_gather.advance()
+    for _ in range(len(rest_gather.orders) - 1):
+        rest_gather.advance()
     weights = first_gather.result()
     qkv_weights = [weights[:, p * columns : (p + 1) * columns] for p in range(early)]
     projected, heads, lses = [], [], []
@@ -935,7 +937,7 @@
             normed_first,
             qkv_weights[pair],
             bias_cols[pair],
-            [ff_gather.held] if pair else [],
+            [ff_gather.held] if pair else [rest_gather.held],
         )
         projected.append(columns_out)
         heads.append(heads_out)
@@ -955,7 +957,7 @@
         swap(attn_other),
         out_bias[None],
         norm_second,
-        [],
+        [ff_gather.got],
     )
     normed_other = swap(normed_own)
     terms_own, terms_other, back_own, back_other, sum_fc, ff_sum = feed_forward(

time: 356 us -> 346 us (0.972)
  waiting for transfers between devices: 57.7 us -> 49.5 us
    ppermute x28, waiting for transfers between devices: 52.5 us -> 37.7 us  [exchange(): return lax.ppermute(block, ('dp', 'tensor'), pairs)]
    ppermute x9, waiting for transfers between devices: 5.11 us -> 11.8 us  [swap(): lax.ppermute(block, 'tensor', [(i, count - 1 - i) for i in range(count)])]
    unnamed x96 -> x100, local copies, waits for them, and re-layouts: 17.8 us -> 16.6 us
  transfers between devices with their start and end apart: 37 -> 37, of which waited for: 15 -> 17; matrix products, arithmetic and copies ran while one was open for 6% -> 6% of each run, Pallas kernels for 40% -> 47%
where the time goes in v2:
time: 346 us; the launch traced here: 342 us
  Pallas kernels  208 us (60%)
  waiting for transfers between devices  49.5 us (14%)
  starting transfers between devices  44.3 us (13%)
  local copies, waits for them, and re-layouts  25.3 us (7%)
  other arithmetic  13.5 us (4%)
    pallas_call x3, Pallas kernels, attend_backward(): pl.pallas_call(functools.partial(backward_kernel, rows=256, ties=len(ties...  70.2 us
    pallas_call x8, Pallas kernels, block_call(): pl.pallas_call(kernel, grid=grid, in_specs=list(in_specs) + [ANY_SPEC] *...  43.6 us
    ppermute x28, starting transfers between devices, exchange(): return lax.ppermute(block, ('dp', 'tensor'), pairs)  43.3 us
    pallas_call x1, Pallas kernels, feed_forward(): pl.pallas_call(functools.partial(feed_forward_kernel, blocks=blocks, plac...  43.1 us
    ppermute x28, waiting for transfers between devices, exchange(): return lax.ppermute(block, ('dp', 'tensor'), pairs)  37.7 us
    pallas_call x3, Pallas kernels, attend_forward(): pl.pallas_call(functools.partial(forward_kernel, rows=512, halves=halves)...  37.1 us
    unnamed x100, local copies, waits for them, and re-layouts  16.6 us
    ppermute x9, waiting for transfers between devices, swap(): lax.ppermute(block, 'tensor', [(i, count - 1 - i) for i in range(count)])  11.8 us
  transfers between devices with their start and end apart: 37, of which 17 were waited for; matrix products, arithmetic and copies ran while one was open for 6% of the time, Pallas kernels for 47%

profile of v2, /device:TPU:0, one launch (start us, length us, event | category | flops | bytes accessed | tf_op | source)
XLA Modules:
  0.0 342.5 jit_solution(721291804184511342)
XLA Ops:
  2.0 4.1 %collective-permute-start = (bf16[1,48,768]{2,1,0:T(8,128)(2,1)S(1)}, bf16[1,48,768]{2,1,0:T(8,128)(2,1)S(1)}, u32[]{:S(2)}, u32[]{:S(2)}) collective-permute-start(bf16[1,48,768]{2,1,0:T(8,128)(2,1)S(1)} %slice_bitcast_fusion), channel_id=1, source_target_pairs={{0,16},{1,9},{2,18},{3,11},{4,20},{5,13},{6,22},{7,15},{8,24},{9,1... | collective-permute-start | bytes 221192 | tf_op jit(solution)/shard_map/ppermute | solution.py:743
  6.1 1.7 convert_reduce_fusion
  8.5 1.8 fusion.5.refs_1_
  10.3 1.2 collective-permute-start.5
  11.5 1.9 collective-permute-start.8
  13.4 1.6 collective-permute-start.1
  15.7 2.4 collective-permute-start.6
  18.1 5.9 %collective-permute-done.1 = bf16[2,48,768]{2,1,0:T(8,128)(2,1)S(1)} collective-permute-done((bf16[2,48,768]{2,1,0:T(8,128)(2,1)S(1)}, bf16[2,48,768]{2,1,0:T(8,128)(2,1)S(1)}, u32[]{:S(2)}, u32[]{:S(2)}) %collective-permute-start.1) | collective-permute-done | bytes 147488 | tf_op jit(solution)/shard_map/ppermute | solution.py:743
  24.0 1.6 collective-permute-start.2
  27.5 1.5 collective-permute-start.7
  29.0 1.8 collective-permute-done.2
  30.9 1.6 collective-permute-start.3
  32.5 3.7 %collective-permute-start.9 = (bf16[2,48,3072]{2,1,0:T(8,128)(2,1)S(1)}, bf16[2,48,3072]{2,1,0:T(8,128)(2,1)}, u32[]{:S(2)}, u32[]{:S(2)}) collective-permute-start(bf16[2,48,3072]{2,1,0:T(8,128)(2,1)S(1)} %pad_maximum_fusion.2.held_ref), channel_id=1, source_target_pairs={{0,8},{1,17},{2,10},{3,19},{4,12},{5,21},{6,14},{7,23},{8,0},{9,25... | collective-permute-start | bytes 1769480 | tf_op jit(solution)/shard_map/ppermute | solution.py:743
  36.9 1.9 pad_maximum_fusion.1.refs_3_.held_ref
  38.8 3.7 %collective-permute-done.3.got_ref = bf16[8,48,768]{2,1,0:T(8,128)(2,1)S(1)} collective-permute-done((bf16[8,48,768]{2,1,0:T(8,128)(2,1)S(1)}, bf16[8,48,768]{2,1,0:T(8,128)(2,1)S(1)}, u32[]{:S(2)}, u32[]{:S(2)}) %collective-permute-start.3) | collective-permute-done | bytes 589856 | tf_op jit(solution)/shard_map/ppermute | solution.py:743
  42.5 2.7 place_rows.2
  47.5 12.5 %attend_forward_0.1 = (bf16[2048,768]{1,0:T(8,128)(2,1)}, bf16[2048,384]{1,0:T(8,128)(2,1)}, bf16[2048,128]{1,0:T(8,128)(2,1)}, f32[2,2048]{1,0:T(2,128)}, f32[1,1]{1,0:T(1,128)}) custom-call(bf16[768,384]{1,0:T(8,128)(2,1)} %get-tuple-element.146.weight_ref.refs_3_, f32[1,384]{1,0:T(1,128)} %bitcast.58, s32[2]{0:T(128)} %copy-done.16, ...), custom_call_target="tpu_custom_call" | custom-call | flops 1 | bytes 1 | tf_op jit(solution)/shard_map/attend_forward_0/pallas_call | solution.py:382
  60.0 3.5 %join_gathered.2.refs_1_.held_ref = bf16[4,48,3072]{2,1,0:T(8,128)(2,1)} custom-call(f32[1,1]{1,0:T(1,128)} %get-tuple-element.77.token_ref, bf16[2,48,3072]{2,1,0:T(8,128)(2,1)} %copy-done.25, bf16[2,48,3072]{2,1,0:T(8,128)(2,1)} %collective-permute-done.9.got_ref), custom_call_target="tpu_custom_call" | custom-call | flops 1 | bytes 1 | tf_op jit(solution)/shard_map/join_gathered/pallas_call | solution.py:527
  63.5 1.6 collective-permute-start.11
  65.1 1.5 collective-permute-start.10
  67.1 12.3 %attend_forward_1.1 = (bf16[2048,384]{1,0:T(8,128)(2,1)}, bf16[2048,128]{1,0:T(8,128)(2,1)}, f32[2,2048]{1,0:T(2,128)}, f32[1,1]{1,0:T(1,128)}) custom-call(bf16[768,384]{1,0:T(8,128)(2,1)} %get-tuple-element.147.weight_ref.refs_4_, f32[1,384]{1,0:T(1,128)} %bitcast.60, bf16[2048,768]{1,0:T(8,128)(2,1)} %get-tuple-element.76.refs_0_.normed_ref, ...), custom_call_target="tpu_custom_call" | custom-call | flops 1 | bytes 1 | tf_op jit(solution)/shard_map/attend_forward_1/pallas_call | solution.py:382
  79.4 6.0 %collective-permute-done.11.got_ref = bf16[4,48,3072]{2,1,0:T(8,128)(2,1)S(1)} collective-permute-done((bf16[4,48,3072]{2,1,0:T(8,128)(2,1)}, bf16[4,48,3072]{2,1,0:T(8,128)(2,1)S(1)}, u32[]{:S(2)}, u32[]{:S(2)}) %collective-permute-start.11) | collective-permute-done | bytes 1179680 | tf_op jit(solution)/shard_map/ppermute | solution.py:743
  86.6 3.8 %join_gathered.3.refs_1_.refs_0_ = bf16[8,48,3072]{2,1,0:T(8,128)(2,1)} custom-call(f32[1,1]{1,0:T(1,128)} %get-tuple-element.78.token_ref, bf16[4,48,3072]{2,1,0:T(8,128)(2,1)} %join_gathered.2.refs_1_.held_ref, bf16[4,48,3072]{2,1,0:T(8,128)(2,1)} %copy-done.31), custom_call_target="tpu_custom_call" | custom-call | flops 1 | bytes 1 | tf_op jit(solution)/shard_map/join_gathered/pallas_call | solution.py:527
  91.4 3.2 place_rows.3
  94.6 1.2 fusion.6
  95.8 12.3 %attend_forward_2.1 = (bf16[2048,384]{1,0:T(8,128)(2,1)}, bf16[2048,128]{1,0:T(8,128)(2,1)}, f32[2,2048]{1,0:T(2,128)}, f32[1,1]{1,0:T(1,128)}) custom-call(bf16[768,384]{1,0:T(8,128)(2,1)} %get-tuple-element.144.weight_ref.refs_5_, f32[1,384]{1,0:T(1,128)} %bitcast.59, bf16[2048,768]{1,0:T(8,128)(2,1)} %get-tuple-element.76.refs_0_.normed_ref, ...), custom_call_target="tpu_custom_call" | custom-call | flops 1 | bytes 1 | tf_op jit(solution)/shard_map/attend_forward_2/pallas_call | solution.py:382
  108.1 5.1 %out_product.1 = (f32[1024,768]{1,0:T(8,128)}, bf16[1024,768]{1,0:T(8,128)(2,1)}) custom-call(s32[2]{0:T(128)} %copy-done.16, bf16[768,384]{1,0:T(8,128)(2,1)} %get-tuple-element.145.weight_ref.out_weight_ref, bf16[2048,128]{1,0:T(8,128)(2,1)} %get-tuple-element.79.refs_0_.heads_ref, bf16[2048,128]{1,0:T(8,128)(2,1)} %get-tuple-element.80.refs_1_.heads_ref, ...), custom_call_target="tpu_custom_call" | custom-call | flops 1 | bytes 1 | tf_op jit(solution)/shard_map/out_product/pallas_call | solution.py:527
  115.0 3.4 collective-permute-done.12.other_ref
  119.6 1.3 copy-done.23
  120.8 5.6 %middle_norm.1 = (f32[1024,768]{1,0:T(8,128)}, bf16[1024,768]{1,0:T(8,128)(2,1)}) custom-call(bf16[1024,768]{1,0:T(8,128)(2,1)} %hidden_ref.3, f32[1024,768]{1,0:T(8,128)} %get-tuple-element.82.own_ref, bf16[1024,768]{1,0:T(8,128)(2,1)} %copy-done.29, f32[1,768]{1,0:T(1,128)} %broadcast_in_dim.24.bias_ref, f32[2,768]{1,0:T(2,128)} %pad_maximum_fusion.8.norm_ref, ...), custom_call_target="tpu_custom_call" | custom-call | flops 1 | bytes 1 | tf_op jit(solution)/shard_map/middle_norm/pallas_call | solution.py:527
  127.0 3.0 collective-permute-done.14.other_ref
  130.0 1.2 copy-done.30
  131.2 43.1 %feed_forward.1 = (f32[1024,768]{1,0:T(8,128)}, bf16[1024,768]{1,0:T(8,128)(2,1)}, f32[1024,768]{1,0:T(8,128)}, bf16[1024,768]{1,0:T(8,128)(2,1)}, f32[1,1536]{1...) custom-call(s32[2]{0:T(128)} %copy-done.16, bf16[1024,768]{1,0:T(8,128)(2,1)} %get-tuple-element.85.own_ref, ...), custom_call_target="tpu_custom_call" | custom-call | flops 1 | bytes 1 | tf_op jit(solution)/shard_map/feed_forward/pallas_call | solution.py:502
  175.5 2.5 collective-permute-done.17.other_ref
  178.0 1.2 copy-done.26
  179.1 8.1 %middle_back.1 = (f32[1024,768]{1,0:T(8,128)}, bf16[1024,768]{1,0:T(8,128)(2,1)}, f32[8,768]{1,0:T(8,128)}) custom-call(f32[1024,768]{1,0:T(8,128)} %get-tuple-element.84.middle_ref, f32[1024,768]{1,0:T(8,128)} %get-tuple-element.90.own_ref, bf16[1024,768]{1,0:T(8,128)(2,1)} %copy-done.26, bf16[1024,768]{1,0:T(8,128)(2,1)} %cot_ref.1, ...), custom_call_target="tpu_custom_call" | custom-call | flops 1 | bytes 1 | tf_op jit(solution)/shard_map/middle_back/pallas_call | solution.py:527
  188.0 2.9 collective-permute-done.18.other_ref
  190.9 1.2 copy-done.22
  192.1 23.5 %attend_backward_0.1 = (bf16[2048,384]{1,0:T(8,128)(2,1)}, f32[1,384]{1,0:T(1,128)}, f32[2,768]{1,0:T(2,128)}, f32[1,1]{1,0:T(1,128)}, f32[8,48,512]{2,1,0:T(8,128)}, /*index=5*/bf16[8,48,512]{2,1,0:T(8,128)(2,1)}) custom-call(s32[2]{0:T(128)} %copy-done.16, bf16[2048,384]{1,0:T(8,128)(2,1)} %get-tuple-element.88.qkv_ref, ...), custom_call_target="tpu_custom_call" | custom-call | flops 1 | bytes 1 | tf_op jit(solution)/shard_map/attend_backward_0/pallas_call | solution.py:428
  215.6 1.7 join_halves.9
  217.3 1.4 copy-done
  218.7 1.5 collective-permute-start.20
  221.2 22.8 %attend_backward_1.1 = (bf16[2048,384]{1,0:T(8,128)(2,1)}, f32[1,384]{1,0:T(1,128)}, f32[2,768]{1,0:T(2,128)}, f32[1,1]{1,0:T(1,128)}, f32[16,48,512]{2,1,0:T(8,128)}) custom-call(s32[2]{0:T(128)} %copy-done.16, bf16[2048,384]{1,0:T(8,128)(2,1)} %get-tuple-element.94.qkv_ref, bf16[2048,128]{1,0:T(8,128)(2,1)} %get-tuple-element.80.refs_1_.heads_ref, ...), custom_call_target="tpu_custom_call" | custom-call | flops 1 | bytes 1 | tf_op jit(solution)/shard_map/attend_backward_1/pallas_call | solution.py:428
  244.0 1.5 join_halves.11
  245.7 1.5 join_halves.10
  248.0 23.9 %attend_backward_2.1 = (bf16[2048,384]{1,0:T(8,128)(2,1)}, f32[1,384]{1,0:T(1,128)}, f32[2,768]{1,0:T(2,128)}, f32[1,1]{1,0:T(1,128)}, f32[8,48,1024]{2,1,0:T(8,128)}, /*index=5*/bf16[8,48,1024]{2,1,0:T(8,128)(2,1)}) custom-call(s32[2]{0:T(128)} %copy-done.16, bf16[2048,384]{1,0:T(8,128)(2,1)} %get-tuple-element.102.qkv_ref, ...), custom_call_target="tpu_custom_call" | custom-call | flops 1 | bytes 1 | tf_op jit(solution)/shard_map/attend_backward_2/pallas_call | solution.py:428
  273.1 1.3 collective-permute-start.24
  275.3 9.8 %back_product.1 = (f32[1024,768]{1,0:T(8,128)}, bf16[1024,768]{1,0:T(8,128)(2,1)}) custom-call(s32[2]{0:T(128)} %copy-done.16, bf16[2048,384]{1,0:T(8,128)(2,1)} %get-tuple-element.93.refs_0_, bf16[2048,384]{1,0:T(8,128)(2,1)} %get-tuple-element.101.refs_1_, bf16[2048,384]{1,0:T(8,128)(2,1)} %get-tuple-element.110.refs_2_, ...), custom_call_target="tpu_custom_call" | custom-call | flops 1 | bytes 1 | tf_op jit(solution)/shard_map/back_product/pallas_call | solution.py:527
  285.1 1.4 copy-done.2
  288.9 2.0 collective-permute-start.36
  292.5 1.4 vectors.1
  297.5 5.0 %add_convert_fusion = bf16[1024,768]{1,0:T(8,128)(2,1)} fusion(f32[1024,768]{1,0:T(8,128)} %get-tuple-element.84.middle_ref, f32[1024,768]{1,0:T(8,128)} %get-tuple-element.86, bf16[1024,768]{1,0:T(8,128)(2,1)} %collective-permute-done.16, f32[768]{0:T(1024)S(1)} %copy-done.40), kind=kLoop, calls=%fused_computation.8 | loop fusion | flops 3932160 | bytes 9440256 | tf_op jit(solution)/shard_map/convert_element_type | solution.py:968
  303.4 1.2 collective-permute-start.27
  304.6 1.8 collective-permute-done.32
  306.5 4.9 %collective-permute-done.27 = f32[16,768]{1,0:T(8,128)S(1)} collective-permute-done((f32[16,768]{1,0:T(8,128)S(1)}, f32[16,768]{1,0:T(8,128)S(1)}, u32[]{:S(2)}, u32[]{:S(2)}) %collective-permute-start.27) | collective-permute-done | bytes 49184 | tf_op jit(solution)/shard_map/ppermute | solution.py:743
  311.3 1.5 collective-permute-start.28
  312.9 2.6 collective-permute-done.28
  315.5 2.0 collective-permute-start.29
  318.4 2.2 collective-permute-done.29
  322.5 1.5 collective-permute-start.34
  324.1 6.3 %first_back.1.refs_1_ = bf16[1024,768]{1,0:T(8,128)(2,1)} custom-call(bf16[1024,768]{1,0:T(8,128)(2,1)} %hidden_ref.3, f32[1024,768]{1,0:T(8,128)} %get-tuple-element.111.own_ref, bf16[1024,768]{1,0:T(8,128)(2,1)} %collective-permute-done.22.other_ref, f32[1024,768]{1,0:T(8,128)} %get-tuple-element.113.grad_ref, f32[2,768]{1,0:T(2,128)} %pad_maximum_fusion.9.norm_ref, ...), custom_call_target="tpu_custom_call" | custom-call | flops 1 | bytes 1 | tf_op jit(solution)/shard_map/first_back/pallas_call | solution.py:527
  330.4 1.4 copy-done.5
  332.4 1.5 collective-permute-start.35
  334.6 5.8 %collective-permute-done.35 = bf16[1,48,1024]{2,1,0:T(8,128)(2,1)S(1)} collective-permute-done((bf16[1,48,1024]{2,1,0:T(8,128)(2,1)S(1)}, bf16[1,48,1024]{2,1,0:T(8,128)(2,1)S(1)}, u32[]{:S(2)}, u32[]{:S(2)}) %collective-permute-start.35) | collective-permute-done | bytes 98336 | tf_op jit(solution)/shard_map/ppermute | solution.py:743
  (190 shorter events, 34.3 us)
Async XLA Ops:
  0.6 7.1 %copy-start.21 = (bf16[1024,768]{1,0:T(8,128)(2,1)S(1)}, bf16[1024,768]{1,0:T(8,128)(2,1)}, u32[]{:S(2)}) copy-start(bf16[1024,768]{1,0:T(8,128)(2,1)} %hidden_ref.3) | copy-start | bytes 4718596
  1.9 6.4 %copy-start.37 = (f32[768]{0:T(1024)S(1)}, f32[768]{0:T(1024)}, u32[]{:S(2)}) copy-start(f32[768]{0:T(1024)} %param.16) | copy-start | bytes 9220
  2.0 6.4 %copy-start.38 = (f32[768]{0:T(1024)S(1)}, f32[768]{0:T(1024)}, u32[]{:S(2)}) copy-start(f32[768]{0:T(1024)} %param.15) | copy-start | bytes 9220
  2.0 11.4 %collective-permute-start = (bf16[1,48,768]{2,1,0:T(8,128)(2,1)S(1)}, bf16[1,48,768]{2,1,0:T(8,128)(2,1)S(1)}, u32[]{:S(2)}, u32[]{:S(2)}) collective-permute-start(bf16[1,48,768]{2,1,0:T(8,128)(2,1)S(1)} %slice_bitcast_fusion), channel_id=1, source_target_pairs={{0,16},{1,9},{2,18},{3,11},{4,20},{5,13},{6,22},{7,15},{8,24},{9,1... | collective-permute-start | bytes 221192 | tf_op jit(solution)/shard_map/ppermute | solution.py:743
  8.4 3.0 copy-start.34
  8.4 3.0 copy-start.35
  8.4 6.6 %copy-start.44 = (f32[2,384]{1,0:T(2,128)S(1)}, f32[2,384]{1,0:T(2,128)}, u32[]{:S(2)}) copy-start(f32[2,384]{1,0:T(2,128)} %param.18) | copy-start | bytes 9220
  10.2 36.1 %collective-permute-start.4 = (bf16[1024,768]{1,0:T(8,128)(2,1)}, bf16[1024,768]{1,0:T(8,128)(2,1)S(1)}, u32[]{:S(2)}, u32[]{:S(2)}) collective-permute-start(bf16[1024,768]{1,0:T(8,128)(2,1)} %fusion.5.refs_1_), channel_id=1, source_target_pairs={{0,1},{1,0},{2,3},{3,2},{4,5},{5,4},{6,7},{7,6},{8,9},{9,8},{10,11... | collective-permute-start | bytes 4718600 | tf_op jit(solution)/shard_map/ppermute | solution.py:748
  10.3 5.4 %collective-permute-start.5 = (bf16[1,48,768]{2,1,0:T(8,128)(2,1)S(1)}, bf16[1,48,768]{2,1,0:T(8,128)(2,1)S(1)}, u32[]{:S(2)}, u32[]{:S(2)}) collective-permute-start(bf16[1,48,768]{2,1,0:T(8,128)(2,1)S(1)} %maximum_bitcast_fusion.1), channel_id=1, source_target_pairs={{0,16},{1,9},{2,18},{3,11},{4,20},{5,13},{6,22},{7,15},{8,24},{9,1... | collective-permute-start | bytes 221192 | tf_op jit(solution)/shard_map/ppermute | solution.py:743
  11.5 21.0 %collective-permute-start.8 = (bf16[1,48,3072]{2,1,0:T(8,128)(2,1)S(1)}, bf16[1,48,3072]{2,1,0:T(8,128)(2,1)S(1)}, u32[]{:S(2)}, u32[]{:S(2)}) collective-permute-start(bf16[1,48,3072]{2,1,0:T(8,128)(2,1)S(1)} %maximum_bitcast_fusion), channel_id=1, source_target_pairs={{0,16},{1,9},{2,18},{3,11},{4,20},{5,13},{6,22},{7,15},{8,24},{9,1... | collective-permute-start | bytes 884744 | tf_op jit(solution)/shard_map/ppermute | solution.py:743
  13.4 10.6 %collective-permute-start.1 = (bf16[2,48,768]{2,1,0:T(8,128)(2,1)S(1)}, bf16[2,48,768]{2,1,0:T(8,128)(2,1)S(1)}, u32[]{:S(2)}, u32[]{:S(2)}) collective-permute-start(bf16[2,48,768]{2,1,0:T(8,128)(2,1)S(1)} %pad_maximum_fusion.6), channel_id=1, source_target_pairs={{0,8},{1,17},{2,10},{3,19},{4,12},{5,21},{6,14},{7,23},{8,0},{9,25... | collective-permute-start | bytes 442376 | tf_op jit(solution)/shard_map/ppermute | solution.py:743
  15.7 11.0 %collective-permute-start.6 = (bf16[2,48,768]{2,1,0:T(8,128)(2,1)S(1)}, bf16[2,48,768]{2,1,0:T(8,128)(2,1)S(1)}, u32[]{:S(2)}, u32[]{:S(2)}) collective-permute-start(bf16[2,48,768]{2,1,0:T(8,128)(2,1)S(1)} %pad_maximum_fusion.7), channel_id=1, source_target_pairs={{0,8},{1,17},{2,10},{3,19},{4,12},{5,21},{6,14},{7,23},{8,0},{9,25... | collective-permute-start | bytes 442376 | tf_op jit(solution)/shard_map/ppermute | solution.py:743
  24.0 6.8 %collective-permute-start.2 = (bf16[4,48,768]{2,1,0:T(8,128)(2,1)S(1)}, bf16[4,48,768]{2,1,0:T(8,128)(2,1)S(1)}, u32[]{:S(2)}, u32[]{:S(2)}) collective-permute-start(bf16[4,48,768]{2,1,0:T(8,128)(2,1)S(1)} %pad_maximum_fusion.3), channel_id=1, source_target_pairs={{0,4},{1,3},{2,6},{3,1},{4,0},{5,7},{6,2},{7,5},{8,12},{9,11},{10,... | collective-permute-start | bytes 884744 | tf_op jit(solution)/shard_map/ppermute | solution.py:743
  26.7 4.1 %copy-start.32 = (bf16[2,48,768]{2,1,0:T(8,128)(2,1)}, bf16[2,48,768]{2,1,0:T(8,128)(2,1)S(1)}, u32[]{:S(2)}) copy-start(bf16[2,48,768]{2,1,0:T(8,128)(2,1)S(1)} %collective-permute-done.6) | copy-start | bytes 442372
  27.5 9.4 %collective-permute-start.7 = (bf16[4,48,768]{2,1,0:T(8,128)(2,1)}, bf16[4,48,768]{2,1,0:T(8,128)(2,1)}, u32[]{:S(2)}, u32[]{:S(2)}) collective-permute-start(bf16[4,48,768]{2,1,0:T(8,128)(2,1)} %pad_maximum_fusion.4), channel_id=1, source_target_pairs={{0,4},{1,3},{2,6},{3,1},{4,0},{5,7},{6,2},{7,5},{8,12},{9,11},{10,... | collective-permute-start | bytes 884744 | tf_op jit(solution)/shard_map/ppermute | solution.py:743
  30.9 11.6 %collective-permute-start.3 = (bf16[8,48,768]{2,1,0:T(8,128)(2,1)S(1)}, bf16[8,48,768]{2,1,0:T(8,128)(2,1)S(1)}, u32[]{:S(2)}, u32[]{:S(2)}) collective-permute-start(bf16[8,48,768]{2,1,0:T(8,128)(2,1)S(1)} %pad_maximum_fusion.held_ref), channel_id=1, source_target_pairs={{0,2},{1,5},{2,0},{3,7},{4,6},{5,1},{6,4},{7,3},{8,10},{9,13},{10,... | collective-permute-start | bytes 1769480 | tf_op jit(solution)/shard_map/ppermute | solution.py:743
  32.5 12.7 %copy-start.25 = (bf16[2,48,3072]{2,1,0:T(8,128)(2,1)}, bf16[2,48,3072]{2,1,0:T(8,128)(2,1)S(1)}, u32[]{:S(2)}) copy-start(bf16[2,48,3072]{2,1,0:T(8,128)(2,1)S(1)} %pad_maximum_fusion.2.held_ref) | copy-start | bytes 1769476
  32.5 27.4 %collective-permute-start.9 = (bf16[2,48,3072]{2,1,0:T(8,128)(2,1)S(1)}, bf16[2,48,3072]{2,1,0:T(8,128)(2,1)}, u32[]{:S(2)}, u32[]{:S(2)}) collective-permute-start(bf16[2,48,3072]{2,1,0:T(8,128)(2,1)S(1)} %pad_maximum_fusion.2.held_ref), channel_id=1, source_target_pairs={{0,8},{1,17},{2,10},{3,19},{4,12},{5,21},{6,14},{7,23},{8,0},{9,25... | collective-permute-start | bytes 1769480 | tf_op jit(solution)/shard_map/ppermute | solution.py:743
  36.9 8.3 %copy-start.16 = (s32[2]{0:T(128)}, s32[2]{0:T(128)S(1)}, u32[]{:S(2)}) copy-start(s32[2]{0:T(128)S(1)} %pad_add_fusion.info_ref.refs_0_) | copy-start | bytes 28
  60.0 5.1 %copy-start.6 = (bf16[8,48,768]{2,1,0:T(8,128)(2,1)S(1)}, bf16[8,48,768]{2,1,0:T(8,128)(2,1)}, u32[]{:S(2)}) copy-start(bf16[8,48,768]{2,1,0:T(8,128)(2,1)} %pad_maximum_fusion.1.refs_3_.held_ref) | copy-start | bytes 1769476
  63.5 22.0 %collective-permute-start.11 = (bf16[4,48,3072]{2,1,0:T(8,128)(2,1)}, bf16[4,48,3072]{2,1,0:T(8,128)(2,1)S(1)}, u32[]{:S(2)}, u32[]{:S(2)}) collective-permute-start(bf16[4,48,3072]{2,1,0:T(8,128)(2,1)} %join_gathered.2.refs_1_.held_ref), channel_id=1, source_target_pairs={{0,4},{1,3},{2,6},{3,1},{4,0},{5,7},{6,2},{7,5},{8,12},{9,11},{10,... | collective-permute-start | bytes 3538952 | tf_op jit(solution)/shard_map/ppermute | solution.py:743
  65.1 26.3 %collective-permute-start.10 = (bf16[8,48,768]{2,1,0:T(8,128)(2,1)S(1)}, bf16[8,48,768]{2,1,0:T(8,128)(2,1)S(1)}, u32[]{:S(2)}, u32[]{:S(2)}) collective-permute-start(bf16[8,48,768]{2,1,0:T(8,128)(2,1)S(1)} %copy-done.6), channel_id=1, source_target_pairs={{0,2},{1,5},{2,0},{3,7},{4,6},{5,1},{6,4},{7,3},{8,10},{9,13},{10,... | collective-permute-start | bytes 1769480 | tf_op jit(solution)/shard_map/ppermute | solution.py:743
  86.6 4.9 %copy-start.17 = (s32[2]{0:T(128)S(1)}, s32[2]{0:T(128)}, u32[]{:S(2)}) copy-start(s32[2]{0:T(128)} %copy-done.16) | copy-start | bytes 28
  90.3 29.1 %collective-permute-start.13 = (bf16[8,48,3072]{2,1,0:T(8,128)(2,1)}, bf16[8,48,3072]{2,1,0:T(8,128)(2,1)S(1)}, u32[]{:S(2)}, u32[]{:S(2)}) collective-permute-start(bf16[8,48,3072]{2,1,0:T(8,128)(2,1)} %join_gathered.3.refs_1_.refs_0_), channel_id=1, source_target_pairs={{0,2},{1,5},{2,0},{3,7},{4,6},{5,1},{6,4},{7,3},{8,10},{9,13},{10,... | collective-permute-start | bytes 7077896 | tf_op jit(solution)/shard_map/ppermute | solution.py:743
  108.1 5.2 %copy-start.24 = (bf16[1024,768]{1,0:T(8,128)(2,1)S(1)}, bf16[1024,768]{1,0:T(8,128)(2,1)}, u32[]{:S(2)}) copy-start(bf16[1024,768]{1,0:T(8,128)(2,1)} %cot_ref.1) | copy-start | bytes 4718596
  108.1 5.7 %copy-start.41 = (f32[768]{0:T(1024)S(1)}, f32[768]{0:T(1024)}, u32[]{:S(2)}) copy-start(f32[768]{0:T(1024)} %param.20) | copy-start | bytes 9220
  108.1 6.3 %copy-start.42 = (f32[768]{0:T(1024)S(1)}, f32[768]{0:T(1024)}, u32[]{:S(2)}) copy-start(f32[768]{0:T(1024)} %param.22) | copy-start | bytes 9220
  108.1 6.2 %copy-start.43 = (f32[768]{0:T(1024)S(1)}, f32[768]{0:T(1024)}, u32[]{:S(2)}) copy-start(f32[768]{0:T(1024)} %param.21) | copy-start | bytes 9220
  113.2 5.1 %collective-permute-start.12 = (bf16[1024,768]{1,0:T(8,128)(2,1)}, bf16[1024,768]{1,0:T(8,128)(2,1)S(1)}, u32[]{:S(2)}, u32[]{:S(2)}) collective-permute-start(bf16[1024,768]{1,0:T(8,128)(2,1)} %get-tuple-element.83), channel_id=1, source_target_pairs={{0,1},{1,0},{2,3},{3,2},{4,5},{5,4},{6,7},{7,6},{8,9},{9,8},{10,11... | collective-permute-start | bytes 4718600 | tf_op jit(solution)/shard_map/ppermute | solution.py:748
  113.3 13.8 %collective-permute-start.15 = (bf16[1024,768]{1,0:T(8,128)(2,1)S(1)}, bf16[1024,768]{1,0:T(8,128)(2,1)S(1)}, u32[]{:S(2)}, u32[]{:S(2)}) collective-permute-start(bf16[1024,768]{1,0:T(8,128)(2,1)S(1)} %copy-done.24), channel_id=1, source_target_pairs={{0,1},{1,0},{2,3},{3,2},{4,5},{5,4},{6,7},{7,6},{8,9},{9,8},{10,11... | collective-permute-start | bytes 4718600 | tf_op jit(solution)/shard_map/ppermute | solution.py:748
  120.8 5.6 %copy-start.39 = (f32[1536]{0:T(1024)S(1)}, f32[1536]{0:T(1024)}, u32[]{:S(2)}) copy-start(f32[1536]{0:T(1024)} %param.24) | copy-start | bytes 18436
  126.4 3.6 %collective-permute-start.14 = (bf16[1024,768]{1,0:T(8,128)(2,1)}, bf16[1024,768]{1,0:T(8,128)(2,1)S(1)}, u32[]{:S(2)}, u32[]{:S(2)}) collective-permute-start(bf16[1024,768]{1,0:T(8,128)(2,1)} %get-tuple-element.85.own_ref), channel_id=1, source_target_pairs={{0,1},{1,0},{2,3},{3,2},{4,5},{5,4},{6,7},{7,6},{8,9},{9,8},{10,11... | collective-permute-start | bytes 4718600 | tf_op jit(solution)/shard_map/ppermute | solution.py:748
  174.3 3.7 %collective-permute-start.17 = (bf16[1024,768]{1,0:T(8,128)(2,1)}, bf16[1024,768]{1,0:T(8,128)(2,1)S(1)}, u32[]{:S(2)}, u32[]{:S(2)}) collective-permute-start(bf16[1024,768]{1,0:T(8,128)(2,1)} %get-tuple-element.91), channel_id=1, source_target_pairs={{0,1},{1,0},{2,3},{3,2},{4,5},{5,4},{6,7},{7,6},{8,9},{9,8},{10,11... | collective-permute-start | bytes 4718600 | tf_op jit(solution)/shard_map/ppermute | solution.py:748
  174.5 41.1 %collective-permute-start.19 = (bf16[8,48,3072]{2,1,0:T(8,128)(2,1)}, bf16[8,48,3072]{2,1,0:T(8,128)(2,1)S(1)}, u32[]{:S(2)}, u32[]{:S(2)}) collective-permute-start(bf16[8,48,3072]{2,1,0:T(8,128)(2,1)} %get-tuple-element.98), channel_id=1, source_target_pairs={{0,2},{1,5},{2,0},{3,7},{4,6},{5,1},{6,4},{7,3},{8,10},{9,13},{10,... | collective-permute-start | bytes 7077896 | tf_op jit(solution)/shard_map/ppermute | solution.py:743
  187.2 3.7 %collective-permute-start.18 = (bf16[1024,768]{1,0:T(8,128)(2,1)}, bf16[1024,768]{1,0:T(8,128)(2,1)S(1)}, u32[]{:S(2)}, u32[]{:S(2)}) collective-permute-start(bf16[1024,768]{1,0:T(8,128)(2,1)} %get-tuple-element.92.own_ref), channel_id=1, source_target_pairs={{0,1},{1,0},{2,3},{3,2},{4,5},{5,4},{6,7},{7,6},{8,9},{9,8},{10,11... | collective-permute-start | bytes 4718600 | tf_op jit(solution)/shard_map/ppermute | solution.py:748
  192.1 23.5 %slice-start = ((s8[4718592]{0:T(1024)(128)(4,1)}), s8[4194304]{0:T(1024)(128)(4,1)S(1)}, s32[]{:S(2)}) async-start(s8[4718592]{0:T(1024)(128)(4,1)} %bitcast.49), calls=%async_computation | async-start | bytes 8388608
  192.1 23.5 %slice-start.1 = ((s8[4718592]{0:T(1024)(128)(4,1)}), s8[524288]{0:T(1024)(128)(4,1)S(1)}, s32[]{:S(2)}) async-start(s8[4718592]{0:T(1024)(128)(4,1)} %bitcast.49), calls=%async_computation.1 | async-start | bytes 1048576
  192.1 23.5 %copy-start.18 = (s32[2]{0:T(128)S(1)}, s32[2]{0:T(128)}, u32[]{:S(2)}) copy-start(s32[2]{0:T(128)} %copy-done.16) | copy-start | bytes 28
  218.7 26.9 %collective-permute-start.20 = (bf16[4,48,3072]{2,1,0:T(8,128)(2,1)S(1)}, bf16[4,48,3072]{2,1,0:T(8,128)(2,1)S(1)}, u32[]{:S(2)}, u32[]{:S(2)}) collective-permute-start(bf16[4,48,3072]{2,1,0:T(8,128)(2,1)S(1)} %get-tuple-element.99.refs_0_), channel_id=1, source_target_pairs={{0,4},{1,3},{2,6},{3,1},{4,0},{5,7},{6,2},{7,5},{8,12},{9,11},{10,... | collective-permute-start | bytes 3538952 | tf_op jit(solution)/shard_map/ppermute | solution.py:743
  220.2 77.3 %collective-permute-start.16 = (bf16[1024,768]{1,0:T(8,128)(2,1)}, bf16[1024,768]{1,0:T(8,128)(2,1)}, u32[]{:S(2)}, u32[]{:S(2)}) collective-permute-start(bf16[1024,768]{1,0:T(8,128)(2,1)} %get-tuple-element.87), channel_id=1, source_target_pairs={{0,1},{1,0},{2,3},{3,2},{4,5},{5,4},{6,7},{7,6},{8,9},{9,8},{10,11... | collective-permute-start | bytes 4718600 | tf_op jit(solution)/shard_map/ppermute | solution.py:748
  220.2 23.8 %collective-permute-start.21 = (bf16[8,48,512]{2,1,0:T(8,128)(2,1)}, bf16[8,48,512]{2,1,0:T(8,128)(2,1)S(1)}, u32[]{:S(2)}, u32[]{:S(2)}) collective-permute-start(bf16[8,48,512]{2,1,0:T(8,128)(2,1)} %get-tuple-element.100.refs_1_), channel_id=1, source_target_pairs={{0,2},{1,5},{2,0},{3,7},{4,6},{5,1},{6,4},{7,3},{8,10},{9,13},{10,... | collective-permute-start | bytes 1179656 | tf_op jit(solution)/shard_map/ppermute | solution.py:743
  221.2 22.8 %copy-start.10 = (f32[8,48,512]{2,1,0:T(8,128)S(1)}, f32[8,48,512]{2,1,0:T(8,128)}, u32[]{:S(2)}) copy-start(f32[8,48,512]{2,1,0:T(8,128)} %get-tuple-element.108.keep_ref.send_ref) | copy-start | bytes 2359300
  221.2 22.8 %copy-start.19 = (s32[2]{0:T(128)S(1)}, s32[2]{0:T(128)}, u32[]{:S(2)}) copy-start(s32[2]{0:T(128)} %copy-done.16) | copy-start | bytes 28
  248.0 25.0 %copy-start.13 = (bf16[2,48,3072]{2,1,0:T(8,128)(2,1)S(1)}, bf16[2,48,3072]{2,1,0:T(8,128)(2,1)}, u32[]{:S(2)}) copy-start(bf16[2,48,3072]{2,1,0:T(8,128)(2,1)} %copy-done.12) | copy-start | bytes 1769476
  248.0 26.4 %copy-start.15 = (bf16[4,48,512]{2,1,0:T(8,128)(2,1)S(1)}, bf16[4,48,512]{2,1,0:T(8,128)(2,1)}, u32[]{:S(2)}) copy-start(bf16[4,48,512]{2,1,0:T(8,128)(2,1)} %copy-done.14) | copy-start | bytes 589828
  271.9 19.0 %collective-permute-start.23 = (bf16[8,48,1024]{2,1,0:T(8,128)(2,1)}, bf16[8,48,1024]{2,1,0:T(8,128)(2,1)S(1)}, u32[]{:S(2)}, u32[]{:S(2)}) collective-permute-start(bf16[8,48,1024]{2,1,0:T(8,128)(2,1)} %get-tuple-element.115), channel_id=1, source_target_pairs={{0,2},{1,5},{2,0},{3,7},{4,6},{5,1},{6,4},{7,3},{8,10},{9,13},{10,... | collective-permute-start | bytes 2359304 | tf_op jit(solution)/shard_map/ppermute | solution.py:743
  273.1 15.2 %collective-permute-start.24 = (bf16[2,48,3072]{2,1,0:T(8,128)(2,1)S(1)}, bf16[2,48,3072]{2,1,0:T(8,128)(2,1)S(1)}, u32[]{:S(2)}, u32[]{:S(2)}) collective-permute-start(bf16[2,48,3072]{2,1,0:T(8,128)(2,1)S(1)} %copy-done.13), channel_id=1, source_target_pairs={{0,8},{1,9},{2,10},{3,11},{4,12},{5,13},{6,14},{7,15},{8,0},{9,1},... | collective-permute-start | bytes 1769480 | tf_op jit(solution)/shard_map/ppermute | solution.py:743
  274.4 10.7 %collective-permute-start.25 = (bf16[4,48,512]{2,1,0:T(8,128)(2,1)S(1)}, bf16[4,48,512]{2,1,0:T(8,128)(2,1)S(1)}, u32[]{:S(2)}, u32[]{:S(2)}) collective-permute-start(bf16[4,48,512]{2,1,0:T(8,128)(2,1)S(1)} %copy-done.15), channel_id=1, source_target_pairs={{0,4},{1,3},{2,6},{3,1},{4,0},{5,7},{6,2},{7,5},{8,12},{9,11},{10,... | collective-permute-start | bytes 589832 | tf_op jit(solution)/shard_map/ppermute | solution.py:743
  275.3 9.8 %copy-start.20 = (s32[2]{0:T(128)S(1)}, s32[2]{0:T(128)}, u32[]{:S(2)}) copy-start(s32[2]{0:T(128)} %copy-done.16) | copy-start | bytes 28
  287.2 7.7 %collective-permute-start.31 = (bf16[2,48,512]{2,1,0:T(8,128)(2,1)S(1)}, bf16[2,48,512]{2,1,0:T(8,128)(2,1)S(1)}, u32[]{:S(2)}, u32[]{:S(2)}) collective-permute-start(bf16[2,48,512]{2,1,0:T(8,128)(2,1)S(1)} %get-tuple-element.119.refs_1_), channel_id=1, source_target_pairs={{0,8},{1,9},{2,10},{3,11},{4,12},{5,13},{6,14},{7,15},{8,0},{9,1},... | collective-permute-start | bytes 294920 | tf_op jit(solution)/shard_map/ppermute | solution.py:743
  288.9 23.9 %collective-permute-start.36 = (bf16[1,48,3072]{2,1,0:T(8,128)(2,1)S(1)}, bf16[1,48,3072]{2,1,0:T(8,128)(2,1)S(1)}, u32[]{:S(2)}, u32[]{:S(2)}) collective-permute-start(bf16[1,48,3072]{2,1,0:T(8,128)(2,1)S(1)} %get-tuple-element.117.refs_0_), channel_id=1, source_target_pairs={{0,16},{1,17},{2,18},{3,19},{4,20},{5,21},{6,22},{7,23},{8,24},{9,... | collective-permute-start | bytes 884744 | tf_op jit(solution)/shard_map/ppermute | solution.py:743
  290.9 6.6 %copy-start.40 = (f32[768]{0:T(1024)S(1)}, f32[768]{0:T(1024)}, u32[]{:S(2)}) copy-start(f32[768]{0:T(1024)} %param.26) | copy-start | bytes 9220
  293.9 9.5 %collective-permute-start.26 = (f32[16,768]{1,0:T(8,128)}, f32[16,768]{1,0:T(8,128)S(1)}, u32[]{:S(2)}, u32[]{:S(2)}) collective-permute-start(f32[16,768]{1,0:T(8,128)} %vectors.1), channel_id=1, source_target_pairs={{0,2},{1,3},{2,0},{3,1},{4,6},{5,7},{6,4},{7,5},{8,10},{9,11},{10,... | collective-permute-start | bytes 147464 | tf_op jit(solution)/shard_map/ppermute | solution.py:743
  296.5 10.0 %collective-permute-start.32 = (bf16[1,48,512]{2,1,0:T(8,128)(2,1)S(1)}, bf16[1,48,512]{2,1,0:T(8,128)(2,1)S(1)}, u32[]{:S(2)}, u32[]{:S(2)}) collective-permute-start(bf16[1,48,512]{2,1,0:T(8,128)(2,1)S(1)} %get-tuple-element.131.refs_0_), channel_id=1, source_target_pairs={{0,16},{1,17},{2,18},{3,19},{4,20},{5,21},{6,22},{7,23},{8,24},{9,... | collective-permute-start | bytes 147464 | tf_op jit(solution)/shard_map/ppermute | solution.py:743
  297.5 5.0 %copy-start.9 = (bf16[4,48,1024]{2,1,0:T(8,128)(2,1)S(1)}, bf16[4,48,1024]{2,1,0:T(8,128)(2,1)}, u32[]{:S(2)}) copy-start(bf16[4,48,1024]{2,1,0:T(8,128)(2,1)} %copy-done.7) | copy-start | bytes 1179652
  297.5 5.9 %copy-start.33 = (f32[16,768]{1,0:T(8,128)S(1)}, f32[16,768]{1,0:T(8,128)}, u32[]{:S(2)}) copy-start(f32[16,768]{1,0:T(8,128)} %vectors.1) | copy-start | bytes 147460
  302.5 21.5 %collective-permute-start.22 = (bf16[1024,768]{1,0:T(8,128)(2,1)S(1)}, bf16[1024,768]{1,0:T(8,128)(2,1)}, u32[]{:S(2)}, u32[]{:S(2)}) collective-permute-start(bf16[1024,768]{1,0:T(8,128)(2,1)S(1)} %copy-done.3), channel_id=1, source_target_pairs={{0,1},{1,0},{2,3},{3,2},{4,5},{5,4},{6,7},{7,6},{8,9},{9,8},{10,11... | collective-permute-start | bytes 4718600 | tf_op jit(solution)/shard_map/ppermute | solution.py:748
  302.5 19.4 %collective-permute-start.33 = (bf16[4,48,1024]{2,1,0:T(8,128)(2,1)S(1)}, bf16[4,48,1024]{2,1,0:T(8,128)(2,1)S(1)}, u32[]{:S(2)}, u32[]{:S(2)}) collective-permute-start(bf16[4,48,1024]{2,1,0:T(8,128)(2,1)S(1)} %copy-done.9), channel_id=1, source_target_pairs={{0,4},{1,3},{2,6},{3,1},{4,0},{5,7},{6,2},{7,5},{8,12},{9,11},{10,... | collective-permute-start | bytes 1179656 | tf_op jit(solution)/shard_map/ppermute | solution.py:743
  303.4 7.9 %collective-permute-start.27 = (f32[16,768]{1,0:T(8,128)S(1)}, f32[16,768]{1,0:T(8,128)S(1)}, u32[]{:S(2)}, u32[]{:S(2)}) collective-permute-start(f32[16,768]{1,0:T(8,128)S(1)} %add.65.refs_1_), channel_id=1, source_target_pairs={{0,4},{1,5},{2,6},{3,7},{4,0},{5,1},{6,2},{7,3},{8,12},{9,13},{10,... | collective-permute-start | bytes 147464 | tf_op jit(solution)/shard_map/ppermute | solution.py:743
  311.3 4.2 %collective-permute-start.28 = (f32[16,768]{1,0:T(8,128)S(1)}, f32[16,768]{1,0:T(8,128)S(1)}, u32[]{:S(2)}, u32[]{:S(2)}) collective-permute-start(f32[16,768]{1,0:T(8,128)S(1)} %add.66), channel_id=1, source_target_pairs={{0,8},{1,9},{2,10},{3,11},{4,12},{5,13},{6,14},{7,15},{8,0},{9,1},... | collective-permute-start | bytes 147464 | tf_op jit(solution)/shard_map/ppermute | solution.py:743
  315.5 5.0 %collective-permute-start.29 = (f32[16,768]{1,0:T(8,128)S(1)}, f32[16,768]{1,0:T(8,128)S(1)}, u32[]{:S(2)}, u32[]{:S(2)}) collective-permute-start(f32[16,768]{1,0:T(8,128)S(1)} %add.67.refs_0_), channel_id=1, source_target_pairs={{0,16},{1,17},{2,18},{3,19},{4,20},{5,21},{6,22},{7,23},{8,24},{9,... | collective-permute-start | bytes 147464 | tf_op jit(solution)/shard_map/ppermute | solution.py:743
  320.6 3.5 %collective-permute-start.30 = (f32[6,768]{1,0:T(8,128)S(1)}, f32[6,768]{1,0:T(8,128)S(1)}, u32[]{:S(2)}, u32[]{:S(2)}) collective-permute-start(f32[6,768]{1,0:T(8,128)S(1)} %slice.112), channel_id=1, source_target_pairs={{0,1},{1,0},{2,3},{3,2},{4,5},{5,4},{6,7},{7,6},{8,9},{9,8},{10,11... | collective-permute-start | bytes 55304 | tf_op jit(solution)/shard_map/ppermute | solution.py:748
  322.5 7.8 %collective-permute-start.34 = (bf16[2,48,1024]{2,1,0:T(8,128)(2,1)S(1)}, bf16[2,48,1024]{2,1,0:T(8,128)(2,1)S(1)}, u32[]{:S(2)}, u32[]{:S(2)}) collective-permute-start(bf16[2,48,1024]{2,1,0:T(8,128)(2,1)S(1)} %get-tuple-element.134), channel_id=1, source_target_pairs={{0,8},{1,9},{2,10},{3,11},{4,12},{5,13},{6,14},{7,15},{8,0},{9,1},... | collective-permute-start | bytes 589832 | tf_op jit(solution)/shard_map/ppermute | solution.py:743
  332.4 8.0 %collective-permute-start.35 = (bf16[1,48,1024]{2,1,0:T(8,128)(2,1)S(1)}, bf16[1,48,1024]{2,1,0:T(8,128)(2,1)S(1)}, u32[]{:S(2)}, u32[]{:S(2)}) collective-permute-start(bf16[1,48,1024]{2,1,0:T(8,128)(2,1)S(1)} %get-tuple-element.136), channel_id=1, source_target_pairs={{0,16},{1,17},{2,18},{3,19},{4,20},{5,21},{6,22},{7,23},{8,24},{9,... | collective-permute-start | bytes 294920 | tf_op jit(solution)/shard_map/ppermute | solution.py:743
  (20 other events, 30.2 us)
